TPU v7x, 512 devices: a whole 4x4x16 slice. The times are simulated.
512 devices in a mesh: dom: 64 (over z, y), rep: 8 (over x, core).
Axes of the slice: x: 4, y: 4, z: 16, core: 2. Of those that a mesh axis runs over, the one named last changes fastest.
Arguments:
- entity: float32 [32768, 400], P('dom'), may hold values from -2 to 2
- adagrad_state: float32 [32768], P('dom'), may hold values from 0.01 to 4
- relation: float32 [237, 400], replicated, may hold values from 0.25 to 1.75
- src_rows: int32 [64, 8, 64, 8], P('dom', 'rep'), may hold values from 0 to 511
- dst_rows: int32 [64, 8, 64, 8], P('dom', 'rep'), may hold values from 0 to 511
- rel_ids: int32 [64, 8, 64, 8], P('dom', 'rep'), may hold values from 0 to 236
- bucket_counts: int32 [64, 8, 64], P('dom', 'rep'), may hold values from 1 to 8, as said below
- noise_rows: int32 [64, 8, 512], P('dom', 'rep'), may hold values from 0 to 511
Outputs:
- new_entity: float32 [32768, 400], P('dom')
- new_state: float32 [32768], P('dom')
Inputs may be any that keep to these rules, and one draw needn't show every extreme that they name: `bucket_counts`: in every draw some destination partition has all 8 slots live in its bucket on every device, and every device has some full bucket. `noise_rows`: noise entities may repeat.
All inputs are finite; a program needn't handle non-finite values.
Results may differ from a plain program's by a relative error of at most 0.0001.
Values sent between devices are 32-bit elements; how exact they have to be, the bound alone decides.
No kernel may reach another device: no remote copies, remote signals or barrier semaphores. Data moves between devices by JAX's collectives and lax.ppermute only.
A program may use at most 64 MiB of HBM per device.

v0:
```python
import jax
import jax.numpy as jnp
from jax import lax
from jax.sharding import PartitionSpec as P

LEARN_RATE = 0.3


def per_device(
    entity, adagrad_state, relation, src_rows, dst_rows, rel_ids, bucket_counts, noise_rows
):
    highest = lax.Precision.HIGHEST
    buckets = lax.axis_size("dom")
    slot_cap = src_rows.shape[3]
    features = entity.shape[1]
    source_rows = src_rows[0, 0]
    slot_live = (
        jnp.arange(slot_cap, dtype=jnp.int32)[None, :] < bucket_counts[0, 0][:, None]
    ).astype(jnp.float32)
    rel_rows = relation[rel_ids[0, 0]]
    source_emb = entity[source_rows]
    query = source_emb * rel_rows
    flat_query = query.reshape(buckets * slot_cap, features)
    noise_local = noise_rows[0, 0].reshape(buckets, -1)
    rows_in = lax.all_to_all(noise_local, "dom", split_axis=0, concat_axis=0, tiled=True)
    replies = lax.all_to_all(entity[rows_in], "dom", split_axis=0, concat_axis=0, tiled=True)
    noise_parts = replies
    noise_all = noise_parts.reshape(-1, features)
    noise_scores = jnp.dot(
        flat_query, noise_all.T, precision=highest, preferred_element_type=jnp.float32
    )
    noise_coef = jax.nn.sigmoid(noise_scores) * slot_live.reshape(-1)[:, None]
    noise_term = jnp.dot(
        noise_coef.T, flat_query, precision=highest, preferred_element_type=jnp.float32
    )
    noise_grad = lax.all_to_all(
        noise_term.reshape(buckets, -1, features), "dom", split_axis=0, concat_axis=0, tiled=True
    )
    slot_ids = lax.all_to_all(dst_rows[0, 0], "dom", split_axis=0, concat_axis=0, tiled=True)
    replies = lax.all_to_all(entity[slot_ids], "dom", split_axis=0, concat_axis=0, tiled=True)
    positive = jnp.sum(query * replies, axis=2)
    pos_coef = -jax.nn.sigmoid(-positive) * slot_live
    source_pos = pos_coef[:, :, None] * replies
    owner_grads = lax.all_to_all(
        pos_coef[:, :, None] * query, "dom", split_axis=0, concat_axis=0, tiled=True
    )
    noise_back = jnp.dot(
        noise_coef, noise_all, precision=highest, preferred_element_type=jnp.float32
    )
    source_grad = rel_rows * (source_pos + noise_back.reshape(buckets, slot_cap, features))
    grad = jnp.zeros(entity.shape, jnp.float32)
    grad = grad.at[source_rows.reshape(-1)].add(source_grad.reshape(-1, features))
    grad = grad.at[slot_ids.reshape(-1)].add(owner_grads.reshape(-1, features))
    grad = grad.at[rows_in.reshape(-1)].add(noise_grad.reshape(-1, features))
    summed = lax.psum(grad, "rep")
    new_state = adagrad_state + jnp.mean(summed * summed, axis=1)
    new_entity = entity - LEARN_RATE * summed / jnp.sqrt(new_state)[:, None]
    return (new_entity, new_state)


def solution(mesh):
    return jax.shard_map(
        per_device,
        mesh=mesh,
        in_specs=(
            P("dom", None),
            P("dom"),
            P(),
            P("dom", "rep", None, None),
            P("dom", "rep", None, None),
            P("dom", "rep", None, None),
            P("dom", "rep", None),
            P("dom", "rep", None),
        ),
        out_specs=(P("dom", None), P("dom")),
        check_vma=False,
    )
```

profile of v0, /device:TPU:1, one launch (start us, length us, event | category | flops | bytes accessed | tf_op | source)
XLA Modules:
  0.0 382.1 jit_solution(6615292369828459782)
XLA Ops:
  7.2 1.4 copy.39
  8.6 19.4 %all-to-all-start = ((s32[64,1,8]{2,1,0:T(1,128)}), s32[64,1,8]{2,1,0:T(1,128)S(1)}, u32[]{:S(2)}, u32[]{:S(2)}) async-start(s32[64,1,8]{2,1,0:T(1,128)} %bitcast.6), calls=%async_computation | async-start | bytes 65536 | tf_op jit(solution)/shard_map/all_to_all | solution.py:39
  28.0 0.5 broadcast.205
  28.5 0.0 copy-done.8
  28.5 0.7 reduce.9
  29.2 0.7 all_to_all.32
  29.9 1.5 copy.46
  31.3 10.2 %all-to-all-done = s32[64,1,8]{2,1,0:T(1,128)S(1)} async-done(((s32[64,1,8]{2,1,0:T(1,128)}), s32[64,1,8]{2,1,0:T(1,128)S(1)}, u32[]{:S(2)}, u32[]{:S(2)}) %all-to-all-start) | async-done | bytes 2080 | tf_op jit(solution)/shard_map/all_to_all | solution.py:39
  41.6 4.6 %all-to-all-start.2 = ((s32[64,1,8]{2,1,0:T(1,128)}), s32[64,1,8]{2,1,0:T(1,128)S(1)}, u32[]{:S(2)}, u32[]{:S(2)}) async-start(s32[64,1,8]{2,1,0:T(1,128)} %bitcast.10), calls=%async_computation.2 | async-start | bytes 65536 | tf_op jit(solution)/shard_map/all_to_all | solution.py:25
  46.2 0.1 reshape.321
  46.3 2.3 gather_fusion.2
  48.6 11.0 %all-to-all-done.2 = s32[64,1,8]{2,1,0:T(1,128)S(1)} async-done(((s32[64,1,8]{2,1,0:T(1,128)}), s32[64,1,8]{2,1,0:T(1,128)S(1)}, u32[]{:S(2)}, u32[]{:S(2)}) %all-to-all-start.2) | async-done | bytes 2080 | tf_op jit(solution)/shard_map/all_to_all | solution.py:25
  59.7 4.7 %all-to-all-start.1 = ((f32[64,8,400]{2,1,0:T(8,128)}), f32[64,8,400]{2,1,0:T(8,128)S(1)}, u32[]{:S(2)}, u32[]{:S(2)}) async-start(f32[64,8,400]{2,1,0:T(8,128)} %bitcast.8), calls=%async_computation.1 | async-start | bytes 2097152 | tf_op jit(solution)/shard_map/all_to_all | solution.py:40
  64.3 0.1 reshape.329
  64.4 2.3 gather_fusion.3
  66.8 46.3 %all-to-all-done.1 = f32[64,8,400]{2,1,0:T(8,128)S(1)} async-done(((f32[64,8,400]{2,1,0:T(8,128)}), f32[64,8,400]{2,1,0:T(8,128)S(1)}, u32[]{:S(2)}, u32[]{:S(2)}) %all-to-all-start.1) | async-done | bytes 819232 | tf_op jit(solution)/shard_map/all_to_all | solution.py:40
  113.1 1.0 copy-done
  114.1 10.6 %all-to-all-start.3 = ((f32[64,8,400]{2,1,0:T(8,128)}), f32[64,8,400]{2,1,0:T(8,128)}, u32[]{:S(2)}, u32[]{:S(2)}) async-start(f32[64,8,400]{2,1,0:T(8,128)} %bitcast.12), calls=%async_computation.3 | async-start | bytes 2097152 | tf_op jit(solution)/shard_map/all_to_all | solution.py:26
  124.7 0.0 copy-done.5
  124.7 0.1 copy.34
  124.8 0.0 copy-start.6
  124.8 0.1 reshape.313
  124.9 0.6 copy-done.6
  125.5 0.1 copy.35
  125.6 0.1 reshape.305
  125.7 0.0 copy-done.4
  125.7 0.2 copy.36
  125.9 2.3 gather_fusion.1
  128.2 1.6 gather_fusion
  129.9 1.8 multiply_reduce_fusion.1
  131.6 0.0 copy-start.7
  131.6 0.6 copy-done.7
  132.3 0.1 negate_select_fusion
  132.4 1.1 broadcast_multiply_fusion
  133.5 40.2 %all-to-all-done.3 = f32[64,8,400]{2,1,0:T(8,128)} async-done(((f32[64,8,400]{2,1,0:T(8,128)}), f32[64,8,400]{2,1,0:T(8,128)}, u32[]{:S(2)}, u32[]{:S(2)}) %all-to-all-start.3) | async-done | bytes 819232 | tf_op jit(solution)/shard_map/all_to_all | solution.py:26
  173.7 10.1 %all-to-all-start.4 = ((f32[64,8,400]{2,1,0:T(8,128)}), f32[64,8,400]{2,1,0:T(8,128)}, u32[]{:S(2)}, u32[]{:S(2)}) async-start(f32[64,8,400]{2,1,0:T(8,128)} %broadcast_multiply_fusion), calls=%async_computation.4 | async-start | bytes 2097152 | tf_op jit(solution)/shard_map/all_to_all | solution.py:44
  183.9 0.1 fusion.19
  184.0 0.1 reshape.302
  184.1 4.2 %fusion.5 = f32[512,512]{1,0:T(8,128)} fusion(f32[64,8,400]{2,1,0:T(8,128)} %all-to-all-done.3, f32[64,8,400]{2,1,0:T(8,128)S(1)} %get-tuple-element.9, f32[512]{0:T(512)S(1)} %reshape.302), kind=kOutput, calls=%fused_computation.14 | convolution fusion | flops 1259339776 | bytes 2689024 | tf_op jit(solution)/shard_map/dot_general | solution.py:29
  188.3 2.6 copy.44
  190.8 4.0 %fusion.6 = f32[64,8,400]{2,1,0:T(8,128)} fusion(f32[64,8,400]{2,1,0:T(8,128)S(1)} %get-tuple-element.9, f32[512,512]{1,0:T(8,128)} %copy.44), kind=kOutput, calls=%fused_computation.15 | convolution fusion | flops 1258291200 | bytes 2686976 | tf_op jit(solution)/shard_map/dot_general | solution.py:33
  194.9 37.9 %all-to-all-done.4 = f32[64,8,400]{2,1,0:T(8,128)} async-done(((f32[64,8,400]{2,1,0:T(8,128)}), f32[64,8,400]{2,1,0:T(8,128)}, u32[]{:S(2)}, u32[]{:S(2)}) %all-to-all-start.4) | async-done | bytes 819232 | tf_op jit(solution)/shard_map/all_to_all | solution.py:44
  232.7 10.0 %all-to-all-start.5 = ((f32[64,8,400]{2,1,0:T(8,128)}), f32[64,8,400]{2,1,0:T(8,128)}, u32[]{:S(2)}, u32[]{:S(2)}) async-start(f32[64,8,400]{2,1,0:T(8,128)} %fusion.6), calls=%async_computation.5 | async-start | bytes 2097152 | tf_op jit(solution)/shard_map/all_to_all | solution.py:36
  242.7 0.0 all-reduce.2.cloned.1.call-start
  242.8 0.1 reshape_squeeze.4
  242.9 0.7 reduce.11
  243.6 0.1 reshape.300
  243.7 0.7 reduce.10
  244.4 0.1 reshape.298
  244.5 4.4 %fusion.1 = f32[512,400]{1,0:T(8,128)} fusion(f32[64,8,400]{2,1,0:T(8,128)} %all-to-all-done.3, f32[512,512]{1,0:T(8,128)} %fusion.5, f32[512,400]{1,0:T(8,128)S(1)} %gather_fusion, f32[64,8,400]{2,1,0:T(8,128)S(1)} %copy-done.1, f32[64,8]{1,0:T(8,128)S(1)} %negate_select_fusion), kind=kOutput, calls=%fused_computation.9 | convolution fusion | flops 1258905600 | bytes 4327424 | tf_op jit(solution)/shard_map/dot_general | solution.py:47
  249.0 4.5 %scatter_custom_fusion = f32[512,400]{1,0:T(8,128)S(1)} fusion(s32[512]{0:T(512)S(1)} %bitcast.66, f32[512,400]{1,0:T(8,128)} %fusion.1, f32[]{:T(128)} %constant.7.clone.1), kind=kCustom, calls=%fused_computation.31 | custom fusion | flops 204800 | bytes 819712 | tf_op jit(solution)/shard_map/scatter-add | solution.py:52
  253.5 5.0 %scatter_custom_fusion.1 = f32[512,400]{1,0:T(8,128)S(1)} fusion(f32[512,400]{1,0:T(8,128)S(1)} %scatter_custom_fusion, s32[512]{0:T(512)S(1)} %bitcast.67, f32[64,8,400]{2,1,0:T(8,128)} %all-to-all-done.4), kind=kCustom, calls=%fused_computation.21 | custom fusion | flops 204800 | bytes 1638400 | tf_op jit(solution)/shard_map/scatter-add | solution.py:53
  258.4 33.0 %all-to-all-done.5 = f32[64,8,400]{2,1,0:T(8,128)} async-done(((f32[64,8,400]{2,1,0:T(8,128)}), f32[64,8,400]{2,1,0:T(8,128)}, u32[]{:S(2)}, u32[]{:S(2)}) %all-to-all-start.5) | async-done | bytes 819232 | tf_op jit(solution)/shard_map/all_to_all | solution.py:36
  291.5 4.7 %scatter_custom_fusion.2 = f32[512,400]{1,0:T(8,128)S(1)} fusion(f32[512,400]{1,0:T(8,128)S(1)} %scatter_custom_fusion.1, s32[512]{0:T(512)S(1)} %bitcast.65, f32[64,8,400]{2,1,0:T(8,128)} %all-to-all-done.5), kind=kCustom, calls=%fused_computation.18 | custom fusion | flops 204800 | bytes 1638400 | tf_op jit(solution)/shard_map/scatter-add | solution.py:54
  296.2 0.0 copy-start.2
  296.2 1.0 copy-done.2
  297.2 0.0 all-reduce.2.cloned.1.call-update
  297.3 0.0 copy-start.9
  297.3 74.5 %all-reduce.2.cloned.1.call-done = f32[512,400]{1,0:T(8,128)} async-done(((f32[512,400]{1,0:T(8,128)}), f32[512,400]{1,0:T(8,128)}) %all-reduce.2.cloned.1.call-update) | async-done | bytes 819216 | tf_op jit(solution)/shard_map/psum | solution.py:55
  371.8 1.5 multiply_reduce_fusion
  373.3 0.0 copy-done.9
  373.3 0.6 fusion.20
  373.8 0.2 divide_subtract_fusion
  374.1 1.2 copy.47
  (19 shorter events, 0.1 us)
Async XLA Ops:
  8.6 19.9 %copy-start.8 = (s32[1,1,512]{2,1,0:T(1,128)S(1)}, s32[1,1,512]{2,1,0:T(1,128)}, u32[]{:S(2)}) copy-start(s32[1,1,512]{2,1,0:T(1,128)} %param.15) | copy-start | bytes 6148
  8.6 33.0 %all-to-all-start = ((s32[64,1,8]{2,1,0:T(1,128)}), s32[64,1,8]{2,1,0:T(1,128)S(1)}, u32[]{:S(2)}, u32[]{:S(2)}) async-start(s32[64,1,8]{2,1,0:T(1,128)} %bitcast.6), calls=%async_computation | async-start | bytes 65536 | tf_op jit(solution)/shard_map/all_to_all | solution.py:39
  41.6 18.1 %all-to-all-start.2 = ((s32[64,1,8]{2,1,0:T(1,128)}), s32[64,1,8]{2,1,0:T(1,128)S(1)}, u32[]{:S(2)}, u32[]{:S(2)}) async-start(s32[64,1,8]{2,1,0:T(1,128)} %bitcast.10), calls=%async_computation.2 | async-start | bytes 65536 | tf_op jit(solution)/shard_map/all_to_all | solution.py:25
  59.7 53.4 %all-to-all-start.1 = ((f32[64,8,400]{2,1,0:T(8,128)}), f32[64,8,400]{2,1,0:T(8,128)S(1)}, u32[]{:S(2)}, u32[]{:S(2)}) async-start(f32[64,8,400]{2,1,0:T(8,128)} %bitcast.8), calls=%async_computation.1 | async-start | bytes 2097152 | tf_op jit(solution)/shard_map/all_to_all | solution.py:40
  113.0 1.0 copy-start
  113.1 11.6 %copy-start.5 = (s32[1,1,64,8]{2,3,1,0:T(8,128)S(1)}, s32[1,1,64,8]{2,3,1,0:T(8,128)}, u32[]{:S(2)}) copy-start(s32[1,1,64,8]{2,3,1,0:T(8,128)} %param.11) | copy-start | bytes 6148
  113.1 12.6 %copy-start.4 = (f32[237,400]{0,1:T(8,128)S(1)}, f32[237,400]{0,1:T(8,128)}, u32[]{:S(2)}) copy-start(f32[237,400]{0,1:T(8,128)} %param.10) | copy-start | bytes 1137604
  114.1 59.7 %all-to-all-start.3 = ((f32[64,8,400]{2,1,0:T(8,128)}), f32[64,8,400]{2,1,0:T(8,128)}, u32[]{:S(2)}, u32[]{:S(2)}) async-start(f32[64,8,400]{2,1,0:T(8,128)} %bitcast.12), calls=%async_computation.3 | async-start | bytes 2097152 | tf_op jit(solution)/shard_map/all_to_all | solution.py:26
  124.8 0.7 copy-start.6
  131.6 0.7 copy-start.7
  173.7 59.0 %all-to-all-start.4 = ((f32[64,8,400]{2,1,0:T(8,128)}), f32[64,8,400]{2,1,0:T(8,128)}, u32[]{:S(2)}, u32[]{:S(2)}) async-start(f32[64,8,400]{2,1,0:T(8,128)} %broadcast_multiply_fusion), calls=%async_computation.4 | async-start | bytes 2097152 | tf_op jit(solution)/shard_map/all_to_all | solution.py:44
  194.9 49.7 %copy-start.1 = (f32[64,8,400]{2,1,0:T(8,128)S(1)}, f32[64,8,400]{2,1,0:T(8,128)}, u32[]{:S(2)}) copy-start(f32[64,8,400]{2,1,0:T(8,128)} %copy-done) | copy-start | bytes 2457604
  232.7 58.7 %all-to-all-start.5 = ((f32[64,8,400]{2,1,0:T(8,128)}), f32[64,8,400]{2,1,0:T(8,128)}, u32[]{:S(2)}, u32[]{:S(2)}) async-start(f32[64,8,400]{2,1,0:T(8,128)} %fusion.6), calls=%async_computation.5 | async-start | bytes 2097152 | tf_op jit(solution)/shard_map/all_to_all | solution.py:36
  242.7 129.1 %all-reduce.2.cloned.1.call-start = ((), (), s32[]{:S(2)}) async-start(), calls=%async_computation.6 | async-start | bytes 2097152 | tf_op jit(solution)/shard_map/psum | solution.py:55
  296.2 1.0 copy-start.2
  297.3 76.0 %copy-start.9 = (f32[512]{0:T(512)S(1)}, f32[512]{0:T(512)}, u32[]{:S(2)}) copy-start(f32[512]{0:T(512)} %param.9) | copy-start | bytes 6148
  371.8 2.1 copy-start.3
Sparse Core Ops, SparseCore 0:
  297.4 74.3 all-reduce.1
where the time goes:
time: 384 us; the launch traced here: 382 us
  waiting for transfers between devices  253 us (66%)
  starting transfers between devices  59.4 us (15%)
  other arithmetic  21.7 us (6%)
  local copies, waits for them, and re-layouts  20.9 us (5%)
  between operations  14.3 us (4%)
  matrix products  12.7 us (3%)
    psum x1, waiting for transfers between devices, per_device(): summed = lax.psum(grad, 'rep')  74.5 us
    all_to_all x1, waiting for transfers between devices, per_device(): lax.all_to_all(entity[slot_ids], 'dom', split_axis=0, concat_axis=0, tile...  46.3 us
    all_to_all x1, waiting for transfers between devices, per_device(): lax.all_to_all(entity[rows_in], 'dom', split_axis=0, concat_axis=0, tiled...  40.2 us
    all_to_all x1, waiting for transfers between devices, per_device(): lax.all_to_all(pos_coef[:, :, None] * query, 'dom', split_axis=0, concat_...  37.9 us
    all_to_all x1, waiting for transfers between devices, per_device(): lax.all_to_all(noise_term.reshape(buckets, -1, features), 'dom', split_ax...  33 us
    all_to_all x1, starting transfers between devices, per_device(): lax.all_to_all(dst_rows[0, 0], 'dom', split_axis=0, concat_axis=0, tiled=...  19.4 us
    all_to_all x1, waiting for transfers between devices, per_device(): lax.all_to_all(noise_local, 'dom', split_axis=0, concat_axis=0, tiled=True)  11 us
    all_to_all x1, starting transfers between devices, per_device(): lax.all_to_all(entity[rows_in], 'dom', split_axis=0, concat_axis=0, tiled...  10.6 us
  transfers between devices with their start and end apart: 7, of which 7 were waited for; matrix products, arithmetic and copies ran while one was open for 11% of the time, Pallas kernels for 0%

commit v1 on v0

v1 whole, which is shorter than its diff:
```python
import functools

import jax
import jax.numpy as jnp
from jax import lax
from jax.experimental import pallas as pl
from jax.experimental.pallas import tpu as pltpu
from jax.sharding import Mesh
from jax.sharding import PartitionSpec as P

LEARN_RATE = 0.3
F32 = jnp.float32
BF16 = jnp.bfloat16
NN = (((1,), (0,)), ((), ()))
NT = (((1,), (1,)), ((), ()))


def round_up(value, unit):
    return -(-value // unit) * unit


def one_hot(row, rows):
    place = lax.broadcasted_iota(jnp.int32, (rows, row.shape[1]), 0)
    return (place == row).astype(F32).astype(BF16)


def split(x, terms):
    out = []
    for _ in range(terms):
        part = x.astype(BF16)
        out.append(part)
        x = x - part.astype(F32)
    return out


def mul(a, b, dims=NN):
    return lax.dot_general(a, b, dims, preferred_element_type=F32)


def pick(x, hot, dims=NN, terms=3):
    parts = split(x, terms)
    out = mul(parts[-1], hot, dims)
    for part in parts[-2::-1]:
        out = out + mul(part, hot, dims)
    return out


def product(a, b, dims=NN):
    a_high, a_low = split(a, 2)
    b_high, b_low = split(b, 2)
    return mul(a_low, b_high, dims) + mul(a_high, b_low, dims) + mul(a_high, b_high, dims)


def with_rows(x, extra, width):
    rest = width - x.shape[0]
    place = lax.broadcasted_iota(jnp.int32, (rest, x.shape[1]), 0)
    block = jnp.zeros((rest, x.shape[1]), F32)
    for i, row in enumerate(extra):
        block = jnp.where(place == i, row, block)
    return jnp.concatenate([x, block], axis=0)


def put_messages(msg_ref, rows, nz, ny):
    slots = msg_ref.shape[1]
    for y in range(ny):
        for z in range(nz):
            at = (y * nz + z) * slots
            msg_ref[z * ny + y] = rows[at : at + slots]


def query_kernel(nz, ny, et_ref, relt_ref, src_ref, rel_ref, dst_ref, live_ref, qt_ref, relation_ref, msg_ref):
    source = pick(et_ref[...], one_hot(src_ref[...], et_ref.shape[1]))
    relation = pick(relt_ref[...], one_hot(rel_ref[...], relt_ref.shape[1]))
    query = source * relation
    qt_ref[...] = query
    relation_ref[...] = relation
    full = with_rows(query, [dst_ref[...].astype(F32), live_ref[...]], msg_ref.shape[2])
    put_messages(msg_ref, full.T, nz, ny)


def owner_kernel(msg_ref, et_ref, grad_ref):
    features, rows = et_ref.shape
    full = msg_ref[...].reshape(-1, msg_ref.shape[2]).T
    query = full[:features]
    hot = one_hot(full[features : features + 1].astype(jnp.int32), rows)
    live = full[features + 1 : features + 2]
    target = pick(et_ref[...], hot)
    positive = jnp.sum(query * target, axis=0, keepdims=True)
    coef = -jax.nn.sigmoid(-positive) * live
    grad_ref[...] = pick(coef * query, hot, NT, 2)


def table_kernel(table_ref, ids_ref, out_ref, got_ref):
    nz, fs, rows = table_ref.shape
    devices = out_ref.shape[0]
    slots = ids_ref.shape[2] // (2 * devices)
    span = nz * slots

    def fetch(z, carry):
        got_ref[z] = pick(table_ref[z], one_hot(ids_ref[z], rows))
        return carry

    lax.fori_loop(0, nz, fetch, 0)
    lane = lax.broadcasted_iota(jnp.int32, (8, span), 1) // slots

    def turn(f8, carry):
        at = pl.ds(pl.multiple_of(f8 * 8, 8), 8)
        for kind in range(2):
            for tile in range(devices // nz):
                start = (kind * devices + tile * nz) * slots
                v = [got_ref[z, at, start : start + span] for z in range(nz)]
                k = nz // 2
                while k:
                    low = (lane & k) == 0
                    w = list(v)
                    for i in range(nz):
                        if not i & k:
                            a, b = v[i], v[i + k]
                            w[i] = jnp.where(low, a, pltpu.roll(b, k * slots, 1))
                            w[i + k] = jnp.where(low, pltpu.roll(a, span - k * slots, 1), b)
                    v = w
                    k //= 2
                for i in range(nz):
                    out_ref[tile * nz + i, at, kind * span : (kind + 1) * span] = v[i]
        return carry

    lax.fori_loop(0, fs // 8, turn, 0)


def lanes_of(got_ref, kind, ny, features):
    devices, fs, lanes = got_ref.shape
    span = lanes // 2
    blocks = []
    per = devices // ny
    for y in range(ny):
        block = got_ref[y * per : (y + 1) * per, :, kind * span : (kind + 1) * span]
        blocks.append(block.reshape(per * fs, span)[:features])
    return jnp.concatenate(blocks, axis=1)


def noise_kernel(nz, ny, got_ref, qt_ref, live_ref, ids_ref, coef_ref, msg_ref):
    features = qt_ref.shape[0]
    noise = lanes_of(got_ref, 0, ny, features)
    query = qt_ref[...]
    scores = product(noise.T, query)
    coef = jax.nn.sigmoid(scores) * live_ref[...]
    coef_ref[...] = coef
    grad = product(query, coef, NT)
    full = with_rows(grad, [ids_ref[...].astype(F32)], msg_ref.shape[2])
    put_messages(msg_ref, full.T, nz, ny)


def source_kernel(ny, got_ref, qt_ref, relation_ref, live_ref, src_ref, coef_ref, owned_ref, out_ref):
    features = qt_ref.shape[0]
    noise = lanes_of(got_ref, 0, ny, features)
    target = lanes_of(got_ref, 1, ny, features)
    back = product(noise, coef_ref[...])
    positive = jnp.sum(qt_ref[...] * target, axis=0, keepdims=True)
    coef = -jax.nn.sigmoid(-positive) * live_ref[...]
    grad = relation_ref[...] * (coef * target + back)
    hot = one_hot(src_ref[...], owned_ref.shape[1])
    out_ref[...] = owned_ref[...] + pick(grad, hot, NT, 2)


def scatter_kernel(msg_ref, early_ref, out_ref):
    features, rows = early_ref.shape
    reps, fs, _ = out_ref.shape
    full = msg_ref[...].reshape(-1, msg_ref.shape[2]).T
    hot = one_hot(full[features : features + 1].astype(jnp.int32), rows)
    grad = early_ref[...] + pick(full[:features], hot, NT, 2)
    rest = reps * fs - features
    if rest:
        grad = jnp.concatenate([grad, jnp.zeros((rest, rows), F32)], axis=0)
    out_ref[...] = grad.reshape(reps, fs, rows)


def update_kernel(grad_ref, et_ref, state_ref, entity_ref, new_state_ref):
    features, rows = et_ref.shape
    grad = grad_ref[...].reshape(-1, rows)[:features]
    state = state_ref[...] + jnp.sum(grad * grad, axis=0, keepdims=True) * (1.0 / features)
    new_state_ref[...] = state
    entity_ref[...] = et_ref[...] - LEARN_RATE * grad / jnp.sqrt(state)


def call(kernel, outs, *args, scratch=(), flops=0):
    shapes = [jax.ShapeDtypeStruct(shape, F32) for shape in outs]
    moved = sum(4 * a.size for a in args) + sum(4 * s.size for s in shapes)
    return pl.pallas_call(
        kernel,
        out_shape=shapes,
        scratch_shapes=list(scratch),
        cost_estimate=pl.CostEstimate(flops=flops, bytes_accessed=moved, transcendentals=0),
        compiler_params=pltpu.CompilerParams(vmem_limit_bytes=48 << 20),
    )(*args)


def per_device(entity, adagrad_state, relation, src_rows, dst_rows, rel_ids, bucket_counts, noise_rows):
    nz, ny, reps = lax.axis_size("z"), lax.axis_size("y"), lax.axis_size("rep")
    rows, features = entity.shape
    slots = src_rows.shape[3]
    parts = nz * ny
    edges = parts * slots
    fs = round_up(features, reps * 8) // reps
    width = round_up(features + 2, 128)

    def ordered(ids):
        return ids.reshape(nz, ny, slots).transpose(1, 0, 2)

    et = entity.T
    padded = jnp.pad(et, ((0, reps * fs - features), (0, 0)))
    mine = lax.dynamic_slice_in_dim(padded, lax.axis_index("rep") * fs, fs, 0)
    table = lax.all_gather(mine, "z")

    src = ordered(src_rows).reshape(1, edges)
    rel = ordered(rel_ids).reshape(1, edges)
    dst = ordered(dst_rows)
    noise = ordered(noise_rows)
    live = (jnp.arange(slots, dtype=jnp.int32) < bucket_counts.reshape(nz, ny).T[:, :, None]).astype(F32)
    live = live.reshape(1, edges)

    wanted = jnp.stack([noise.reshape(ny, -1), dst.reshape(ny, -1)], axis=1)
    wanted = jnp.broadcast_to(wanted[:, None], (ny, reps) + wanted.shape[1:])
    asked = lax.all_to_all(
        wanted.reshape(ny * reps, 2, nz * slots), ("y", "rep"), split_axis=0, concat_axis=0, tiled=True
    )
    asked = asked.reshape(ny * reps, 2, nz, slots).transpose(2, 1, 0, 3).reshape(nz, 1, -1)

    dst = dst.reshape(1, edges)
    noise = noise.reshape(1, edges)
    relt = jnp.pad(relation.T, ((0, 0), (0, round_up(relation.shape[0], 128) - relation.shape[0])))
    dense = (features, rows)
    unit = 2 * edges * features * rows
    qt, relation_rows, queries = call(
        functools.partial(query_kernel, nz, ny),
        [(features, edges), (features, edges), (parts, slots, width)],
        et, relt, src, rel, dst, live,
        flops=5 * unit,
    )
    queries = lax.all_to_all(queries, ("z", "y"), split_axis=0, concat_axis=0, tiled=True)
    (owned,) = call(owner_kernel, [dense], queries, et, flops=5 * unit)
    (found,) = call(
        table_kernel,
        [(ny * reps, fs, 2 * nz * slots)],
        table, asked,
        scratch=[pltpu.VMEM((nz, fs, 2 * ny * reps * slots), F32)],
        flops=8 * unit,
    )
    got = lax.all_to_all(found, ("y", "rep"), split_axis=0, concat_axis=0, tiled=True)
    coef, noise_grads = call(
        functools.partial(noise_kernel, nz, ny),
        [(edges, edges), (parts, slots, width)],
        got, qt, live, noise,
        flops=6 * unit,
    )
    noise_grads = lax.all_to_all(noise_grads, ("z", "y"), split_axis=0, concat_axis=0, tiled=True)
    (early,) = call(
        functools.partial(source_kernel, ny),
        [dense],
        got, qt, relation_rows, live, src, coef, owned,
        flops=5 * unit,
    )
    (partial,) = call(scatter_kernel, [(reps, fs, rows)], noise_grads, early, flops=2 * unit)
    shares = lax.all_to_all(partial, "rep", split_axis=0, concat_axis=0, tiled=True)
    summed = lax.all_gather(jnp.sum(shares, axis=0), "rep")
    new_entity, new_state = call(
        update_kernel, [dense, (1, rows)], summed, et, adagrad_state.reshape(1, rows)
    )
    return new_entity.T, new_state.reshape(rows)


def solution(mesh):
    dom, reps = mesh.devices.shape
    ny = 4 if dom >= 16 else 2
    split_mesh = Mesh(mesh.devices.reshape(dom // ny, ny, reps), ("z", "y", "rep"))
    zy = ("z", "y")
    return jax.shard_map(
        per_device,
        mesh=split_mesh,
        in_specs=(
            P(zy, None),
            P(zy),
            P(),
            P(zy, "rep", None, None),
            P(zy, "rep", None, None),
            P(zy, "rep", None, None),
            P(zy, "rep", None),
            P(zy, "rep", None),
        ),
        out_specs=(P(zy, None), P(zy)),
        check_vma=False,
    )
```

time: 384 us -> 304 us (0.79)
  waiting for transfers between devices: 253 us -> 162 us
  blocking collectives: 0 us -> 52.9 us
  starting transfers between devices: 59.4 us -> 35.5 us
  other arithmetic: 21.7 us -> 2.16 us
  Pallas kernels: 0 us -> 18.1 us
  matrix products: 12.7 us -> 0 us
    psum x1 -> x0, waiting for transfers between devices: 74.5 us -> none  [per_device(): summed = lax.psum(grad, 'rep')]
    all_to_all x6 -> x3, waiting for transfers between devices: 179 us -> 111 us  [the longest x1 47.3 us: per_device(): lax.all_to_all(queries, ('z', 'y'), split_axis=0, concat_axis=0, tiled=True)]
    all_gather x0 -> x1, waiting for transfers between devices: none -> 50.7 us  [per_device(): table = lax.all_gather(mine, 'z')]
    all_to_all x0 -> x2, blocking collectives: none -> 38.6 us  [the longest x1 21.7 us: per_device(): lax.all_to_all(partial, 'rep', split_axis=0, concat_axis=0, tiled=True)]
    all_to_all x6 -> x3, starting transfers between devices: 59.4 us -> 35.4 us  [the longest x1 16.7 us: per_device(): lax.all_to_all(found, ('y', 'rep'), split_axis=0, concat_axis=0, tiled=True)]
    pallas_call x0 -> x7, Pallas kernels: none -> 18.1 us  [call(): pl.pallas_call(kernel, out_shape=shapes, scratch_shapes=list(scratch), co...]
    all_gather x0 -> x1, blocking collectives: none -> 14.3 us  [per_device(): summed = lax.all_gather(jnp.sum(shares, axis=0), 'rep')]
    scatter-add x3 -> x0, other arithmetic: 14.2 us -> none  [the longest x1 4.95 us: per_device(): grad = grad.at[slot_ids.reshape(-1)].add(owner_grads.reshape(-1, features))]
  transfers between devices with their start and end apart: 7 -> 4, of which waited for: 7 -> 4; matrix products, arithmetic and copies ran while one was open for 11% -> 2% of each run, Pallas kernels for 0% -> 2%
where the time goes in v1:
time: 304 us; the launch traced here: 303 us
  waiting for transfers between devices  162 us (53%)
  blocking collectives  52.9 us (17%)
  starting transfers between devices  35.5 us (12%)
  local copies, waits for them, and re-layouts  18.6 us (6%)
  Pallas kernels  18.1 us (6%)
  between operations  14.3 us (5%)
    all_gather x1, waiting for transfers between devices, per_device(): table = lax.all_gather(mine, 'z')  50.7 us
    all_to_all x1, waiting for transfers between devices, per_device(): lax.all_to_all(queries, ('z', 'y'), split_axis=0, concat_axis=0, tiled=True)  47.3 us
    all_to_all x1, waiting for transfers between devices, per_device(): lax.all_to_all(noise_grads, ('z', 'y'), split_axis=0, concat_axis=0, tile...  44.5 us
    all_to_all x1, blocking collectives, per_device(): lax.all_to_all(partial, 'rep', split_axis=0, concat_axis=0, tiled=True)  21.7 us
    all_to_all x1, waiting for transfers between devices, per_device(): lax.all_to_all(found, ('y', 'rep'), split_axis=0, concat_axis=0, tiled=True)  19.2 us
    pallas_call x7, Pallas kernels, call(): pl.pallas_call(kernel, out_shape=shapes, scratch_shapes=list(scratch), co...  18.1 us
    all_to_all x1, blocking collectives, per_device(): lax.all_to_all(wanted.reshape(ny * reps, 2, nz * slots), ('y', 'rep'), sp...  16.9 us
    all_to_all x1, starting transfers between devices, per_device(): lax.all_to_all(found, ('y', 'rep'), split_axis=0, concat_axis=0, tiled=True)  16.7 us
  transfers between devices with their start and end apart: 4, of which 4 were waited for; matrix products, arithmetic and copies ran while one was open for 2% of the time, Pallas kernels for 2%

profile of v1, /device:TPU:1, one launch (start us, length us, event | category | flops | bytes accessed | tf_op | source)
XLA Modules:
  0.0 303.2 jit_solution(15466879777719730725)
XLA Ops:
  7.2 0.0 all-gather.4.cloned.1.call-start
  7.2 1.6 pad_dynamic-slice_fusion
  8.8 0.0 all-gather.4.cloned.1.call-update
  8.8 0.5 broadcast.16
  9.3 1.3 reduce.6
  10.7 0.1 reshape.76
  10.8 0.1 stack_reshape.6
  10.9 0.8 copy.43
  11.6 0.1 stack_reshape.7
  11.8 16.9 %all_to_all.25 = s32[32,2,128]{2,1,0:T(2,128)S(1)} all-to-all(s32[32,2,128]{2,1,0:T(2,128)S(1)} %copy.45), channel_id=1, replica_groups=mesh['z'=16,'y'=4,'rep'=8] {'y','rep'}, dimensions={0} | all-to-all | bytes 65536 | tf_op jit(solution)/shard_map/all_to_all | solution.py:223
  28.7 0.1 copy.46
  28.8 0.2 copy.47
  28.9 0.1 copy.48.ids_ref
  29.0 50.7 %all-gather.4.cloned.1.call-done = f32[896,512]{1,0:T(8,128)} async-done(((f32[56,512]{1,0:T(8,128)}), f32[896,512]{1,0:T(8,128)}) %all-gather.4.cloned.1.call-update) | async-done | bytes 1835024 | tf_op jit(solution)/shard_map/all_gather | solution.py:212
  79.7 1.5 copy-done.18
  81.2 9.9 %shard_map.95 = f32[32,56,256]{2,1,0:T(8,128)S(1)} custom-call(f32[16,56,512]{2,1,0:T(8,128)S(1)} %bitcast.30, s32[16,1,512]{2,1,0:T(1,128)S(1)} %copy.48.ids_ref), custom_call_target="tpu_custom_call" | custom-call | flops 1677721600 | bytes 3702784 | tf_op jit(solution)/shard_map/pallas_call | solution.py:188
  91.2 0.0 copy-start.5
  91.2 1.2 copy-done.5
  92.4 0.0 copy-start
  92.5 16.7 %all-to-all-start.1 = ((f32[32,56,256]{2,1,0:T(8,128)}), f32[32,56,256]{2,1,0:T(8,128)S(1)}, u32[]{:S(2)}, u32[]{:S(2)}) async-start(f32[32,56,256]{2,1,0:T(8,128)} %copy-done.5), calls=%async_computation.1 | async-start | bytes 3670016 | tf_op jit(solution)/shard_map/all_to_all | solution.py:248
  109.1 0.1 reshape.85.dst_ref
  109.2 0.0 copy-done.22
  109.2 0.7 reduce.7
  109.9 0.1 reshape.86
  110.0 0.1 copy.54
  110.1 0.1 fusion
  110.2 0.1 reshape.90.live_ref
  110.3 0.1 copy.49
  110.4 0.1 reshape.82.src_ref
  110.5 0.1 copy.51
  110.6 0.1 reshape.84.rel_ref
  110.7 0.0 copy-done.19
  110.7 0.0 copy-done
  110.7 1.4 shard_map.96
  112.1 1.0 copy-done.7
  113.1 0.9 copy-done.12
  114.0 0.9 copy-done.15
  114.9 19.2 %all-to-all-done.1.got_ref = f32[32,56,256]{2,1,0:T(8,128)S(1)} async-done(((f32[32,56,256]{2,1,0:T(8,128)}), f32[32,56,256]{2,1,0:T(8,128)S(1)}, u32[]{:S(2)}, u32[]{:S(2)}) %all-to-all-start.1) | async-done | bytes 1835040 | tf_op jit(solution)/shard_map/all_to_all | solution.py:248
  134.1 10.8 %all-to-all-start.3 = ((f32[64,8,512]{2,1,0:T(8,128)}), f32[64,8,512]{2,1,0:T(8,128)S(1)}, u32[]{:S(2)}, u32[]{:S(2)}) async-start(f32[64,8,512]{2,1,0:T(8,128)} %copy-done.7), calls=%async_computation.3 | async-start | bytes 2097152 | tf_op jit(solution)/shard_map/all_to_all | solution.py:239
  144.9 0.1 reshape.87.ids_ref
  145.0 1.1 copy-done.13
  146.1 2.1 shard_map.97
  148.2 1.0 copy-done.6
  149.2 1.0 copy-done.10
  150.2 47.3 %all-to-all-done.3.msg_ref = f32[64,8,512]{2,1,0:T(8,128)S(1)} async-done(((f32[64,8,512]{2,1,0:T(8,128)}), f32[64,8,512]{2,1,0:T(8,128)S(1)}, u32[]{:S(2)}, u32[]{:S(2)}) %all-to-all-start.3) | async-done | bytes 1048608 | tf_op jit(solution)/shard_map/all_to_all | solution.py:239
  197.5 1.0 copy-done.8
  198.4 7.9 %all-to-all-start.2 = ((f32[64,8,512]{2,1,0:T(8,128)}), f32[64,8,512]{2,1,0:T(8,128)S(1)}, u32[]{:S(2)}, u32[]{:S(2)}) async-start(f32[64,8,512]{2,1,0:T(8,128)} %copy-done.6), calls=%async_computation.2 | async-start | bytes 2097152 | tf_op jit(solution)/shard_map/all_to_all | solution.py:255
  206.4 0.0 copy-start.1
  206.4 1.1 copy-done.1
  207.5 1.2 copy-done.9
  208.8 1.5 shard_map.98.owned_ref
  210.3 0.1 copy-done.16
  210.5 1.4 shard_map.99.early_ref
  211.8 0.0 copy-start.3
  211.8 0.9 copy-done.3
  212.7 44.5 %all-to-all-done.2.msg_ref = f32[64,8,512]{2,1,0:T(8,128)S(1)} async-done(((f32[64,8,512]{2,1,0:T(8,128)}), f32[64,8,512]{2,1,0:T(8,128)S(1)}, u32[]{:S(2)}, u32[]{:S(2)}) %all-to-all-start.2) | async-done | bytes 1048608 | tf_op jit(solution)/shard_map/all_to_all | solution.py:255
  257.3 1.1 copy-done.4
  258.4 0.7 shard_map.100
  259.1 0.0 copy-start.2
  259.1 0.0 copy-start.17
  259.2 21.7 %all_to_all.26 = f32[8,56,512]{2,1,0:T(8,128)S(1)} all-to-all(f32[8,56,512]{2,1,0:T(8,128)S(1)} %shard_map.100), channel_id=1, replica_groups=mesh['z'=16,'y'=4,'rep'=8] {'rep'}, dimensions={0} | all-to-all | bytes 1835008 | tf_op jit(solution)/shard_map/all_to_all | solution.py:263
  280.9 0.1 reduce_sum.9
  281.0 14.3 %all-gather.1 = f32[448,512]{1,0:T(8,128)S(1)} all-gather(f32[56,512]{1,0:T(8,128)S(1)} %reduce_sum.9), channel_id=3, replica_groups=mesh['z'=16,'y'=4,'rep'=8] {'rep'}, dimensions={0}, use_global_device_ids=true | all-gather | bytes 1032192 | tf_op jit(solution)/shard_map/all_gather | solution.py:264
  295.3 1.1 shard_map.101
  (31 shorter events, 0.1 us)
Async XLA Ops:
  7.2 72.6 %all-gather.4.cloned.1.call-start = ((), (), s32[]{:S(2)}) async-start(), calls=%async_computation.5 | async-start | bytes 1949696 | tf_op jit(solution)/shard_map/all_gather | solution.py:212
  79.7 1.5 copy-start.18
  91.2 1.3 copy-start.5
  92.4 16.8 %copy-start.22 = (s32[1,1,64]{2,1,0:T(1,128)S(1)}, s32[1,1,64]{2,1,0:T(1,128)}, u32[]{:S(2)}) copy-start(s32[1,1,64]{2,1,0:T(1,128)} %param.14) | copy-start | bytes 772
  92.4 17.8 %copy-start.20 = (s32[1,1,64,8]{2,3,1,0:T(8,128)S(1)}, s32[1,1,64,8]{2,3,1,0:T(8,128)}, u32[]{:S(2)}) copy-start(s32[1,1,64,8]{2,3,1,0:T(8,128)} %param.11) | copy-start | bytes 6148
  92.4 18.0 %copy-start.21 = (s32[1,1,64,8]{2,3,1,0:T(8,128)S(1)}, s32[1,1,64,8]{2,3,1,0:T(8,128)}, u32[]{:S(2)}) copy-start(s32[1,1,64,8]{2,3,1,0:T(8,128)} %param.13) | copy-start | bytes 6148
  92.4 18.2 %copy-start.19 = (f32[237,400]{0,1:T(8,128)S(1)}, f32[237,400]{0,1:T(8,128)}, u32[]{:S(2)}) copy-start(f32[237,400]{0,1:T(8,128)} %param.10) | copy-start | bytes 1137604
  92.4 18.3 %copy-start = (f32[512,400]{0,1:T(8,128)S(1)}, f32[512,400]{0,1:T(8,128)}, u32[]{:S(2)}) copy-start(f32[512,400]{0,1:T(8,128)} %param.8) | copy-start | bytes 2457604
  92.5 41.6 %all-to-all-start.1 = ((f32[32,56,256]{2,1,0:T(8,128)}), f32[32,56,256]{2,1,0:T(8,128)S(1)}, u32[]{:S(2)}, u32[]{:S(2)}) async-start(f32[32,56,256]{2,1,0:T(8,128)} %copy-done.5), calls=%async_computation.1 | async-start | bytes 3670016 | tf_op jit(solution)/shard_map/all_to_all | solution.py:248
  112.1 1.0 copy-start.7
  113.1 0.9 copy-start.12
  114.0 0.9 copy-start.15
  134.1 63.4 %all-to-all-start.3 = ((f32[64,8,512]{2,1,0:T(8,128)}), f32[64,8,512]{2,1,0:T(8,128)S(1)}, u32[]{:S(2)}, u32[]{:S(2)}) async-start(f32[64,8,512]{2,1,0:T(8,128)} %copy-done.7), calls=%async_computation.3 | async-start | bytes 2097152 | tf_op jit(solution)/shard_map/all_to_all | solution.py:239
  145.0 1.1 copy-start.13
  148.2 1.0 copy-start.6
  149.2 1.0 copy-start.10
  197.5 1.0 copy-start.8
  198.4 58.8 %all-to-all-start.2 = ((f32[64,8,512]{2,1,0:T(8,128)}), f32[64,8,512]{2,1,0:T(8,128)S(1)}, u32[]{:S(2)}, u32[]{:S(2)}) async-start(f32[64,8,512]{2,1,0:T(8,128)} %copy-done.6), calls=%async_computation.2 | async-start | bytes 2097152 | tf_op jit(solution)/shard_map/all_to_all | solution.py:255
  206.4 1.1 copy-start.1
  207.5 1.2 copy-start.9
  208.7 1.5 copy-start.11
  208.8 1.6 copy-start.14
  208.8 1.7 copy-start.16
  211.8 0.9 copy-start.3
  257.3 1.1 copy-start.4
  259.1 36.2 %copy-start.2 = (f32[512,400]{0,1:T(8,128)S(1)}, f32[512,400]{0,1:T(8,128)}, u32[]{:S(2)}) copy-start(f32[512,400]{0,1:T(8,128)} %param.8) | copy-start | bytes 2457604
  259.1 36.1 %copy-start.17 = (f32[512]{0:T(512)S(1)}, f32[512]{0:T(512)}, u32[]{:S(2)}) copy-start(f32[512]{0:T(512)} %param.9) | copy-start | bytes 6148
Sparse Core Ops, SparseCore 0:
  10.7 69.0 all-gather.3

commit v2 on v1

--- a/solution.py
+++ b/solution.py
@@ -38,11 +38,10 @@
 
 
 def pick(x, hot, dims=NN, terms=3):
-    parts = split(x, terms)
-    out = mul(parts[-1], hot, dims)
-    for part in parts[-2::-1]:
-        out = out + mul(part, hot, dims)
-    return out
+    n = x.shape[0]
+    parts = [part.astype(F32) for part in split(x, terms)]
+    out = mul(jnp.concatenate(parts, axis=0).astype(BF16), hot, dims)
+    return sum(out[i * n : (i + 1) * n] for i in range(terms - 1, -1, -1))
 
 
 def product(a, b, dims=NN):
@@ -100,7 +99,7 @@
         got_ref[z] = pick(table_ref[z], one_hot(ids_ref[z], rows))
         return carry
 
-    lax.fori_loop(0, nz, fetch, 0)
+    lax.fori_loop(0, nz, fetch, 0, unroll=4)
     lane = lax.broadcasted_iota(jnp.int32, (8, span), 1) // slots
 
     def turn(f8, carry):
@@ -237,14 +236,15 @@
         flops=5 * unit,
     )
     queries = lax.all_to_all(queries, ("z", "y"), split_axis=0, concat_axis=0, tiled=True)
-    (owned,) = call(owner_kernel, [dense], queries, et, flops=5 * unit)
     (found,) = call(
         table_kernel,
         [(ny * reps, fs, 2 * nz * slots)],
         table, asked,
         scratch=[pltpu.VMEM((nz, fs, 2 * ny * reps * slots), F32)],
-        flops=8 * unit,
-    )
+        flops=1000 * unit,
+    )
+    queries, found = lax.optimization_barrier((queries, found))
+    (owned,) = call(owner_kernel, [dense], queries, et, flops=5 * unit)
     got = lax.all_to_all(found, ("y", "rep"), split_axis=0, concat_axis=0, tiled=True)
     coef, noise_grads = call(
         functools.partial(noise_kernel, nz, ny),

time: 304 us -> 268 us (0.88)
  waiting for transfers between devices: 162 us -> 134 us
  blocking collectives: 52.9 us -> 34.3 us
  starting transfers between devices: 35.5 us -> 50.2 us
  local copies, waits for them, and re-layouts: 18.6 us -> 15.4 us
    all_to_all x1, waiting for transfers between devices: 47.3 us -> 0.01 us  [per_device(): lax.all_to_all(queries, ('z', 'y'), split_axis=0, concat_axis=0, tiled=True)]
    all_to_all x1 -> x0, blocking collectives: 16.9 us -> none  [per_device(): lax.all_to_all(wanted.reshape(ny * reps, 2, nz * slots), ('y', 'rep'), sp...]
    all_gather x1, waiting for transfers between devices: 50.7 us -> 62 us  [per_device(): table = lax.all_gather(mine, 'z')]
    all_to_all x0 -> x1, starting transfers between devices: none -> 10.4 us  [per_device(): lax.all_to_all(wanted.reshape(ny * reps, 2, nz * slots), ('y', 'rep'), sp...]
    all_to_all x1, waiting for transfers between devices: 19.2 us -> 24.8 us  [per_device(): lax.all_to_all(found, ('y', 'rep'), split_axis=0, concat_axis=0, tiled=True)]
    all_to_all x1, starting transfers between devices: 10.8 us -> 16.4 us  [per_device(): lax.all_to_all(queries, ('z', 'y'), split_axis=0, concat_axis=0, tiled=True)]
    all_to_all x1, starting transfers between devices: 16.7 us -> 11.2 us  [per_device(): lax.all_to_all(found, ('y', 'rep'), split_axis=0, concat_axis=0, tiled=True)]
    all_to_all x1, starting transfers between devices: 7.92 us -> 12.2 us  [per_device(): lax.all_to_all(noise_grads, ('z', 'y'), split_axis=0, concat_axis=0, tile...]
  transfers between devices with their start and end apart: 4 -> 5, of which waited for: 4 -> 4; matrix products, arithmetic and copies ran while one was open for 2% -> 3% of each run, Pallas kernels for 2% -> 5%
where the time goes in v2:
time: 268 us; the launch traced here: 267 us
  waiting for transfers between devices  134 us (50%)
  starting transfers between devices  50.2 us (19%)
  blocking collectives  34.3 us (13%)
  Pallas kernels  16.6 us (6%)
  local copies, waits for them, and re-layouts  15.4 us (6%)
  between operations  14.3 us (5%)
  other arithmetic  2.82 us (1%)
    all_gather x1, waiting for transfers between devices, per_device(): table = lax.all_gather(mine, 'z')  62 us
    all_to_all x1, waiting for transfers between devices, per_device(): lax.all_to_all(noise_grads, ('z', 'y'), split_axis=0, concat_axis=0, tile...  46.3 us
    all_to_all x1, waiting for transfers between devices, per_device(): lax.all_to_all(found, ('y', 'rep'), split_axis=0, concat_axis=0, tiled=True)  24.8 us
    all_to_all x1, blocking collectives, per_device(): lax.all_to_all(partial, 'rep', split_axis=0, concat_axis=0, tiled=True)  20 us
    pallas_call x7, Pallas kernels, call(): pl.pallas_call(kernel, out_shape=shapes, scratch_shapes=list(scratch), co...  16.6 us
    all_to_all x1, starting transfers between devices, per_device(): lax.all_to_all(queries, ('z', 'y'), split_axis=0, concat_axis=0, tiled=True)  16.4 us
    all_gather x1, blocking collectives, per_device(): summed = lax.all_gather(jnp.sum(shares, axis=0), 'rep')  14.3 us
    all_to_all x1, starting transfers between devices, per_device(): lax.all_to_all(noise_grads, ('z', 'y'), split_axis=0, concat_axis=0, tile...  12.2 us
  transfers between devices with their start and end apart: 5, of which 4 were waited for; matrix products, arithmetic and copies ran while one was open for 3% of the time, Pallas kernels for 5%

profile of v2, /device:TPU:1, one launch (start us, length us, event | category | flops | bytes accessed | tf_op | source)
XLA Modules:
  0.0 267.2 jit_solution(10000009440988673856)
XLA Ops:
  7.2 0.0 copy-start
  7.2 0.0 copy-start.19
  7.2 0.0 all-gather.4.cloned.1.call-start
  7.2 1.7 pad_dynamic-slice_fusion
  8.9 0.0 all-gather.4.cloned.1.call-update
  9.0 0.5 broadcast.16
  9.5 1.3 reduce.7
  10.8 0.1 reshape.83
  10.9 0.0 copy-start.20
  10.9 0.1 stack_reshape.6
  11.0 0.8 copy.46
  11.8 0.1 stack_reshape.7
  11.9 0.6 copy.51
  12.6 10.4 %all-to-all-start.1 = ((s32[32,2,128]{2,1,0:T(2,128)}), s32[32,2,128]{2,1,0:T(2,128)S(1)}, u32[]{:S(2)}, u32[]{:S(2)}) async-start(s32[32,2,128]{2,1,0:T(2,128)} %copy.51), calls=%async_computation.1 | async-start | bytes 65536 | tf_op jit(solution)/shard_map/all_to_all | solution.py:222
  22.9 0.1 reshape.81.dst_ref
  23.0 1.3 reduce.6
  24.3 0.1 reshape.82
  24.4 0.1 copy.48
  24.5 0.1 fusion
  24.6 0.1 reshape.90.live_ref
  24.7 0.0 copy-start.13
  24.7 0.8 copy.42
  25.5 0.1 reshape.77.src_ref
  25.6 0.8 copy.44
  26.4 0.1 reshape.79.rel_ref
  26.5 0.0 copy-done.19
  26.5 0.0 copy-done
  26.5 2.4 shard_map.95
  28.9 0.0 copy-done.20
  28.9 0.9 copy-done.11
  29.8 0.5 all-to-all-done.1
  30.3 16.4 %all-to-all-start = ((f32[64,8,512]{2,1,0:T(8,128)}), f32[64,8,512]{2,1,0:T(8,128)}, u32[]{:S(2)}, u32[]{:S(2)}) async-start(f32[64,8,512]{2,1,0:T(8,128)} %get-tuple-element.11), calls=%async_computation | async-start | bytes 2097152 | tf_op jit(solution)/shard_map/all_to_all | solution.py:238
  46.7 0.1 copy.52
  46.8 0.2 copy.53
  47.0 0.1 copy.54.ids_ref
  47.1 62.0 %all-gather.4.cloned.1.call-done = f32[896,512]{1,0:T(8,128)} async-done(((f32[56,512]{1,0:T(8,128)}), f32[896,512]{1,0:T(8,128)}) %all-gather.4.cloned.1.call-update) | async-done | bytes 1835024 | tf_op jit(solution)/shard_map/all_gather | solution.py:211
  109.1 1.5 copy-done.18
  110.6 6.1 %shard_map.96 = f32[32,56,256]{2,1,0:T(8,128)S(1)} custom-call(f32[16,56,512]{2,1,0:T(8,128)S(1)} %bitcast.30, s32[16,1,512]{2,1,0:T(1,128)S(1)} %copy.54.ids_ref), custom_call_target="tpu_custom_call" | custom-call | flops 209715200000 | bytes 3702784 | tf_op jit(solution)/shard_map/pallas_call | solution.py:187
  116.7 1.2 copy-done.5
  118.0 0.0 all-to-all-done.msg_ref
  118.0 11.2 %all-to-all-start.2 = ((f32[32,56,256]{2,1,0:T(8,128)}), f32[32,56,256]{2,1,0:T(8,128)S(1)}, u32[]{:S(2)}, u32[]{:S(2)}) async-start(f32[32,56,256]{2,1,0:T(8,128)} %copy-done.5), calls=%async_computation.2 | async-start | bytes 3670016 | tf_op jit(solution)/shard_map/all_to_all | solution.py:248
  129.2 0.1 reshape.87.ids_ref
  129.2 24.8 %all-to-all-done.2.got_ref = f32[32,56,256]{2,1,0:T(8,128)S(1)} async-done(((f32[32,56,256]{2,1,0:T(8,128)}), f32[32,56,256]{2,1,0:T(8,128)S(1)}, u32[]{:S(2)}, u32[]{:S(2)}) %all-to-all-start.2) | async-done | bytes 1835040 | tf_op jit(solution)/shard_map/all_to_all | solution.py:248
  154.1 2.1 shard_map.97
  156.1 0.0 copy-start.6
  156.1 1.0 copy-done.6
  157.2 1.0 copy-done.7
  158.2 12.2 %all-to-all-start.3 = ((f32[64,8,512]{2,1,0:T(8,128)}), f32[64,8,512]{2,1,0:T(8,128)S(1)}, u32[]{:S(2)}, u32[]{:S(2)}) async-start(f32[64,8,512]{2,1,0:T(8,128)} %copy-done.6), calls=%async_computation.3 | async-start | bytes 2097152 | tf_op jit(solution)/shard_map/all_to_all | solution.py:255
  170.4 0.0 copy-start.1
  170.4 1.1 copy-done.1
  171.6 2.9 %shard_map.98.owned_ref = f32[400,512]{1,0:T(8,128)S(1)} custom-call(f32[64,8,512]{2,1,0:T(8,128)} %all-to-all-done.msg_ref, f32[400,512]{1,0:T(8,128)S(1)} %bitcast.27), custom_call_target="tpu_custom_call" | custom-call | flops 1048576000 | bytes 2686976 | tf_op jit(solution)/shard_map/pallas_call | solution.py:187
  174.5 1.3 shard_map.99.early_ref
  175.8 0.0 copy-start.3
  175.8 0.9 copy-done.3
  176.7 46.3 %all-to-all-done.3.msg_ref = f32[64,8,512]{2,1,0:T(8,128)S(1)} async-done(((f32[64,8,512]{2,1,0:T(8,128)}), f32[64,8,512]{2,1,0:T(8,128)S(1)}, u32[]{:S(2)}, u32[]{:S(2)}) %all-to-all-start.3) | async-done | bytes 1048608 | tf_op jit(solution)/shard_map/all_to_all | solution.py:255
  223.0 1.1 copy-done.4
  224.1 0.7 shard_map.100
  224.8 0.0 copy-start.2
  224.9 0.0 copy-start.17
  224.9 20.0 %all_to_all.25 = f32[8,56,512]{2,1,0:T(8,128)S(1)} all-to-all(f32[8,56,512]{2,1,0:T(8,128)S(1)} %shard_map.100), channel_id=1, replica_groups=mesh['z'=16,'y'=4,'rep'=8] {'rep'}, dimensions={0} | all-to-all | bytes 1835008 | tf_op jit(solution)/shard_map/all_to_all | solution.py:263
  244.8 0.1 reduce_sum.9
  244.9 14.3 %all-gather.1 = f32[448,512]{1,0:T(8,128)S(1)} all-gather(f32[56,512]{1,0:T(8,128)S(1)} %reduce_sum.9), channel_id=3, replica_groups=mesh['z'=16,'y'=4,'rep'=8] {'rep'}, dimensions={0}, use_global_device_ids=true | all-gather | bytes 1032192 | tf_op jit(solution)/shard_map/all_gather | solution.py:264
  259.2 0.0 copy-done.2
  259.2 1.1 shard_map.101
  (30 shorter events, 0.1 us)
Async XLA Ops:
  7.2 19.3 %copy-start = (f32[512,400]{0,1:T(8,128)S(1)}, f32[512,400]{0,1:T(8,128)}, u32[]{:S(2)}) copy-start(f32[512,400]{0,1:T(8,128)} %param.8) | copy-start | bytes 2457604
  7.2 19.3 %copy-start.19 = (f32[237,400]{0,1:T(8,128)S(1)}, f32[237,400]{0,1:T(8,128)}, u32[]{:S(2)}) copy-start(f32[237,400]{0,1:T(8,128)} %param.10) | copy-start | bytes 1137604
  7.2 101.9 %all-gather.4.cloned.1.call-start = ((), (), s32[]{:S(2)}) async-start(), calls=%async_computation.5 | async-start | bytes 1949696 | tf_op jit(solution)/shard_map/all_gather | solution.py:211
  10.9 18.0 %copy-start.20 = (s32[4,16,8]{2,1,0:T(8,128)}, s32[4,16,8]{2,1,0:T(8,128)S(1)}, u32[]{:S(2)}) copy-start(s32[4,16,8]{2,1,0:T(8,128)S(1)} %copy.49) | copy-start | bytes 6148
  12.6 17.7 %all-to-all-start.1 = ((s32[32,2,128]{2,1,0:T(2,128)}), s32[32,2,128]{2,1,0:T(2,128)S(1)}, u32[]{:S(2)}, u32[]{:S(2)}) async-start(s32[32,2,128]{2,1,0:T(2,128)} %copy.51), calls=%async_computation.1 | async-start | bytes 65536 | tf_op jit(solution)/shard_map/all_to_all | solution.py:222
  24.7 4.2 %copy-start.13 = (f32[1,512]{1,0:T(1,128)}, f32[1,512]{1,0:T(1,128)S(1)}, u32[]{:S(2)}) copy-start(f32[1,512]{1,0:T(1,128)S(1)} %reshape.90.live_ref) | copy-start | bytes 6148
  25.6 3.3 %copy-start.15 = (s32[1,512]{1,0:T(1,128)}, s32[1,512]{1,0:T(1,128)S(1)}, u32[]{:S(2)}) copy-start(s32[1,512]{1,0:T(1,128)S(1)} %reshape.77.src_ref) | copy-start | bytes 6148
  28.9 0.9 copy-start.11
  29.8 124.3 %copy-start.9 = (f32[400,512]{1,0:T(8,128)}, f32[400,512]{1,0:T(8,128)S(1)}, u32[]{:S(2)}) copy-start(f32[400,512]{1,0:T(8,128)S(1)} %get-tuple-element.13.qt_ref) | copy-start | bytes 2457604
  30.3 87.7 %all-to-all-start = ((f32[64,8,512]{2,1,0:T(8,128)}), f32[64,8,512]{2,1,0:T(8,128)}, u32[]{:S(2)}, u32[]{:S(2)}) async-start(f32[64,8,512]{2,1,0:T(8,128)} %get-tuple-element.11), calls=%async_computation | async-start | bytes 2097152 | tf_op jit(solution)/shard_map/all_to_all | solution.py:238
  109.1 1.5 copy-start.18
  116.7 1.3 copy-start.5
  117.9 11.2 %copy-start.21 = (s32[4,16,8]{2,1,0:T(8,128)S(1)}, s32[4,16,8]{2,1,0:T(8,128)}, u32[]{:S(2)}) copy-start(s32[4,16,8]{2,1,0:T(8,128)} %copy-done.20) | copy-start | bytes 6148
  117.9 36.1 %copy-start.14 = (f32[1,512]{1,0:T(1,128)S(1)}, f32[1,512]{1,0:T(1,128)}, u32[]{:S(2)}) copy-start(f32[1,512]{1,0:T(1,128)} %copy-done.13) | copy-start | bytes 6148
  118.0 36.1 %all-to-all-start.2 = ((f32[32,56,256]{2,1,0:T(8,128)}), f32[32,56,256]{2,1,0:T(8,128)S(1)}, u32[]{:S(2)}, u32[]{:S(2)}) async-start(f32[32,56,256]{2,1,0:T(8,128)} %copy-done.5), calls=%async_computation.2 | async-start | bytes 3670016 | tf_op jit(solution)/shard_map/all_to_all | solution.py:248
  156.1 1.0 copy-start.6
  157.2 1.0 copy-start.7
  158.2 64.8 %all-to-all-start.3 = ((f32[64,8,512]{2,1,0:T(8,128)}), f32[64,8,512]{2,1,0:T(8,128)S(1)}, u32[]{:S(2)}, u32[]{:S(2)}) async-start(f32[64,8,512]{2,1,0:T(8,128)} %copy-done.6), calls=%async_computation.3 | async-start | bytes 2097152 | tf_op jit(solution)/shard_map/all_to_all | solution.py:255
  170.4 1.1 copy-start.1
  171.5 2.9 %copy-start.8 = (f32[512,512]{1,0:T(8,128)S(1)}, f32[512,512]{1,0:T(8,128)}, u32[]{:S(2)}) copy-start(f32[512,512]{1,0:T(8,128)} %copy-done.7) | copy-start | bytes 3145732
  171.5 2.9 %copy-start.10 = (f32[400,512]{1,0:T(8,128)S(1)}, f32[400,512]{1,0:T(8,128)}, u32[]{:S(2)}) copy-start(f32[400,512]{1,0:T(8,128)} %copy-done.9) | copy-start | bytes 2457604
  171.5 2.9 %copy-start.12 = (f32[400,512]{1,0:T(8,128)S(1)}, f32[400,512]{1,0:T(8,128)}, u32[]{:S(2)}) copy-start(f32[400,512]{1,0:T(8,128)} %copy-done.11) | copy-start | bytes 2457604
  171.5 3.0 %copy-start.16 = (s32[1,512]{1,0:T(1,128)S(1)}, s32[1,512]{1,0:T(1,128)}, u32[]{:S(2)}) copy-start(s32[1,512]{1,0:T(1,128)} %copy-done.15) | copy-start | bytes 6148
  175.8 0.9 copy-start.3
  223.0 1.1 copy-start.4
  224.8 34.4 %copy-start.2 = (f32[512,400]{0,1:T(8,128)S(1)}, f32[512,400]{0,1:T(8,128)}, u32[]{:S(2)}) copy-start(f32[512,400]{0,1:T(8,128)} %param.8) | copy-start | bytes 2457604
  224.9 34.4 %copy-start.17 = (f32[512]{0:T(512)S(1)}, f32[512]{0:T(512)}, u32[]{:S(2)}) copy-start(f32[512]{0:T(512)} %param.9) | copy-start | bytes 6148
Sparse Core Ops, SparseCore 0:
  10.1 98.9 all-gather.3

commit v3 on v0

v3 whole, which is shorter than its diff:
```python
import functools

import jax
import jax.numpy as jnp
from jax import lax
from jax.experimental import pallas as pl
from jax.experimental.pallas import tpu as pltpu
from jax.sharding import Mesh
from jax.sharding import PartitionSpec as P

LEARN_RATE = 0.3
F32 = jnp.float32
BF16 = jnp.bfloat16
NN = (((1,), (0,)), ((), ()))
NT = (((1,), (1,)), ((), ()))


def round_up(value, unit):
    return -(-value // unit) * unit


def one_hot(row, rows):
    place = lax.broadcasted_iota(jnp.int32, (rows, row.shape[1]), 0)
    return (place == row).astype(F32).astype(BF16)


def split(x, terms):
    out = []
    for _ in range(terms):
        part = x.astype(BF16)
        out.append(part)
        x = x - part.astype(F32)
    return out


def mul(a, b, dims=NN):
    return lax.dot_general(a, b, dims, preferred_element_type=F32)


def pick(x, hot, dims=NN, terms=3):
    n = x.shape[0]
    parts = [part.astype(F32) for part in split(x, terms)]
    out = mul(jnp.concatenate(parts, axis=0).astype(BF16), hot, dims)
    return sum(out[i * n : (i + 1) * n] for i in range(terms - 1, -1, -1))


def product(a, b, dims=NN):
    a_high, a_low = split(a, 2)
    b_high, b_low = split(b, 2)
    return mul(a_low, b_high, dims) + mul(a_high, b_low, dims) + mul(a_high, b_high, dims)


def swap_blocks(v, slots, lane):
    n, span = len(v), v[0].shape[1]
    k = n // 2
    while k:
        low = (lane & k) == 0
        w = list(v)
        for i in range(n):
            if not i & k:
                a, b = v[i], v[i + k]
                w[i] = jnp.where(low, a, pltpu.roll(b, k * slots, 1))
                w[i + k] = jnp.where(low, pltpu.roll(a, span - k * slots, 1), b)
        v = w
        k //= 2
    return v


def query_kernel(et_ref, relt_ref, src_ref, rel_ref, query_ref, relation_ref):
    source = pick(et_ref[...], one_hot(src_ref[...], et_ref.shape[1]))
    relation = pick(relt_ref[...], one_hot(rel_ref[...], relt_ref.shape[1]))
    query_ref[...] = source * relation
    relation_ref[...] = relation


def table_kernel(table_ref, ids_ref, out_ref, got_ref):
    nh, fs, rows = table_ref.shape
    devices, _, span = out_ref.shape
    n = 2 * nh
    slots = span // n

    def fetch(h, carry):
        got_ref[h] = pick(table_ref[h], one_hot(ids_ref[h], rows))
        return carry

    lax.fori_loop(0, nh, fetch, 0, unroll=2)
    lane = lax.broadcasted_iota(jnp.int32, (8, span), 1) // slots

    def turn(f8, carry):
        at = pl.ds(pl.multiple_of(f8 * 8, 8), 8)
        for tile in range(devices // n):
            v = []
            for kind in range(2):
                start = (kind * devices + tile * n) * slots
                v += [got_ref[h, at, start : start + span] for h in range(nh)]
            v = swap_blocks(v, slots, lane)
            for i in range(n):
                out_ref[tile * n + i, at, :] = v[i]
        return carry

    lax.fori_loop(0, fs // 8, turn, 0)


def scatter_kernel(msg_ref, ids_ref, out_ref, got_ref):
    nh, fs, rows = out_ref.shape
    devices, _, span = msg_ref.shape
    n = 2 * nh
    slots = span // n
    lane = lax.broadcasted_iota(jnp.int32, (8, span), 1) // slots

    def turn(f8, carry):
        at = pl.ds(pl.multiple_of(f8 * 8, 8), 8)
        for tile in range(devices // n):
            v = swap_blocks([msg_ref[tile * n + i, at, :] for i in range(n)], slots, lane)
            for kind in range(2):
                start = (kind * devices + tile * n) * slots
                for h in range(nh):
                    got_ref[h, at, start : start + span] = v[kind * nh + h]
        return carry

    lax.fori_loop(0, fs // 8, turn, 0)

    def add(h, carry):
        out_ref[h] = pick(got_ref[h], one_hot(ids_ref[h], rows), NT, 2)
        return carry

    lax.fori_loop(0, nh, add, 0, unroll=2)


def received(got_ref, ny, features):
    devices, fs, span = got_ref.shape
    per = devices // (2 * ny)
    low = lax.broadcasted_iota(jnp.int32, (1, span), 1) < span // 2
    noise, target = [], []
    for y in range(ny):
        first, second = (
            got_ref[(l * ny + y) * per : (l * ny + y + 1) * per].reshape(per * fs, span)[:features] for l in range(2)
        )
        noise.append(jnp.where(low, first, pltpu.roll(second, span // 2, 1)))
        target.append(jnp.where(low, pltpu.roll(first, span // 2, 1), second))
    return jnp.concatenate(noise, axis=1), jnp.concatenate(target, axis=1)


def send(msg_ref, ny, noise, target):
    devices, fs, span = msg_ref.shape
    per = devices // (2 * ny)
    low = lax.broadcasted_iota(jnp.int32, (1, span), 1) < span // 2
    rest = jnp.zeros((per * fs - noise.shape[0], span), F32)
    for y in range(ny):
        a, b = noise[:, y * span : (y + 1) * span], target[:, y * span : (y + 1) * span]
        first = jnp.where(low, a, pltpu.roll(b, span // 2, 1))
        second = jnp.where(low, pltpu.roll(a, span // 2, 1), b)
        for l, block in enumerate((first, second)):
            full = jnp.concatenate([block, rest], axis=0) if rest.shape[0] else block
            msg_ref[(l * ny + y) * per : (l * ny + y + 1) * per] = full.reshape(per, fs, span)


def coefficients(query, noise, target, live):
    coef = jax.nn.sigmoid(product(noise.T, query)) * live
    positive = jnp.sum(query * target, axis=0, keepdims=True)
    return coef, -jax.nn.sigmoid(-positive) * live


def terms_kernel(ny, got_ref, query_ref, live_ref, msg_ref):
    query = query_ref[...]
    noise, target = received(got_ref, ny, query.shape[0])
    coef, pos_coef = coefficients(query, noise, target, live_ref[...])
    send(msg_ref, ny, product(query, coef, NT), pos_coef * query)


def source_kernel(ny, got_ref, query_ref, relation_ref, live_ref, src_ref, out_ref):
    reps, fs, rows = out_ref.shape
    query = query_ref[...]
    features = query.shape[0]
    noise, target = received(got_ref, ny, features)
    coef, pos_coef = coefficients(query, noise, target, live_ref[...])
    grad = relation_ref[...] * (pos_coef * target + product(noise, coef))
    grad = pick(grad, one_hot(src_ref[...], rows), NT, 2)
    rest = reps * fs - features
    if rest:
        grad = jnp.concatenate([grad, jnp.zeros((rest, rows), F32)], axis=0)
    out_ref[...] = grad.reshape(reps, fs, rows)


def update_kernel(grad_ref, et_ref, state_ref, entity_ref, new_state_ref):
    features, rows = et_ref.shape
    grad = grad_ref[...].reshape(-1, rows)[:features]
    state = state_ref[...] + jnp.sum(grad * grad, axis=0, keepdims=True) * (1.0 / features)
    new_state_ref[...] = state
    entity_ref[...] = et_ref[...] - LEARN_RATE * grad / jnp.sqrt(state)


def call(kernel, outs, *args, scratch=(), flops=0):
    shapes = [jax.ShapeDtypeStruct(shape, F32) for shape in outs]
    moved = sum(4 * a.size for a in args) + sum(4 * s.size for s in shapes)
    return pl.pallas_call(
        kernel,
        out_shape=shapes,
        scratch_shapes=list(scratch),
        cost_estimate=pl.CostEstimate(flops=flops, bytes_accessed=moved, transcendentals=0),
        compiler_params=pltpu.CompilerParams(vmem_limit_bytes=48 << 20),
    )(*args)


def per_device(entity, adagrad_state, relation, src_rows, dst_rows, rel_ids, bucket_counts, noise_rows):
    nh, nl, ny, reps = (lax.axis_size(name) for name in ("h", "l", "y", "rep"))
    near = ("l", "y", "rep")
    devices = nl * ny * reps
    rows, features = entity.shape
    slots = src_rows.shape[3]
    edges = nh * nl * ny * slots
    fs = round_up(features, reps * 8) // reps

    def ordered(ids):
        return ids.reshape(nh, nl, ny, slots).transpose(2, 1, 0, 3).reshape(1, edges)

    et = entity.T
    padded = jnp.pad(et, ((0, reps * fs - features), (0, 0)))
    mine = lax.dynamic_slice_in_dim(padded, lax.axis_index("rep") * fs, fs, 0)
    table = lax.all_gather(mine, "h")

    wanted = jnp.stack([noise_rows.reshape(nh, nl, ny, slots), dst_rows.reshape(nh, nl, ny, slots)])
    wanted = wanted.transpose(2, 3, 0, 1, 4).reshape(nl, ny, 1, 2 * nh * slots)
    wanted = jnp.broadcast_to(wanted, (nl, ny, reps, 2 * nh * slots)).reshape(devices, -1)
    asked = lax.all_to_all(wanted, near, split_axis=0, concat_axis=0, tiled=True)
    asked = asked.reshape(devices, 2, nh, slots).transpose(2, 1, 0, 3).reshape(nh, 1, -1)

    src = ordered(src_rows)
    rel = ordered(rel_ids)
    live = jnp.arange(slots, dtype=jnp.int32) < bucket_counts.reshape(nh, nl, ny).transpose(2, 1, 0)[..., None]
    live = live.astype(F32).reshape(1, edges)
    relt = jnp.pad(relation.T, ((0, 0), (0, round_up(relation.shape[0], 128) - relation.shape[0])))

    unit = 2 * edges * features * rows
    message = (devices, fs, 2 * nh * slots)
    got_shape = pltpu.VMEM((nh, fs, 2 * devices * slots), F32)
    query, relation_rows = call(query_kernel, [(features, edges)] * 2, et, relt, src, rel, flops=5 * unit)
    (found,) = call(table_kernel, [message], table, asked, scratch=[got_shape], flops=8 * unit)
    got = lax.all_to_all(found, near, split_axis=0, concat_axis=0, tiled=True)
    (terms,) = call(functools.partial(terms_kernel, ny), [message], got, query, live, flops=6 * unit)
    terms = lax.all_to_all(terms, near, split_axis=0, concat_axis=0, tiled=True)
    (source,) = call(
        functools.partial(source_kernel, ny), [(reps, fs, rows)], got, query, relation_rows, live, src, flops=8 * unit
    )
    (partial,) = call(scatter_kernel, [(nh, fs, rows)], terms, asked, scratch=[got_shape], flops=8 * unit)
    grad = lax.psum_scatter(partial, "h", scatter_dimension=0)
    shares = lax.all_to_all(source, "rep", split_axis=0, concat_axis=0, tiled=True)
    summed = lax.all_gather(grad + jnp.sum(shares, axis=0), "rep")
    new_entity, new_state = call(
        update_kernel, [(features, rows), (1, rows)], summed, et, adagrad_state.reshape(1, rows)
    )
    return new_entity.T, new_state.reshape(rows)


def solution(mesh):
    dom, reps = mesh.devices.shape
    ny = 4 if dom >= 16 else 2
    axes = ("h", "l", "y", "rep")
    cut = Mesh(mesh.devices.reshape(dom // (2 * ny), 2, ny, reps), axes)
    part = axes[:3]
    return jax.shard_map(
        per_device,
        mesh=cut,
        in_specs=(
            P(part, None),
            P(part),
            P(),
            P(part, "rep", None, None),
            P(part, "rep", None, None),
            P(part, "rep", None, None),
            P(part, "rep", None),
            P(part, "rep", None),
        ),
        out_specs=(P(part, None), P(part)),
        check_vma=False,
    )
```

time: 384 us -> 214 us (0.56)
  waiting for transfers between devices: 253 us -> 41.3 us
  blocking collectives: 0 us -> 102 us
  starting transfers between devices: 59.4 us -> 24.8 us
  Pallas kernels: 0 us -> 19.7 us
  other arithmetic: 21.7 us -> 3.09 us
  matrix products: 12.7 us -> 0 us
  local copies, waits for them, and re-layouts: 20.9 us -> 8.54 us
    all_to_all x6 -> x2, waiting for transfers between devices: 179 us -> 21.2 us  [the longest x1 21.2 us: per_device(): got = lax.all_to_all(found, near, split_axis=0, concat_axis=0, tiled=True)]
    psum x1 -> x0, waiting for transfers between devices: 74.5 us -> none  [per_device(): summed = lax.psum(grad, 'rep')]
    all_gather x0 -> x2, blocking collectives: none -> 52.4 us  [the longest x1 33.5 us: per_device(): table = lax.all_gather(mine, 'h')]
    all_to_all x0 -> x2, blocking collectives: none -> 49.5 us  [the longest x1 31.1 us: per_device(): terms = lax.all_to_all(terms, near, split_axis=0, concat_axis=0, tiled=True)]
    all_to_all x6 -> x2, starting transfers between devices: 59.4 us -> 24.8 us  [the longest x1 13.8 us: per_device(): got = lax.all_to_all(found, near, split_axis=0, concat_axis=0, tiled=True)]
    reduce_scatter x0 -> x1, waiting for transfers between devices: none -> 20 us  [per_device(): grad = lax.psum_scatter(partial, 'h', scatter_dimension=0)]
    pallas_call x0 -> x6, Pallas kernels: none -> 19.7 us  [call(): pl.pallas_call(kernel, out_shape=shapes, scratch_shapes=list(scratch), co...]
    scatter-add x3 -> x0, other arithmetic: 14.2 us -> none  [the longest x1 4.95 us: per_device(): grad = grad.at[slot_ids.reshape(-1)].add(owner_grads.reshape(-1, features))]
  transfers between devices with their start and end apart: 7 -> 3, of which waited for: 7 -> 2; matrix products, arithmetic and copies ran while one was open for 11% -> 1% of each run, Pallas kernels for 0% -> 2%
where the time goes in v3:
time: 214 us
  blocking collectives  102 us (48%)
  waiting for transfers between devices  41.3 us (19%)
  starting transfers between devices  24.8 us (12%)
  Pallas kernels  19.7 us (9%)
  between operations  14.2 us (7%)
  local copies, waits for them, and re-layouts  8.54 us (4%)
  other arithmetic  3.09 us (1%)
    all_gather x1, blocking collectives, per_device(): table = lax.all_gather(mine, 'h')  33.5 us
    all_to_all x1, blocking collectives, per_device(): terms = lax.all_to_all(terms, near, split_axis=0, concat_axis=0, tiled=True)  31.1 us
    all_to_all x1, waiting for transfers between devices, per_device(): got = lax.all_to_all(found, near, split_axis=0, concat_axis=0, tiled=True)  21.2 us
    reduce_scatter x1, waiting for transfers between devices, per_device(): grad = lax.psum_scatter(partial, 'h', scatter_dimension=0)  20 us
    pallas_call x6, Pallas kernels, call(): pl.pallas_call(kernel, out_shape=shapes, scratch_shapes=list(scratch), co...  19.7 us
    all_gather x1, blocking collectives, per_device(): summed = lax.all_gather(grad + jnp.sum(shares, axis=0), 'rep')  18.9 us
    all_to_all x1, blocking collectives, per_device(): lax.all_to_all(source, 'rep', split_axis=0, concat_axis=0, tiled=True)  18.4 us
    all_to_all x1, starting transfers between devices, per_device(): got = lax.all_to_all(found, near, split_axis=0, concat_axis=0, tiled=True)  13.8 us
  transfers between devices with their start and end apart: 3, of which 2 were waited for; matrix products, arithmetic and copies ran while one was open for 1% of the time, Pallas kernels for 2%

profile of v3, /device:TPU:1, one launch (start us, length us, event | category | flops | bytes accessed | tf_op | source)
XLA Modules:
  0.0 213.5 jit_solution(3478719339013954246)
XLA Ops:
  7.2 0.5 broadcast.15
  7.7 1.3 reduce.6
  9.0 0.1 stack_reshape.6
  9.1 0.8 copy.36
  9.9 0.1 broadcast_in_dim.4
  10.0 0.6 broadcast_in_dim.10
  10.7 10.9 %all-to-all-start = ((s32[64,1,128]{2,1,0:T(1,128)}), s32[64,1,128]{2,1,0:T(1,128)S(1)}, u32[]{:S(2)}, u32[]{:S(2)}) async-start(s32[64,1,128]{2,1,0:T(1,128)} %bitcast.5), calls=%async_computation | async-start | bytes 65536 | tf_op jit(solution)/shard_map/all_to_all | solution.py:225
  21.6 0.9 pad_dynamic-slice_fusion
  22.5 33.5 %all-gather = f32[448,512]{1,0:T(8,128)S(1)} all-gather(f32[56,512]{1,0:T(8,128)S(1)} %pad_dynamic-slice_fusion), channel_id=2, replica_groups=mesh['h'=8,'l'=2,'y'=4,'rep'=8] {'h'}, dimensions={0}, use_global_device_ids=true | all-gather | bytes 1032192 | tf_op jit(solution)/shard_map/all_gather | solution.py:220
  55.9 0.0 all-to-all-done
  56.0 0.1 copy.39
  56.0 0.2 copy.40
  56.3 0.3 reshape.79.ids_ref
  56.6 6.0 %shard_map.95 = f32[64,56,128]{2,1,0:T(8,128)S(1)} custom-call(f32[8,56,512]{2,1,0:T(8,128)S(1)} %bitcast.37, s32[8,1,1024]{2,1,0:T(1,128)S(1)} %reshape.79.ids_ref), custom_call_target="tpu_custom_call" | custom-call | flops 1677721600 | bytes 2785280 | tf_op jit(solution)/shard_map/pallas_call | solution.py:196
  62.6 0.0 copy-start.1
  62.6 1.2 copy-done.1
  63.9 0.0 copy-start.7
  63.9 0.0 copy-start.8
  63.9 0.0 copy-start.9
  63.9 0.0 copy-start.6
  63.9 0.0 copy-start
  63.9 13.8 %all-to-all-start.1 = ((f32[64,56,128]{2,1,0:T(8,128)}), f32[64,56,128]{2,1,0:T(8,128)S(1)}, u32[]{:S(2)}, u32[]{:S(2)}) async-start(f32[64,56,128]{2,1,0:T(8,128)} %copy-done.1), calls=%async_computation.1 | async-start | bytes 3670016 | tf_op jit(solution)/shard_map/all_to_all | solution.py:239
  77.7 0.0 reduce-scatter.2.cloned.1.call-start
  77.8 0.0 copy-done.7
  77.8 0.1 copy.42
  77.9 0.1 reshape.71.src_ref
  78.0 0.0 copy-done.8
  78.0 0.1 copy.44
  78.1 0.1 reshape.73.rel_ref
  78.2 0.0 copy-done.9
  78.2 0.7 reduce.7
  78.9 0.1 reshape.74
  79.0 0.1 copy.46
  79.1 0.1 fusion
  79.1 0.1 reshape.77.live_ref
  79.2 0.0 copy-done.6
  79.3 0.0 copy-done
  79.3 1.1 shard_map.96
  80.4 0.0 copy-start.4
  80.4 0.9 copy-done.4
  81.3 21.2 %all-to-all-done.1.got_ref = f32[64,56,128]{2,1,0:T(8,128)S(1)} async-done(((f32[64,56,128]{2,1,0:T(8,128)}), f32[64,56,128]{2,1,0:T(8,128)S(1)}, u32[]{:S(2)}, u32[]{:S(2)}) %all-to-all-start.1) | async-done | bytes 1835040 | tf_op jit(solution)/shard_map/all_to_all | solution.py:239
  102.5 2.3 %shard_map.97 = f32[64,56,128]{2,1,0:T(8,128)S(1)} custom-call(f32[64,56,128]{2,1,0:T(8,128)S(1)} %all-to-all-done.1.got_ref, f32[400,512]{1,0:T(8,128)S(1)} %get-tuple-element.6.query_ref, f32[1,512]{1,0:T(1,128)S(1)} %reshape.77.live_ref), custom_call_target="tpu_custom_call" | custom-call | flops 1258291200 | bytes 4491264 | tf_op jit(solution)/shard_map/pallas_call | solution.py:196
  104.8 31.1 %all_to_all.24.msg_ref = f32[64,56,128]{2,1,0:T(8,128)S(1)} all-to-all(f32[64,56,128]{2,1,0:T(8,128)S(1)} %shard_map.97), channel_id=1, replica_groups=mesh['h'=8,'l'=2,'y'=4,'rep'=8] {'l','y','rep'}, dimensions={0} | all-to-all | bytes 3670016 | tf_op jit(solution)/shard_map/all_to_all | solution.py:241
  136.0 6.6 %shard_map.98 = f32[8,56,512]{2,1,0:T(8,128)S(1)} custom-call(f32[64,56,128]{2,1,0:T(8,128)S(1)} %all_to_all.24.msg_ref, s32[8,1,1024]{2,1,0:T(1,128)S(1)} %reshape.79.ids_ref), custom_call_target="tpu_custom_call" | custom-call | flops 1677721600 | bytes 2785280 | tf_op jit(solution)/shard_map/pallas_call | solution.py:196
  142.6 0.0 copy-start.2
  142.6 0.9 copy-done.2
  143.6 0.0 reduce-scatter.2.cloned.1.call-update
  143.6 0.0 copy-start.5
  143.6 1.1 copy-done.5
  144.7 2.5 %shard_map.99 = f32[8,56,512]{2,1,0:T(8,128)S(1)} custom-call(f32[64,56,128]{2,1,0:T(8,128)S(1)} %all-to-all-done.1.got_ref, f32[400,512]{1,0:T(8,128)S(1)} %get-tuple-element.6.query_ref, f32[400,512]{1,0:T(8,128)S(1)} %copy-done.5, f32[1,512]{1,0:T(1,128)S(1)} %reshape.77.live_ref, s32[1,512]{1,0:T(1,128)S(1)} %reshape.71.src_ref), custom_call_target="tpu_custom_call" | custom-call | flops 1677721600 | bytes 4395008 | tf_op jit(solution)/shard_map/pallas_call | solution.py:196
  147.3 0.0 copy-start.3
  147.3 18.4 %all_to_all.25 = f32[8,56,512]{2,1,0:T(8,128)S(1)} all-to-all(f32[8,56,512]{2,1,0:T(8,128)S(1)} %shard_map.99), channel_id=1, replica_groups=mesh['h'=8,'l'=2,'y'=4,'rep'=8] {'rep'}, dimensions={0} | all-to-all | bytes 1835008 | tf_op jit(solution)/shard_map/all_to_all | solution.py:247
  165.6 0.1 reduce_sum.11
  165.7 20.0 %reduce-scatter.2.cloned.1.call-done = f32[1,56,512]{2,1,0:T(8,128)} async-done(((f32[8,56,512]{2,1,0:T(8,128)}), f32[1,56,512]{2,1,0:T(8,128)}) %reduce-scatter.2.cloned.1.call-update) | async-done | bytes 114704 | tf_op jit(solution)/shard_map/reduce_scatter | solution.py:246
  185.7 0.9 bitcast_add_fusion
  186.7 18.9 %all_gather.12.grad_ref = f32[8,56,512]{2,1,0:T(8,128)S(1)} all-gather(f32[1,56,512]{2,1,0:T(8,128)S(1)} %bitcast_add_fusion), channel_id=1, replica_groups=mesh['h'=8,'l'=2,'y'=4,'rep'=8] {'rep'}, dimensions={0}, use_global_device_ids=true | all-gather | bytes 1032192 | tf_op jit(solution)/shard_map/all_gather | solution.py:248
  205.6 0.0 copy-done.3
  205.6 1.1 shard_map.100
  (5 shorter events, 0.1 us)
Async XLA Ops:
  10.7 45.3 %all-to-all-start = ((s32[64,1,128]{2,1,0:T(1,128)}), s32[64,1,128]{2,1,0:T(1,128)S(1)}, u32[]{:S(2)}, u32[]{:S(2)}) async-start(s32[64,1,128]{2,1,0:T(1,128)} %bitcast.5), calls=%async_computation | async-start | bytes 65536 | tf_op jit(solution)/shard_map/all_to_all | solution.py:225
  62.6 1.2 copy-start.1
  63.9 13.9 %copy-start.7 = (s32[1,1,64,8]{2,3,1,0:T(8,128)S(1)}, s32[1,1,64,8]{2,3,1,0:T(8,128)}, u32[]{:S(2)}) copy-start(s32[1,1,64,8]{2,3,1,0:T(8,128)} %param.11) | copy-start | bytes 6148
  63.9 14.1 %copy-start.8 = (s32[1,1,64,8]{2,3,1,0:T(8,128)S(1)}, s32[1,1,64,8]{2,3,1,0:T(8,128)}, u32[]{:S(2)}) copy-start(s32[1,1,64,8]{2,3,1,0:T(8,128)} %param.13) | copy-start | bytes 6148
  63.9 14.3 %copy-start.9 = (s32[1,1,64]{2,1,0:T(1,128)S(1)}, s32[1,1,64]{2,1,0:T(1,128)}, u32[]{:S(2)}) copy-start(s32[1,1,64]{2,1,0:T(1,128)} %param.14) | copy-start | bytes 772
  63.9 15.4 %copy-start.6 = (f32[237,400]{0,1:T(8,128)S(1)}, f32[237,400]{0,1:T(8,128)}, u32[]{:S(2)}) copy-start(f32[237,400]{0,1:T(8,128)} %param.10) | copy-start | bytes 1137604
  63.9 15.4 %copy-start = (f32[512,400]{0,1:T(8,128)S(1)}, f32[512,400]{0,1:T(8,128)}, u32[]{:S(2)}) copy-start(f32[512,400]{0,1:T(8,128)} %param.8) | copy-start | bytes 2457604
  63.9 38.7 %all-to-all-start.1 = ((f32[64,56,128]{2,1,0:T(8,128)}), f32[64,56,128]{2,1,0:T(8,128)S(1)}, u32[]{:S(2)}, u32[]{:S(2)}) async-start(f32[64,56,128]{2,1,0:T(8,128)} %copy-done.1), calls=%async_computation.1 | async-start | bytes 3670016 | tf_op jit(solution)/shard_map/all_to_all | solution.py:239
  77.7 108.0 %reduce-scatter.2.cloned.1.call-start = ((), (), s32[]{:S(2)}) async-start(), calls=%async_computation.5 | async-start | bytes 1032192 | tf_op jit(solution)/shard_map/reduce_scatter | solution.py:246
  80.4 0.9 copy-start.4
  142.6 0.9 copy-start.2
  143.6 1.1 copy-start.5
  147.3 58.3 %copy-start.3 = (f32[512]{0:T(512)S(1)}, f32[512]{0:T(512)}, u32[]{:S(2)}) copy-start(f32[512]{0:T(512)} %param.9) | copy-start | bytes 6148
Sparse Core Ops, SparseCore 0:
  143.7 41.9 reduce-scatter.1

commit v4 on v3

--- a/solution.py
+++ b/solution.py
@@ -101,9 +101,9 @@
     lax.fori_loop(0, fs // 8, turn, 0)
 
 
-def scatter_kernel(msg_ref, ids_ref, out_ref, got_ref):
-    nh, fs, rows = out_ref.shape
-    devices, _, span = msg_ref.shape
+def scatter_kernel(msg_ref, ids_ref, first_ref, second_ref, got_ref):
+    nh, cut, rows = first_ref.shape
+    devices, fs, span = msg_ref.shape
     n = 2 * nh
     slots = span // n
     lane = lax.broadcasted_iota(jnp.int32, (8, span), 1) // slots
@@ -121,7 +121,9 @@
     lax.fori_loop(0, fs // 8, turn, 0)
 
     def add(h, carry):
-        out_ref[h] = pick(got_ref[h], one_hot(ids_ref[h], rows), NT, 2)
+        grad = pick(got_ref[h], one_hot(ids_ref[h], rows), NT, 2)
+        first_ref[h] = grad[:cut]
+        second_ref[h] = grad[cut:]
         return carry
 
     lax.fori_loop(0, nh, add, 0, unroll=2)
@@ -242,10 +244,14 @@
     (source,) = call(
         functools.partial(source_kernel, ny), [(reps, fs, rows)], got, query, relation_rows, live, src, flops=8 * unit
     )
-    (partial,) = call(scatter_kernel, [(nh, fs, rows)], terms, asked, scratch=[got_shape], flops=8 * unit)
-    grad = lax.psum_scatter(partial, "h", scatter_dimension=0)
-    shares = lax.all_to_all(source, "rep", split_axis=0, concat_axis=0, tiled=True)
-    summed = lax.all_gather(grad + jnp.sum(shares, axis=0), "rep")
+    source = lax.psum_scatter(source, "rep", scatter_dimension=0)
+    cut = round_up(3 * fs // 8, 8)
+    first, second = call(
+        scatter_kernel, [(nh, cut, rows), (nh, fs - cut, rows)], terms, asked, scratch=[got_shape], flops=8 * unit
+    )
+    second = lax.psum_scatter(second, "h", scatter_dimension=0)
+    first = jnp.sum(lax.all_to_all(first, "h", split_axis=0, concat_axis=0, tiled=True), axis=0)
+    summed = lax.all_gather(source + jnp.concatenate([first, second], axis=0), "rep")
     new_entity, new_state = call(
         update_kernel, [(features, rows), (1, rows)], summed, et, adagrad_state.reshape(1, rows)
     )

time: 214 us -> 231 us (1.079)
  blocking collectives: 102 us -> 52.5 us
  waiting for transfers between devices: 41.3 us -> 89 us
  starting transfers between devices: 24.8 us -> 39.5 us
  Pallas kernels: 19.7 us -> 22.2 us
    all_to_all x2 -> x0, blocking collectives: 49.5 us -> none  [the longest x1 31.1 us: per_device(): terms = lax.all_to_all(terms, near, split_axis=0, concat_axis=0, tiled=True)]
    all_to_all x0 -> x2, waiting for transfers between devices: none -> 40 us  [the longest x1 20 us: per_device(): terms = lax.all_to_all(terms, near, split_axis=0, concat_axis=0, tiled=True)]
    all_to_all x0 -> x2, starting transfers between devices: none -> 14.6 us  [the longest x1 7.93 us: per_device(): lax.all_to_all(first, 'h', split_axis=0, concat_axis=0, tiled=True)]
    reduce_scatter x1 -> x2, waiting for transfers between devices: 20 us -> 27 us  [the longest x1 26.9 us: per_device(): second = lax.psum_scatter(second, 'h', scatter_dimension=0)]
    pallas_call x6, Pallas kernels: 19.7 us -> 22.2 us  [call(): pl.pallas_call(kernel, out_shape=shapes, scratch_shapes=list(scratch), co...]
    unnamed x24 -> x26, local copies, waits for them, and re-layouts: 5.68 us -> 6.94 us
  transfers between devices with their start and end apart: 3 -> 6, of which waited for: 2 -> 4; matrix products, arithmetic and copies ran while one was open for 1% -> 1% of each run, Pallas kernels for 2% -> 6%
where the time goes in v4:
time: 231 us; the launch traced here: 230 us
  waiting for transfers between devices  89 us (39%)
  blocking collectives  52.5 us (23%)
  starting transfers between devices  39.5 us (17%)
  Pallas kernels  22.2 us (10%)
  between operations  14.3 us (6%)
  local copies, waits for them, and re-layouts  9.8 us (4%)
  other arithmetic  3.05 us (1%)
    all_gather x1, blocking collectives, per_device(): table = lax.all_gather(mine, 'h')  33.5 us
    reduce_scatter x1, waiting for transfers between devices, per_device(): second = lax.psum_scatter(second, 'h', scatter_dimension=0)  26.9 us
    pallas_call x6, Pallas kernels, call(): pl.pallas_call(kernel, out_shape=shapes, scratch_shapes=list(scratch), co...  22.2 us
    all_to_all x1, waiting for transfers between devices, per_device(): got = lax.all_to_all(found, near, split_axis=0, concat_axis=0, tiled=True)  21.3 us
    all_to_all x1, waiting for transfers between devices, per_device(): terms = lax.all_to_all(terms, near, split_axis=0, concat_axis=0, tiled=True)  20 us
    all_to_all x1, waiting for transfers between devices, per_device(): lax.all_to_all(first, 'h', split_axis=0, concat_axis=0, tiled=True)  20 us
    all_gather x1, blocking collectives, per_device(): lax.all_gather(source + jnp.concatenate([first, second], axis=0), 'rep')  19 us
    all_to_all x1, starting transfers between devices, per_device(): got = lax.all_to_all(found, near, split_axis=0, concat_axis=0, tiled=True)  13.8 us
  transfers between devices with their start and end apart: 6, of which 4 were waited for; matrix products, arithmetic and copies ran while one was open for 1% of the time, Pallas kernels for 6%

profile of v4, /device:TPU:1, one launch (start us, length us, event | category | flops | bytes accessed | tf_op | source)
XLA Modules:
  0.0 230.2 jit_solution(1746026087802500864)
XLA Ops:
  7.2 0.5 broadcast.15
  7.7 1.3 reduce.6
  9.0 0.1 stack_reshape.6
  9.1 0.8 copy.36
  9.9 0.1 broadcast_in_dim.4
  10.0 0.6 broadcast_in_dim.10
  10.7 10.9 %all-to-all-start = ((s32[64,1,128]{2,1,0:T(1,128)}), s32[64,1,128]{2,1,0:T(1,128)S(1)}, u32[]{:S(2)}, u32[]{:S(2)}) async-start(s32[64,1,128]{2,1,0:T(1,128)} %bitcast.5), calls=%async_computation | async-start | bytes 65536 | tf_op jit(solution)/shard_map/all_to_all | solution.py:227
  21.6 0.9 pad_dynamic-slice_fusion
  22.5 33.5 %all-gather = f32[448,512]{1,0:T(8,128)S(1)} all-gather(f32[56,512]{1,0:T(8,128)S(1)} %pad_dynamic-slice_fusion), channel_id=2, replica_groups=mesh['h'=8,'l'=2,'y'=4,'rep'=8] {'h'}, dimensions={0}, use_global_device_ids=true | all-gather | bytes 1032192 | tf_op jit(solution)/shard_map/all_gather | solution.py:222
  55.9 0.0 all-to-all-done
  56.0 0.1 copy.39
  56.0 0.2 copy.40
  56.3 0.3 reshape.81.ids_ref
  56.6 6.1 %shard_map.95 = f32[64,56,128]{2,1,0:T(8,128)S(1)} custom-call(f32[8,56,512]{2,1,0:T(8,128)S(1)} %bitcast.36, s32[8,1,1024]{2,1,0:T(1,128)S(1)} %reshape.81.ids_ref), custom_call_target="tpu_custom_call" | custom-call | flops 1677721600 | bytes 2785280 | tf_op jit(solution)/shard_map/pallas_call | solution.py:198
  62.6 0.0 copy-start.1
  62.6 1.3 copy-done.1
  63.9 0.0 copy-start.8
  63.9 0.0 copy-start.9
  63.9 0.0 copy-start.10
  63.9 0.0 copy-start.7
  63.9 0.0 copy-start
  63.9 13.8 %all-to-all-start.1 = ((f32[64,56,128]{2,1,0:T(8,128)}), f32[64,56,128]{2,1,0:T(8,128)S(1)}, u32[]{:S(2)}, u32[]{:S(2)}) async-start(f32[64,56,128]{2,1,0:T(8,128)} %copy-done.1), calls=%async_computation.1 | async-start | bytes 3670016 | tf_op jit(solution)/shard_map/all_to_all | solution.py:241
  77.8 0.0 copy-done.8
  77.8 0.1 copy.42
  77.9 0.1 reshape.73.src_ref
  78.0 0.0 copy-done.9
  78.0 0.1 copy.44
  78.1 0.1 reshape.75.rel_ref
  78.2 0.0 copy-done.10
  78.2 0.7 reduce.7
  78.8 0.1 reshape.76
  78.9 0.1 copy.46
  79.0 0.1 fusion
  79.1 0.1 reshape.79.live_ref
  79.2 0.0 copy-done.7
  79.3 0.0 copy-done
  79.3 1.1 shard_map.96
  80.4 0.0 copy-start.5
  80.4 0.9 copy-done.5
  81.3 21.3 %all-to-all-done.1.got_ref = f32[64,56,128]{2,1,0:T(8,128)S(1)} async-done(((f32[64,56,128]{2,1,0:T(8,128)}), f32[64,56,128]{2,1,0:T(8,128)S(1)}, u32[]{:S(2)}, u32[]{:S(2)}) %all-to-all-start.1) | async-done | bytes 1835040 | tf_op jit(solution)/shard_map/all_to_all | solution.py:241
  102.6 2.3 shard_map.98
  104.9 0.0 copy-start.2
  104.9 1.2 copy-done.2
  106.1 6.7 %all-to-all-start.2 = ((f32[64,56,128]{2,1,0:T(8,128)}), f32[64,56,128]{2,1,0:T(8,128)}, u32[]{:S(2)}, u32[]{:S(2)}) async-start(f32[64,56,128]{2,1,0:T(8,128)} %copy-done.2), calls=%async_computation.3 | async-start | bytes 3670016 | tf_op jit(solution)/shard_map/all_to_all | solution.py:243
  112.8 0.0 reduce-scatter.3.cloned.1.call-start
  112.9 0.0 copy-start.6
  112.9 1.1 copy-done.6
  114.0 2.5 %shard_map.97 = f32[8,56,512]{2,1,0:T(8,128)S(1)} custom-call(f32[64,56,128]{2,1,0:T(8,128)S(1)} %all-to-all-done.1.got_ref, f32[400,512]{1,0:T(8,128)S(1)} %get-tuple-element.8.query_ref, f32[400,512]{1,0:T(8,128)S(1)} %copy-done.6, f32[1,512]{1,0:T(1,128)S(1)} %reshape.79.live_ref, s32[1,512]{1,0:T(1,128)S(1)} %reshape.73.src_ref), custom_call_target="tpu_custom_call" | custom-call | flops 1677721600 | bytes 4395008 | tf_op jit(solution)/shard_map/pallas_call | solution.py:198
  116.6 0.0 copy-start.3
  116.6 0.9 copy-done.3
  117.5 0.0 reduce-scatter.3.cloned.1.call-update
  117.5 20.0 %all-to-all-done.2.msg_ref = f32[64,56,128]{2,1,0:T(8,128)} async-done(((f32[64,56,128]{2,1,0:T(8,128)}), f32[64,56,128]{2,1,0:T(8,128)}, u32[]{:S(2)}, u32[]{:S(2)}) %all-to-all-start.2) | async-done | bytes 1835040 | tf_op jit(solution)/shard_map/all_to_all | solution.py:243
  137.6 9.1 %shard_map.99 = (f32[8,24,512]{2,1,0:T(8,128)}, f32[8,32,512]{2,1,0:T(8,128)}) custom-call(f32[64,56,128]{2,1,0:T(8,128)} %all-to-all-done.2.msg_ref, s32[8,1,1024]{2,1,0:T(1,128)S(1)} %reshape.81.ids_ref), custom_call_target="tpu_custom_call" | custom-call | flops 1677721600 | bytes 2785280 | tf_op jit(solution)/shard_map/pallas_call | solution.py:198
  146.6 0.0 copy-start.4
  146.6 7.9 %all-to-all-start.3 = ((f32[8,24,512]{2,1,0:T(8,128)}), f32[8,24,512]{2,1,0:T(8,128)S(1)}, u32[]{:S(2)}, u32[]{:S(2)}) async-start(f32[8,24,512]{2,1,0:T(8,128)} %get-tuple-element.10), calls=%async_computation.4 | async-start | bytes 786432 | tf_op jit(solution)/shard_map/all_to_all | solution.py:253
  154.6 0.0 reduce-scatter.5.cloned.1.call-start
  154.6 0.7 reduce-scatter.5.cloned.1.call-update
  155.3 20.0 %all-to-all-done.3 = f32[8,24,512]{2,1,0:T(8,128)S(1)} async-done(((f32[8,24,512]{2,1,0:T(8,128)}), f32[8,24,512]{2,1,0:T(8,128)S(1)}, u32[]{:S(2)}, u32[]{:S(2)}) %all-to-all-start.3) | async-done | bytes 393248 | tf_op jit(solution)/shard_map/all_to_all | solution.py:253
  175.3 0.0 reduce-scatter.3.cloned.1.call-done
  175.4 26.9 %reduce-scatter.5.cloned.1.call-done = f32[1,32,512]{2,1,0:T(8,128)} async-done(((f32[8,32,512]{2,1,0:T(8,128)}), f32[1,32,512]{2,1,0:T(8,128)}) %reduce-scatter.5.cloned.1.call-update) | async-done | bytes 65552 | tf_op jit(solution)/shard_map/reduce_scatter | solution.py:252
  202.3 0.9 maximum_add_fusion
  203.2 19.0 %all_gather.12.grad_ref = f32[8,56,512]{2,1,0:T(8,128)S(1)} all-gather(f32[1,56,512]{2,1,0:T(8,128)S(1)} %maximum_add_fusion), channel_id=1, replica_groups=mesh['h'=8,'l'=2,'y'=4,'rep'=8] {'rep'}, dimensions={0}, use_global_device_ids=true | all-gather | bytes 1032192 | tf_op jit(solution)/shard_map/all_gather | solution.py:254
  222.2 0.0 copy-done.4
  222.2 1.1 shard_map.100
  (6 shorter events, 0.1 us)
Async XLA Ops:
  10.7 45.3 %all-to-all-start = ((s32[64,1,128]{2,1,0:T(1,128)}), s32[64,1,128]{2,1,0:T(1,128)S(1)}, u32[]{:S(2)}, u32[]{:S(2)}) async-start(s32[64,1,128]{2,1,0:T(1,128)} %bitcast.5), calls=%async_computation | async-start | bytes 65536 | tf_op jit(solution)/shard_map/all_to_all | solution.py:227
  62.6 1.3 copy-start.1
  63.9 13.9 %copy-start.8 = (s32[1,1,64,8]{2,3,1,0:T(8,128)S(1)}, s32[1,1,64,8]{2,3,1,0:T(8,128)}, u32[]{:S(2)}) copy-start(s32[1,1,64,8]{2,3,1,0:T(8,128)} %param.11) | copy-start | bytes 6148
  63.9 14.1 %copy-start.9 = (s32[1,1,64,8]{2,3,1,0:T(8,128)S(1)}, s32[1,1,64,8]{2,3,1,0:T(8,128)}, u32[]{:S(2)}) copy-start(s32[1,1,64,8]{2,3,1,0:T(8,128)} %param.13) | copy-start | bytes 6148
  63.9 14.3 %copy-start.10 = (s32[1,1,64]{2,1,0:T(1,128)S(1)}, s32[1,1,64]{2,1,0:T(1,128)}, u32[]{:S(2)}) copy-start(s32[1,1,64]{2,1,0:T(1,128)} %param.14) | copy-start | bytes 772
  63.9 15.3 %copy-start.7 = (f32[237,400]{0,1:T(8,128)S(1)}, f32[237,400]{0,1:T(8,128)}, u32[]{:S(2)}) copy-start(f32[237,400]{0,1:T(8,128)} %param.10) | copy-start | bytes 1137604
  63.9 15.4 %copy-start = (f32[512,400]{0,1:T(8,128)S(1)}, f32[512,400]{0,1:T(8,128)}, u32[]{:S(2)}) copy-start(f32[512,400]{0,1:T(8,128)} %param.8) | copy-start | bytes 2457604
  63.9 38.6 %all-to-all-start.1 = ((f32[64,56,128]{2,1,0:T(8,128)}), f32[64,56,128]{2,1,0:T(8,128)S(1)}, u32[]{:S(2)}, u32[]{:S(2)}) async-start(f32[64,56,128]{2,1,0:T(8,128)} %copy-done.1), calls=%async_computation.1 | async-start | bytes 3670016 | tf_op jit(solution)/shard_map/all_to_all | solution.py:241
  80.4 0.9 copy-start.5
  104.9 1.3 copy-start.2
  106.1 31.4 %all-to-all-start.2 = ((f32[64,56,128]{2,1,0:T(8,128)}), f32[64,56,128]{2,1,0:T(8,128)}, u32[]{:S(2)}, u32[]{:S(2)}) async-start(f32[64,56,128]{2,1,0:T(8,128)} %copy-done.2), calls=%async_computation.3 | async-start | bytes 3670016 | tf_op jit(solution)/shard_map/all_to_all | solution.py:243
  112.8 62.5 %reduce-scatter.3.cloned.1.call-start = ((), (), s32[]{:S(2)}) async-start(), calls=%async_computation.6 | async-start | bytes 1032192 | tf_op jit(solution)/shard_map/reduce_scatter | solution.py:247
  112.9 1.1 copy-start.6
  116.6 0.9 copy-start.3
  146.6 75.6 %copy-start.4 = (f32[512]{0:T(512)S(1)}, f32[512]{0:T(512)}, u32[]{:S(2)}) copy-start(f32[512]{0:T(512)} %param.9) | copy-start | bytes 6148
  146.6 28.7 %all-to-all-start.3 = ((f32[8,24,512]{2,1,0:T(8,128)}), f32[8,24,512]{2,1,0:T(8,128)S(1)}, u32[]{:S(2)}, u32[]{:S(2)}) async-start(f32[8,24,512]{2,1,0:T(8,128)} %get-tuple-element.10), calls=%async_computation.4 | async-start | bytes 786432 | tf_op jit(solution)/shard_map/all_to_all | solution.py:253
  154.6 47.7 %reduce-scatter.5.cloned.1.call-start = ((), (), s32[]{:S(2)}) async-start(), calls=%async_computation.7 | async-start | bytes 589824 | tf_op jit(solution)/shard_map/reduce_scatter | solution.py:252
Sparse Core Ops, SparseCore 0:
  117.6 35.2 reduce-scatter.2
  159.0 43.2 reduce-scatter.4

commit v5 on v3

--- a/solution.py
+++ b/solution.py
@@ -1,4 +1,5 @@
 import functools
+import math
 
 import jax
 import jax.numpy as jnp
@@ -66,11 +67,52 @@
     return v
 
 
-def query_kernel(et_ref, relt_ref, src_ref, rel_ref, query_ref, relation_ref):
+def order_kernel(nh, nl, ny, *refs):
+    given, (src_out, rel_out, live_out, wanted_ref), held, sems = refs[:5], refs[5:9], refs[9:14], refs[14]
+    copies = [pltpu.make_async_copy(a, b, sems.at[i]) for i, (a, b) in enumerate(zip(given, held))]
+    for copy in copies:
+        copy.start()
+    for copy in copies:
+        copy.wait()
+    src_ref, rel_ref, dst_ref, noise_ref, count_ref = held
+    slots, parts = src_ref.shape
+    edges = parts * slots
+    lane = lax.broadcasted_iota(jnp.int32, (1, edges), 1)
+    slot, group = lane % slots, lane // slots
+    h, l, y = group % nh, group // nh % nl, group // (nh * nl)
+    part = (h * nl + l) * ny + y
+    here = one_hot(part, parts)
+    stack = jnp.concatenate([src_ref[...], rel_ref[...], dst_ref[...]], axis=0).astype(F32)
+    spread = pick(stack, here, terms=2)
+    row = lax.broadcasted_iota(jnp.int32, (slots, edges), 0)
+
+    def own(i):
+        mine = jnp.where(row == slot, spread[i * slots : (i + 1) * slots], 0.0)
+        return jnp.sum(mine, axis=0, keepdims=True).astype(jnp.int32)
+
+    src_out[...] = own(0)
+    rel_out[...] = own(1)
+    target = own(2)
+    wide = jnp.broadcast_to(noise_ref[...].astype(F32), (8, edges))
+    noise = pick(wide, one_hot(part * slots + slot, edges), terms=2)[:1].astype(jnp.int32)
+    wide = jnp.broadcast_to(count_ref[...].astype(F32), (8, parts))
+    count = mul(wide.astype(BF16), here)[:1].astype(jnp.int32)
+    live_out[...] = (slot < count).astype(F32)
+    devices, span = wanted_ref.shape
+    per = devices // (nl * ny)
+    low = lax.broadcasted_iota(jnp.int32, (1, span), 1) < span // 2
+    for i in range(ny):
+        a, b = noise[:, i * span : (i + 1) * span], target[:, i * span : (i + 1) * span]
+        first = jnp.where(low, a, pltpu.roll(b, span // 2, 1))
+        second = jnp.where(low, pltpu.roll(a, span // 2, 1), b)
+        for k, block in enumerate((first, second)):
+            wanted_ref[(k * ny + i) * per : (k * ny + i + 1) * per] = jnp.broadcast_to(block, (per, span))
+
+
+def queries(et_ref, relt_ref, src_ref, rel_ref):
     source = pick(et_ref[...], one_hot(src_ref[...], et_ref.shape[1]))
     relation = pick(relt_ref[...], one_hot(rel_ref[...], relt_ref.shape[1]))
-    query_ref[...] = source * relation
-    relation_ref[...] = relation
+    return source * relation, relation
 
 
 def table_kernel(table_ref, ids_ref, out_ref, got_ref):
@@ -101,7 +143,7 @@
     lax.fori_loop(0, fs // 8, turn, 0)
 
 
-def scatter_kernel(msg_ref, ids_ref, out_ref, got_ref):
+def scatter_kernel(msg_ref, ids_ref, out_ref, got_ref, sum_ref, sems):
     nh, fs, rows = out_ref.shape
     devices, _, span = msg_ref.shape
     n = 2 * nh
@@ -120,11 +162,13 @@
 
     lax.fori_loop(0, fs // 8, turn, 0)
 
-    def add(h, carry):
-        out_ref[h] = pick(got_ref[h], one_hot(ids_ref[h], rows), NT, 2)
-        return carry
-
-    lax.fori_loop(0, nh, add, 0, unroll=2)
+    copies = []
+    for h in range(nh):
+        sum_ref[h] = pick(got_ref[h], one_hot(ids_ref[h], rows), NT, 2)
+        copies.append(pltpu.make_async_copy(sum_ref.at[h], out_ref.at[h], sems.at[h]))
+        copies[-1].start()
+    for copy in copies:
+        copy.wait()
 
 
 def received(got_ref, ny, features):
@@ -161,20 +205,20 @@
     return coef, -jax.nn.sigmoid(-positive) * live
 
 
-def terms_kernel(ny, got_ref, query_ref, live_ref, msg_ref):
-    query = query_ref[...]
+def terms_kernel(ny, got_ref, et_ref, relt_ref, src_ref, rel_ref, live_ref, msg_ref):
+    query, _ = queries(et_ref, relt_ref, src_ref, rel_ref)
     noise, target = received(got_ref, ny, query.shape[0])
     coef, pos_coef = coefficients(query, noise, target, live_ref[...])
     send(msg_ref, ny, product(query, coef, NT), pos_coef * query)
 
 
-def source_kernel(ny, got_ref, query_ref, relation_ref, live_ref, src_ref, out_ref):
+def source_kernel(ny, got_ref, et_ref, relt_ref, src_ref, rel_ref, live_ref, out_ref):
     reps, fs, rows = out_ref.shape
-    query = query_ref[...]
+    query, relation = queries(et_ref, relt_ref, src_ref, rel_ref)
     features = query.shape[0]
     noise, target = received(got_ref, ny, features)
     coef, pos_coef = coefficients(query, noise, target, live_ref[...])
-    grad = relation_ref[...] * (pos_coef * target + product(noise, coef))
+    grad = relation * (pos_coef * target + product(noise, coef))
     grad = pick(grad, one_hot(src_ref[...], rows), NT, 2)
     rest = reps * fs - features
     if rest:
@@ -190,12 +234,19 @@
     entity_ref[...] = et_ref[...] - LEARN_RATE * grad / jnp.sqrt(state)
 
 
-def call(kernel, outs, *args, scratch=(), flops=0):
-    shapes = [jax.ShapeDtypeStruct(shape, F32) for shape in outs]
-    moved = sum(4 * a.size for a in args) + sum(4 * s.size for s in shapes)
+def floats(*shapes):
+    return [(shape, F32) for shape in shapes]
+
+
+def call(kernel, outs, *args, scratch=(), flops=0, inputs=pltpu.VMEM, outputs=pltpu.VMEM):
+    make = pltpu.HBM if outputs == pltpu.HBM else jax.ShapeDtypeStruct
+    shapes = [make(shape, dtype) for shape, dtype in outs]
+    moved = sum(4 * a.size for a in args) + sum(4 * math.prod(shape) for shape, _ in outs)
     return pl.pallas_call(
         kernel,
         out_shape=shapes,
+        in_specs=[pl.BlockSpec(memory_space=inputs)] * len(args),
+        out_specs=[pl.BlockSpec(memory_space=outputs)] * len(outs),
         scratch_shapes=list(scratch),
         cost_estimate=pl.CostEstimate(flops=flops, bytes_accessed=moved, transcendentals=0),
         compiler_params=pltpu.CompilerParams(vmem_limit_bytes=48 << 20),
@@ -211,43 +262,50 @@
     edges = nh * nl * ny * slots
     fs = round_up(features, reps * 8) // reps
 
-    def ordered(ids):
-        return ids.reshape(nh, nl, ny, slots).transpose(2, 1, 0, 3).reshape(1, edges)
-
     et = entity.T
     padded = jnp.pad(et, ((0, reps * fs - features), (0, 0)))
     mine = lax.dynamic_slice_in_dim(padded, lax.axis_index("rep") * fs, fs, 0)
     table = lax.all_gather(mine, "h")
 
-    wanted = jnp.stack([noise_rows.reshape(nh, nl, ny, slots), dst_rows.reshape(nh, nl, ny, slots)])
-    wanted = wanted.transpose(2, 3, 0, 1, 4).reshape(nl, ny, 1, 2 * nh * slots)
-    wanted = jnp.broadcast_to(wanted, (nl, ny, reps, 2 * nh * slots)).reshape(devices, -1)
+    def turned(ids):
+        return ids.reshape(nh * nl * ny, slots).T
+
+    given = [turned(ids) for ids in (src_rows, rel_ids, dst_rows)]
+    given += [noise_rows.reshape(1, edges), bucket_counts.reshape(1, -1)]
+    row = ((1, edges), jnp.int32)
+    src, rel, live, wanted = call(
+        functools.partial(order_kernel, nh, nl, ny),
+        [row, row, ((1, edges), F32), ((devices, 2 * nh * slots), jnp.int32)],
+        *(pltpu.with_memory_space_constraint(a, pltpu.HBM) for a in given),
+        scratch=[pltpu.VMEM(a.shape, a.dtype) for a in given] + [pltpu.SemaphoreType.DMA((len(given),))],
+        inputs=pltpu.HBM,
+    )
     asked = lax.all_to_all(wanted, near, split_axis=0, concat_axis=0, tiled=True)
     asked = asked.reshape(devices, 2, nh, slots).transpose(2, 1, 0, 3).reshape(nh, 1, -1)
-
-    src = ordered(src_rows)
-    rel = ordered(rel_ids)
-    live = jnp.arange(slots, dtype=jnp.int32) < bucket_counts.reshape(nh, nl, ny).transpose(2, 1, 0)[..., None]
-    live = live.astype(F32).reshape(1, edges)
-    relt = jnp.pad(relation.T, ((0, 0), (0, round_up(relation.shape[0], 128) - relation.shape[0])))
+    relt = relation.T
 
     unit = 2 * edges * features * rows
     message = (devices, fs, 2 * nh * slots)
     got_shape = pltpu.VMEM((nh, fs, 2 * devices * slots), F32)
-    query, relation_rows = call(query_kernel, [(features, edges)] * 2, et, relt, src, rel, flops=5 * unit)
-    (found,) = call(table_kernel, [message], table, asked, scratch=[got_shape], flops=8 * unit)
+    (found,) = call(table_kernel, floats(message), table, asked, scratch=[got_shape], flops=8 * unit)
     got = lax.all_to_all(found, near, split_axis=0, concat_axis=0, tiled=True)
-    (terms,) = call(functools.partial(terms_kernel, ny), [message], got, query, live, flops=6 * unit)
+    edge_args = (got, et, relt, src, rel, live)
+    (terms,) = call(functools.partial(terms_kernel, ny), floats(message), *edge_args, flops=11 * unit)
     terms = lax.all_to_all(terms, near, split_axis=0, concat_axis=0, tiled=True)
-    (source,) = call(
-        functools.partial(source_kernel, ny), [(reps, fs, rows)], got, query, relation_rows, live, src, flops=8 * unit
+    (partial,) = call(
+        scatter_kernel,
+        floats((nh, fs, rows)),
+        terms, asked,
+        scratch=[got_shape, pltpu.VMEM((nh, fs, rows), F32), pltpu.SemaphoreType.DMA((nh,))],
+        flops=8 * unit,
+        outputs=pltpu.HBM,
     )
-    (partial,) = call(scatter_kernel, [(nh, fs, rows)], terms, asked, scratch=[got_shape], flops=8 * unit)
+    (source,) = call(functools.partial(source_kernel, ny), floats((reps, fs, rows)), *edge_args, flops=13 * unit)
     grad = lax.psum_scatter(partial, "h", scatter_dimension=0)
     shares = lax.all_to_all(source, "rep", split_axis=0, concat_axis=0, tiled=True)
     summed = lax.all_gather(grad + jnp.sum(shares, axis=0), "rep")
     new_entity, new_state = call(
-        update_kernel, [(features, rows), (1, rows)], summed, et, adagrad_state.reshape(1, rows)
+        update_kernel, floats((features, rows), (1, rows)), summed, et, adagrad_state.reshape(1, rows)
     )
     return new_entity.T, new_state.reshape(rows)
 

time: 214 us -> 211 us (0.986)
  blocking collectives: 102 us -> 140 us
  waiting for transfers between devices: 41.3 us -> 20.2 us
  starting transfers between devices: 24.8 us -> 11 us
  local copies, waits for them, and re-layouts: 8.54 us -> 1.53 us
  Pallas kernels: 19.7 us -> 22.4 us
    all_to_all x0 -> x1, blocking collectives: none -> 38.4 us  [per_device(): got = lax.all_to_all(found, near, split_axis=0, concat_axis=0, tiled=True)]
    all_to_all x1 -> x0, waiting for transfers between devices: 21.2 us -> none  [per_device(): got = lax.all_to_all(found, near, split_axis=0, concat_axis=0, tiled=True)]
    all_to_all x1 -> x0, starting transfers between devices: 13.8 us -> none  [per_device(): got = lax.all_to_all(found, near, split_axis=0, concat_axis=0, tiled=True)]
    unnamed x24 -> x6, local copies, waits for them, and re-layouts: 5.68 us -> 0.02 us
    pallas_call x6, Pallas kernels: 19.7 us -> 22.4 us  [call(): pl.pallas_call(kernel, out_shape=shapes, in_specs=[pl.BlockSpec(memory_sp...]
  transfers between devices with their start and end apart: 3 -> 2, of which waited for: 2 -> 1; matrix products, arithmetic and copies ran while one was open for 1% -> 0% of each run, Pallas kernels for 2% -> 2%
where the time goes in v5:
time: 211 us
  blocking collectives  140 us (66%)
  Pallas kernels  22.4 us (11%)
  waiting for transfers between devices  20.2 us (10%)
  between operations  14.1 us (7%)
  starting transfers between devices  11 us (5%)
    all_to_all x1, blocking collectives, per_device(): got = lax.all_to_all(found, near, split_axis=0, concat_axis=0, tiled=True)  38.4 us
    all_gather x1, blocking collectives, per_device(): table = lax.all_gather(mine, 'h')  33.5 us
    all_to_all x1, blocking collectives, per_device(): terms = lax.all_to_all(terms, near, split_axis=0, concat_axis=0, tiled=True)  31.1 us
    pallas_call x6, Pallas kernels, call(): pl.pallas_call(kernel, out_shape=shapes, in_specs=[pl.BlockSpec(memory_sp...  22.4 us
    reduce_scatter x1, waiting for transfers between devices, per_device(): grad = lax.psum_scatter(partial, 'h', scatter_dimension=0)  20.2 us
    all_gather x1, blocking collectives, per_device(): summed = lax.all_gather(grad + jnp.sum(shares, axis=0), 'rep')  18.9 us
    all_to_all x1, blocking collectives, per_device(): lax.all_to_all(source, 'rep', split_axis=0, concat_axis=0, tiled=True)  18.4 us
    all_to_all x1, starting transfers between devices, per_device(): lax.all_to_all(wanted, near, split_axis=0, concat_axis=0, tiled=True)  10.9 us
  transfers between devices with their start and end apart: 2, of which 1 were waited for; matrix products, arithmetic and copies ran while one was open for 0% of the time, Pallas kernels for 2%

profile of v5, /device:TPU:1, one launch (start us, length us, event | category | flops | bytes accessed | tf_op | source)
XLA Modules:
  0.0 210.5 jit_solution(6698862910601895993)
XLA Ops:
  7.2 1.7 shard_map.95
  8.9 10.9 %all-to-all-start = ((s32[64,1,128]{2,1,0:T(1,128)}), s32[64,1,128]{2,1,0:T(1,128)S(1)}, u32[]{:S(2)}, u32[]{:S(2)}) async-start(s32[64,1,128]{2,1,0:T(1,128)} %bitcast.11), calls=%async_computation | async-start | bytes 65536 | tf_op jit(solution)/shard_map/all_to_all | solution.py:283
  19.8 0.0 reduce-scatter.2.cloned.1.call-start
  19.8 0.9 pad_dynamic-slice_fusion
  20.8 33.5 %all-gather = f32[448,512]{1,0:T(8,128)S(1)} all-gather(f32[56,512]{1,0:T(8,128)S(1)} %pad_dynamic-slice_fusion), channel_id=2, replica_groups=mesh['h'=8,'l'=2,'y'=4,'rep'=8] {'h'}, dimensions={0}, use_global_device_ids=true | all-gather | bytes 1032192 | tf_op jit(solution)/shard_map/all_gather | solution.py:268
  54.2 0.0 all-to-all-done
  54.2 0.1 copy.16
  54.3 0.2 copy.17
  54.6 0.3 reshape.45.ids_ref
  54.9 6.1 %shard_map.96 = f32[64,56,128]{2,1,0:T(8,128)S(1)} custom-call(f32[8,56,512]{2,1,0:T(8,128)S(1)} %bitcast.31, s32[8,1,1024]{2,1,0:T(1,128)S(1)} %reshape.45.ids_ref), custom_call_target="tpu_custom_call" | custom-call | flops 1677721600 | bytes 2785280 | tf_op jit(solution)/shard_map/pallas_call | solution.py:245
  60.9 0.0 copy-start
  60.9 0.0 copy-start.2
  60.9 38.4 %all_to_all.24.got_ref = f32[64,56,128]{2,1,0:T(8,128)S(1)} all-to-all(f32[64,56,128]{2,1,0:T(8,128)S(1)} %shard_map.96), channel_id=1, replica_groups=mesh['h'=8,'l'=2,'y'=4,'rep'=8] {'l','y','rep'}, dimensions={0} | all-to-all | bytes 3670016 | tf_op jit(solution)/shard_map/all_to_all | solution.py:291
  99.3 0.0 copy-done
  99.4 0.0 copy-done.2
  99.4 3.1 %shard_map.97 = f32[64,56,128]{2,1,0:T(8,128)S(1)} custom-call(f32[64,56,128]{2,1,0:T(8,128)S(1)} %all_to_all.24.got_ref, f32[400,512]{1,0:T(8,128)S(1)} %bitcast.28, f32[400,237]{1,0:T(8,128)S(1)} %bitcast.33, s32[1,512]{1,0:T(1,128)S(1)} %get-tuple-element.9.src_ref, s32[1,512]{1,0:T(1,128)S(1)} %get-tuple-element.10.rel_ref, ...), custom_call_target="tpu_custom_call" | custom-call | flops 2306867200 | bytes 4874560 | tf_op jit(solution)/shard_map/pallas_call | solution.py:245
  102.5 31.1 %all_to_all.25.msg_ref = f32[64,56,128]{2,1,0:T(8,128)S(1)} all-to-all(f32[64,56,128]{2,1,0:T(8,128)S(1)} %shard_map.97), channel_id=1, replica_groups=mesh['h'=8,'l'=2,'y'=4,'rep'=8] {'l','y','rep'}, dimensions={0} | all-to-all | bytes 3670016 | tf_op jit(solution)/shard_map/all_to_all | solution.py:294
  133.6 7.0 %shard_map.98 = f32[8,56,512]{2,1,0:T(8,128)} custom-call(f32[64,56,128]{2,1,0:T(8,128)S(1)} %all_to_all.25.msg_ref, s32[8,1,1024]{2,1,0:T(1,128)S(1)} %reshape.45.ids_ref), custom_call_target="tpu_custom_call" | custom-call | flops 1677721600 | bytes 2785280 | tf_op jit(solution)/shard_map/pallas_call | solution.py:245
  140.6 0.0 reduce-scatter.2.cloned.1.call-update
  140.6 3.5 %shard_map.99 = f32[8,56,512]{2,1,0:T(8,128)S(1)} custom-call(f32[64,56,128]{2,1,0:T(8,128)S(1)} %all_to_all.24.got_ref, f32[400,512]{1,0:T(8,128)S(1)} %bitcast.29, f32[400,237]{1,0:T(8,128)S(1)} %bitcast.34, s32[1,512]{1,0:T(1,128)S(1)} %get-tuple-element.9.src_ref, s32[1,512]{1,0:T(1,128)S(1)} %get-tuple-element.10.rel_ref, ...), custom_call_target="tpu_custom_call" | custom-call | flops 2726297600 | bytes 3957056 | tf_op jit(solution)/shard_map/pallas_call | solution.py:245
  144.1 0.0 copy-start.1
  144.1 18.4 %all_to_all.26 = f32[8,56,512]{2,1,0:T(8,128)S(1)} all-to-all(f32[8,56,512]{2,1,0:T(8,128)S(1)} %shard_map.99), channel_id=1, replica_groups=mesh['h'=8,'l'=2,'y'=4,'rep'=8] {'rep'}, dimensions={0} | all-to-all | bytes 1835008 | tf_op jit(solution)/shard_map/all_to_all | solution.py:305
  162.5 0.1 reduce_sum.11
  162.6 20.2 %reduce-scatter.2.cloned.1.call-done = f32[1,56,512]{2,1,0:T(8,128)} async-done(((f32[8,56,512]{2,1,0:T(8,128)}), f32[1,56,512]{2,1,0:T(8,128)}) %reduce-scatter.2.cloned.1.call-update) | async-done | bytes 114704 | tf_op jit(solution)/shard_map/reduce_scatter | solution.py:304
  182.8 0.9 bitcast_add_fusion
  183.7 18.9 %all_gather.12.grad_ref = f32[8,56,512]{2,1,0:T(8,128)S(1)} all-gather(f32[1,56,512]{2,1,0:T(8,128)S(1)} %bitcast_add_fusion), channel_id=1, replica_groups=mesh['h'=8,'l'=2,'y'=4,'rep'=8] {'rep'}, dimensions={0}, use_global_device_ids=true | all-gather | bytes 1032192 | tf_op jit(solution)/shard_map/all_gather | solution.py:306
  202.6 0.0 copy-done.1
  202.6 1.1 shard_map.100
Async XLA Ops:
  8.9 45.4 %all-to-all-start = ((s32[64,1,128]{2,1,0:T(1,128)}), s32[64,1,128]{2,1,0:T(1,128)S(1)}, u32[]{:S(2)}, u32[]{:S(2)}) async-start(s32[64,1,128]{2,1,0:T(1,128)} %bitcast.11), calls=%async_computation | async-start | bytes 65536 | tf_op jit(solution)/shard_map/all_to_all | solution.py:283
  19.8 163.0 %reduce-scatter.2.cloned.1.call-start = ((), (), s32[]{:S(2)}) async-start(), calls=%async_computation.5 | async-start | bytes 1032192 | tf_op jit(solution)/shard_map/reduce_scatter | solution.py:304
  60.9 38.4 %copy-start = (f32[512,400]{0,1:T(8,128)S(1)}, f32[512,400]{0,1:T(8,128)}, u32[]{:S(2)}) copy-start(f32[512,400]{0,1:T(8,128)} %param.8) | copy-start | bytes 2457604
  60.9 38.4 %copy-start.2 = (f32[237,400]{0,1:T(8,128)S(1)}, f32[237,400]{0,1:T(8,128)}, u32[]{:S(2)}) copy-start(f32[237,400]{0,1:T(8,128)} %param.10) | copy-start | bytes 1137604
  144.1 58.5 %copy-start.1 = (f32[512]{0:T(512)S(1)}, f32[512]{0:T(512)}, u32[]{:S(2)}) copy-start(f32[512]{0:T(512)} %param.9) | copy-start | bytes 6148
Sparse Core Ops, SparseCore 0:
  140.7 42.0 reduce-scatter.1

commit v6 on v5

--- a/solution.py
+++ b/solution.py
@@ -115,56 +115,67 @@
     return source * relation, relation
 
 
-def table_kernel(table_ref, ids_ref, out_ref, got_ref):
-    nh, fs, rows = table_ref.shape
-    devices, _, span = out_ref.shape
+def chunks(fs):
+    return list(range(0, fs - 7, 8)) + ([fs - 8] if fs % 8 else [])
+
+
+def table_kernel(fs, table_ref, ids_ref, out_ref, got_ref, stack_ref):
+    nh, held, lanes = got_ref.shape
+    span = out_ref.shape[1]
+    devices = out_ref.shape[0] // fs
+    tiles = table_ref.shape[0] // (nh * fs)
     n = 2 * nh
     slots = span // n
-
-    def fetch(h, carry):
-        got_ref[h] = pick(table_ref[h], one_hot(ids_ref[h], rows))
-        return carry
-
-    lax.fori_loop(0, nh, fetch, 0, unroll=2)
+    terms = stack_ref.shape[0] // held
+
+    for h in range(nh):
+        for t in range(tiles):
+            rows = table_ref[pl.ds(h * tiles * fs + t, fs, stride=tiles), :]
+            for i, part in enumerate(split(rows, terms)):
+                stack_ref[i * held : i * held + fs, t * 128 : (t + 1) * 128] = part.astype(F32)
+        found = mul(stack_ref[...].astype(BF16), one_hot(ids_ref[h], tiles * 128))
+        got_ref[h] = sum(found[i * held : (i + 1) * held] for i in range(terms - 1, -1, -1))
     lane = lax.broadcasted_iota(jnp.int32, (8, span), 1) // slots
 
-    def turn(f8, carry):
-        at = pl.ds(pl.multiple_of(f8 * 8, 8), 8)
-        for tile in range(devices // n):
+    def turn(tile, carry):
+        for f in chunks(fs):
             v = []
             for kind in range(2):
-                start = (kind * devices + tile * n) * slots
-                v += [got_ref[h, at, start : start + span] for h in range(nh)]
+                start = pl.multiple_of((kind * devices + tile * n) * slots, span)
+                v += [got_ref[h, f : f + 8, pl.ds(start, span)] for h in range(nh)]
             v = swap_blocks(v, slots, lane)
             for i in range(n):
-                out_ref[tile * n + i, at, :] = v[i]
+                out_ref[pl.ds((tile * n + i) * fs + f, 8), :] = v[i]
         return carry
 
-    lax.fori_loop(0, fs // 8, turn, 0)
-
-
-def scatter_kernel(msg_ref, ids_ref, out_ref, got_ref, sum_ref, sems):
-    nh, fs, rows = out_ref.shape
-    devices, _, span = msg_ref.shape
+    lax.fori_loop(0, devices // n, turn, 0)
+
+
+def scatter_kernel(fs, msg_ref, ids_ref, out_ref, got_ref, sum_ref, sems):
+    nh, held, lanes = got_ref.shape
+    span = msg_ref.shape[1]
+    devices = msg_ref.shape[0] // fs
+    tiles = out_ref.shape[1] // fs
     n = 2 * nh
     slots = span // n
     lane = lax.broadcasted_iota(jnp.int32, (8, span), 1) // slots
 
-    def turn(f8, carry):
-        at = pl.ds(pl.multiple_of(f8 * 8, 8), 8)
-        for tile in range(devices // n):
-            v = swap_blocks([msg_ref[tile * n + i, at, :] for i in range(n)], slots, lane)
+    def turn(tile, carry):
+        for f in chunks(fs):
+            v = swap_blocks([msg_ref[pl.ds((tile * n + i) * fs + f, 8), :] for i in range(n)], slots, lane)
             for kind in range(2):
-                start = (kind * devices + tile * n) * slots
+                start = pl.multiple_of((kind * devices + tile * n) * slots, span)
                 for h in range(nh):
-                    got_ref[h, at, start : start + span] = v[kind * nh + h]
+                    got_ref[h, f : f + 8, pl.ds(start, span)] = v[kind * nh + h]
         return carry
 
-    lax.fori_loop(0, fs // 8, turn, 0)
+    lax.fori_loop(0, devices // n, turn, 0)
 
     copies = []
     for h in range(nh):
-        sum_ref[h] = pick(got_ref[h], one_hot(ids_ref[h], rows), NT, 2)
+        grad = pick(got_ref[h], one_hot(ids_ref[h], tiles * 128), NT, 2)
+        for t in range(tiles):
+            sum_ref[h, t * fs : (t + 1) * fs] = grad[:fs, t * 128 : (t + 1) * 128]
         copies.append(pltpu.make_async_copy(sum_ref.at[h], out_ref.at[h], sems.at[h]))
         copies[-1].start()
     for copy in copies:
@@ -172,31 +183,25 @@
 
 
 def received(got_ref, ny, features):
-    devices, fs, span = got_ref.shape
-    per = devices // (2 * ny)
+    span = got_ref.shape[1]
     low = lax.broadcasted_iota(jnp.int32, (1, span), 1) < span // 2
     noise, target = [], []
     for y in range(ny):
-        first, second = (
-            got_ref[(l * ny + y) * per : (l * ny + y + 1) * per].reshape(per * fs, span)[:features] for l in range(2)
-        )
+        first, second = (got_ref[(l * ny + y) * features : (l * ny + y + 1) * features] for l in range(2))
         noise.append(jnp.where(low, first, pltpu.roll(second, span // 2, 1)))
         target.append(jnp.where(low, pltpu.roll(first, span // 2, 1), second))
     return jnp.concatenate(noise, axis=1), jnp.concatenate(target, axis=1)
 
 
 def send(msg_ref, ny, noise, target):
-    devices, fs, span = msg_ref.shape
-    per = devices // (2 * ny)
+    features, span = noise.shape[0], msg_ref.shape[1]
     low = lax.broadcasted_iota(jnp.int32, (1, span), 1) < span // 2
-    rest = jnp.zeros((per * fs - noise.shape[0], span), F32)
     for y in range(ny):
         a, b = noise[:, y * span : (y + 1) * span], target[:, y * span : (y + 1) * span]
         first = jnp.where(low, a, pltpu.roll(b, span // 2, 1))
         second = jnp.where(low, pltpu.roll(a, span // 2, 1), b)
         for l, block in enumerate((first, second)):
-            full = jnp.concatenate([block, rest], axis=0) if rest.shape[0] else block
-            msg_ref[(l * ny + y) * per : (l * ny + y + 1) * per] = full.reshape(per, fs, span)
+            msg_ref[(l * ny + y) * features : (l * ny + y + 1) * features] = block
 
 
 def coefficients(query, noise, target, live):
@@ -212,26 +217,33 @@
     send(msg_ref, ny, product(query, coef, NT), pos_coef * query)
 
 
-def source_kernel(ny, got_ref, et_ref, relt_ref, src_ref, rel_ref, live_ref, out_ref):
-    reps, fs, rows = out_ref.shape
+def source_kernel(ny, reps, got_ref, et_ref, relt_ref, src_ref, rel_ref, live_ref, out_ref):
     query, relation = queries(et_ref, relt_ref, src_ref, rel_ref)
-    features = query.shape[0]
+    features, rows = et_ref.shape
+    fs, tiles = features // reps, rows // 128
     noise, target = received(got_ref, ny, features)
     coef, pos_coef = coefficients(query, noise, target, live_ref[...])
     grad = relation * (pos_coef * target + product(noise, coef))
     grad = pick(grad, one_hot(src_ref[...], rows), NT, 2)
-    rest = reps * fs - features
-    if rest:
-        grad = jnp.concatenate([grad, jnp.zeros((rest, rows), F32)], axis=0)
-    out_ref[...] = grad.reshape(reps, fs, rows)
-
-
-def update_kernel(grad_ref, et_ref, state_ref, entity_ref, new_state_ref):
+    for r in range(reps):
+        for t in range(tiles):
+            at = (r * tiles + t) * fs
+            out_ref[at : at + fs] = grad[r * fs : (r + 1) * fs, t * 128 : (t + 1) * 128]
+
+
+def update_kernel(reps, grad_ref, et_ref, state_ref, entity_ref, new_state_ref):
     features, rows = et_ref.shape
-    grad = grad_ref[...].reshape(-1, rows)[:features]
-    state = state_ref[...] + jnp.sum(grad * grad, axis=0, keepdims=True) * (1.0 / features)
-    new_state_ref[...] = state
-    entity_ref[...] = et_ref[...] - LEARN_RATE * grad / jnp.sqrt(state)
+    fs, tiles = features // reps, rows // 128
+    for t in range(tiles):
+        lanes = slice(t * 128, (t + 1) * 128)
+        grads = [grad_ref[(r * tiles + t) * fs : (r * tiles + t + 1) * fs] for r in range(reps)]
+        squares = sum(jnp.sum(grad * grad, axis=0, keepdims=True) for grad in grads)
+        state = state_ref[:, lanes] + squares * (1.0 / features)
+        new_state_ref[:, lanes] = state
+        scale = LEARN_RATE / jnp.sqrt(state)
+        for r, grad in enumerate(grads):
+            at = slice(r * fs, (r + 1) * fs)
+            entity_ref[at, lanes] = et_ref[at, lanes] - grad * scale
 
 
 def floats(*shapes):
@@ -260,12 +272,12 @@
     rows, features = entity.shape
     slots = src_rows.shape[3]
     edges = nh * nl * ny * slots
-    fs = round_up(features, reps * 8) // reps
+    fs, tiles = features // reps, rows // 128
+    packed = tiles * fs
 
     et = entity.T
-    padded = jnp.pad(et, ((0, reps * fs - features), (0, 0)))
-    mine = lax.dynamic_slice_in_dim(padded, lax.axis_index("rep") * fs, fs, 0)
-    table = lax.all_gather(mine, "h")
+    mine = lax.dynamic_slice_in_dim(et, lax.axis_index("rep") * fs, fs, 0)
+    table = lax.all_gather(mine.reshape(packed, 128), "h").reshape(nh * packed, 128)
 
     def turned(ids):
         return ids.reshape(nh * nl * ny, slots).T
@@ -285,27 +297,40 @@
     relt = relation.T
 
     unit = 2 * edges * features * rows
-    message = (devices, fs, 2 * nh * slots)
-    got_shape = pltpu.VMEM((nh, fs, 2 * devices * slots), F32)
-    (found,) = call(table_kernel, floats(message), table, asked, scratch=[got_shape], flops=8 * unit)
-    got = lax.all_to_all(found, near, split_axis=0, concat_axis=0, tiled=True)
+    span = 2 * nh * slots
+    message = (devices * fs, span)
+    wire = (devices, fs // 2, 2, span)
+    held = round_up(fs, 8)
+    got_shape = pltpu.VMEM((nh, held, 2 * devices * slots), F32)
+    (found,) = call(
+        functools.partial(table_kernel, fs),
+        floats(message),
+        table, asked,
+        scratch=[got_shape, pltpu.VMEM((3 * held, rows), F32)],
+        flops=8 * unit,
+    )
+    got = lax.all_to_all(found.reshape(wire), near, split_axis=0, concat_axis=0, tiled=True).reshape(message)
     edge_args = (got, et, relt, src, rel, live)
     (terms,) = call(functools.partial(terms_kernel, ny), floats(message), *edge_args, flops=11 * unit)
-    terms = lax.all_to_all(terms, near, split_axis=0, concat_axis=0, tiled=True)
+    terms = lax.all_to_all(terms.reshape(wire), near, split_axis=0, concat_axis=0, tiled=True).reshape(message)
     (partial,) = call(
-        scatter_kernel,
-        floats((nh, fs, rows)),
+        functools.partial(scatter_kernel, fs),
+        floats((nh, packed, 128)),
         terms, asked,
-        scratch=[got_shape, pltpu.VMEM((nh, fs, rows), F32), pltpu.SemaphoreType.DMA((nh,))],
+        scratch=[got_shape, pltpu.VMEM((nh, packed, 128), F32), pltpu.SemaphoreType.DMA((nh,))],
         flops=8 * unit,
         outputs=pltpu.HBM,
     )
-    (source,) = call(functools.partial(source_kernel, ny), floats((reps, fs, rows)), *edge_args, flops=13 * unit)
+    (source,) = call(
+        functools.partial(source_kernel, ny, reps), floats((reps * packed, 128)), *edge_args, flops=13 * unit
+    )
     grad = lax.psum_scatter(partial, "h", scatter_dimension=0)
-    shares = lax.all_to_all(source, "rep", split_axis=0, concat_axis=0, tiled=True)
-    summed = lax.all_gather(grad + jnp.sum(shares, axis=0), "rep")
+    shares = lax.all_to_all(source.reshape(reps, packed, 128), "rep", split_axis=0, concat_axis=0, tiled=True)
+    summed = lax.all_gather(grad + jnp.sum(shares, axis=0), "rep").reshape(reps * packed, 128)
     new_entity, new_state = call(
-        update_kernel, floats((features, rows), (1, rows)), summed, et, adagrad_state.reshape(1, rows)
+        functools.partial(update_kernel, reps),
+        floats((features, rows), (1, rows)),
+        summed, et, adagrad_state.reshape(1, rows),
     )
     return new_entity.T, new_state.reshape(rows)
 

time: 211 us -> 207 us (0.981)
  blocking collectives: 140 us -> 134 us
    unnamed x1 -> x2, waiting for transfers between devices: 0.02 us -> 20.9 us
    reduce_scatter x1 -> x0, waiting for transfers between devices: 20.2 us -> none  [per_device(): grad = lax.psum_scatter(partial, 'h', scatter_dimension=0)]
    all_to_all x3, blocking collectives: 88 us -> 83.6 us  [the longest x1 37.2 us: per_device(): lax.all_to_all(found.reshape(wire), near, split_axis=0, concat_axis=0, ti...]
where the time goes in v6:
time: 207 us
  blocking collectives  134 us (65%)
  Pallas kernels  24.4 us (12%)
  waiting for transfers between devices  20.9 us (10%)
  between operations  14.1 us (7%)
  starting transfers between devices  11 us (5%)
    all_to_all x1, blocking collectives, per_device(): lax.all_to_all(found.reshape(wire), near, split_axis=0, concat_axis=0, ti...  37.2 us
    all_gather x1, blocking collectives, per_device(): lax.all_gather(mine.reshape(packed, 128), 'h').reshape(nh * packed, 128)  31.9 us
    all_to_all x1, blocking collectives, per_device(): lax.all_to_all(terms.reshape(wire), near, split_axis=0, concat_axis=0, ti...  29.1 us
    pallas_call x6, Pallas kernels, call(): pl.pallas_call(kernel, out_shape=shapes, in_specs=[pl.BlockSpec(memory_sp...  24.4 us
    unnamed x2, waiting for transfers between devices  20.9 us
    all_gather x1, blocking collectives, per_device(): lax.all_gather(grad + jnp.sum(shares, axis=0), 'rep')  18.4 us
    all_to_all x1, blocking collectives, per_device(): lax.all_to_all(source.reshape(reps, packed, 128), 'rep', split_axis=0, co...  17.3 us
    all_to_all x1, starting transfers between devices, per_device(): lax.all_to_all(wanted, near, split_axis=0, concat_axis=0, tiled=True)  10.9 us
  transfers between devices with their start and end apart: 2, of which 1 were waited for; matrix products, arithmetic and copies ran while one was open for 0% of the time, Pallas kernels for 2%

profile of v6, /device:TPU:1, one launch (start us, length us, event | category | flops | bytes accessed | tf_op | source)
XLA Modules:
  0.0 206.7 jit_solution(8945265890730579948)
XLA Ops:
  7.2 1.7 shard_map.95
  8.9 10.9 %all-to-all-start = ((s32[64,1,128]{2,1,0:T(1,128)}), s32[64,1,128]{2,1,0:T(1,128)S(1)}, u32[]{:S(2)}, u32[]{:S(2)}) async-start(s32[64,1,128]{2,1,0:T(1,128)} %bitcast.11), calls=%async_computation | async-start | bytes 65536 | tf_op jit(solution)/shard_map/all_to_all | solution.py:295
  19.8 0.0 reduce-scatter.4.cloned.1.call-start
  19.8 0.9 dynamic-slice_bitcast_fusion
  20.8 31.9 %all_gather.7 = f32[8,200,128]{2,1,0:T(8,128)S(1)} all-gather(f32[1,200,128]{2,1,0:T(8,128)S(1)} %all_gather_reshape.3), channel_id=1, replica_groups=mesh['h'=8,'l'=2,'y'=4,'rep'=8] {'h'}, dimensions={0}, use_global_device_ids=true | all-gather | bytes 921600 | tf_op jit(solution)/shard_map/all_gather | solution.py:280
  52.7 0.0 all-to-all-done
  52.7 0.1 copy.16
  52.8 0.2 copy.17
  53.0 0.3 reshape.73.ids_ref
  53.3 7.1 %shard_map.96 = f32[3200,128]{1,0:T(8,128)S(1)} custom-call(f32[1600,128]{1,0:T(8,128)S(1)} %bitcast.45, s32[8,1,1024]{2,1,0:T(1,128)S(1)} %reshape.73.ids_ref), custom_call_target="tpu_custom_call" | custom-call | flops 1677721600 | bytes 2490368 | tf_op jit(solution)/shard_map/pallas_call | solution.py:257
  60.4 0.0 copy-start
  60.4 0.0 copy-start.2
  60.4 37.2 %all_to_all.24 = f32[64,25,2,128]{3,2,1,0:T(2,128)S(1)} all-to-all(f32[64,25,2,128]{3,2,1,0:T(2,128)S(1)} %bitcast.40), channel_id=1, replica_groups=mesh['h'=8,'l'=2,'y'=4,'rep'=8] {'l','y','rep'}, dimensions={0} | all-to-all | bytes 3276800 | tf_op jit(solution)/shard_map/all_to_all | solution.py:312
  97.7 0.0 copy-done
  97.7 0.0 copy-done.2
  97.7 3.1 %shard_map.97 = f32[3200,128]{1,0:T(8,128)S(1)} custom-call(f32[3200,128]{1,0:T(8,128)S(1)} %bitcast.37, f32[400,512]{1,0:T(8,128)S(1)} %bitcast.42, f32[400,237]{1,0:T(8,128)S(1)} %bitcast.48, s32[1,512]{1,0:T(1,128)S(1)} %get-tuple-element.9.src_ref, s32[1,512]{1,0:T(1,128)S(1)} %get-tuple-element.10.rel_ref, f32[1,512]{1,0:T(1,128)S(1)} %get-tuple-element.11.live_ref), custom_call_target="tpu_custom_call" | custom-call | flops 2306867200 | bytes 4481344 | tf_op jit(solution)/shard_map/pallas_call | solution.py:257
  100.7 29.1 %all_to_all.25 = f32[64,25,2,128]{3,2,1,0:T(2,128)S(1)} all-to-all(f32[64,25,2,128]{3,2,1,0:T(2,128)S(1)} %bitcast.41), channel_id=1, replica_groups=mesh['h'=8,'l'=2,'y'=4,'rep'=8] {'l','y','rep'}, dimensions={0} | all-to-all | bytes 3276800 | tf_op jit(solution)/shard_map/all_to_all | solution.py:315
  129.8 8.0 %shard_map.98 = f32[8,200,128]{2,1,0:T(8,128)} custom-call(f32[3200,128]{1,0:T(8,128)S(1)} %bitcast.39, s32[8,1,1024]{2,1,0:T(1,128)S(1)} %reshape.73.ids_ref), custom_call_target="tpu_custom_call" | custom-call | flops 1677721600 | bytes 2490368 | tf_op jit(solution)/shard_map/pallas_call | solution.py:257
  137.8 0.0 reduce-scatter.4.cloned.1.call-update
  137.8 3.5 %shard_map.99 = f32[1600,128]{1,0:T(8,128)S(1)} custom-call(f32[3200,128]{1,0:T(8,128)S(1)} %bitcast.38, f32[400,512]{1,0:T(8,128)S(1)} %bitcast.43, f32[400,237]{1,0:T(8,128)S(1)} %bitcast.49, s32[1,512]{1,0:T(1,128)S(1)} %get-tuple-element.9.src_ref, s32[1,512]{1,0:T(1,128)S(1)} %get-tuple-element.10.rel_ref, f32[1,512]{1,0:T(1,128)S(1)} %get-tuple-element.11.live_ref), custom_call_target="tpu_custom_call" | custom-call | flops 2726297600 | bytes 3662144 | tf_op jit(solution)/shard_map/pallas_call | solution.py:257
  141.2 0.0 copy-start.1
  141.3 17.3 %all_to_all.26 = f32[8,200,128]{2,1,0:T(8,128)S(1)} all-to-all(f32[8,200,128]{2,1,0:T(8,128)S(1)} %bitcast.46), channel_id=1, replica_groups=mesh['h'=8,'l'=2,'y'=4,'rep'=8] {'rep'}, dimensions={0} | all-to-all | bytes 1638400 | tf_op jit(solution)/shard_map/all_to_all | solution.py:328
  158.6 20.9 %reduce-scatter.4.cloned.1.call-done = f32[1,200,128]{2,1,0:T(8,128)} async-done(((f32[8,200,128]{2,1,0:T(8,128)}), f32[1,200,128]{2,1,0:T(8,128)}) %reduce-scatter.4.cloned.1.call-update) | async-done | bytes 102416
  179.4 0.9 bitcast_add_fusion
  180.4 18.4 %all_gather.8 = f32[8,200,128]{2,1,0:T(8,128)S(1)} all-gather(f32[1,200,128]{2,1,0:T(8,128)S(1)} %bitcast_add_fusion), channel_id=1, replica_groups=mesh['h'=8,'l'=2,'y'=4,'rep'=8] {'rep'}, dimensions={0}, use_global_device_ids=true | all-gather | bytes 921600 | tf_op jit(solution)/shard_map/all_gather | solution.py:329
  198.7 0.0 copy-done.1
  198.7 1.2 shard_map.100
  (2 shorter events, 0.1 us)
Async XLA Ops:
  8.9 43.8 %all-to-all-start = ((s32[64,1,128]{2,1,0:T(1,128)}), s32[64,1,128]{2,1,0:T(1,128)S(1)}, u32[]{:S(2)}, u32[]{:S(2)}) async-start(s32[64,1,128]{2,1,0:T(1,128)} %bitcast.11), calls=%async_computation | async-start | bytes 65536 | tf_op jit(solution)/shard_map/all_to_all | solution.py:295
  19.8 159.7 %reduce-scatter.4.cloned.1.call-start = ((), (), s32[]{:S(2)}) async-start(), calls=%async_computation.5 | async-start | bytes 921600
  60.4 37.3 %copy-start = (f32[512,400]{0,1:T(8,128)S(1)}, f32[512,400]{0,1:T(8,128)}, u32[]{:S(2)}) copy-start(f32[512,400]{0,1:T(8,128)} %param.8) | copy-start | bytes 2457604
  60.4 37.3 %copy-start.2 = (f32[237,400]{0,1:T(8,128)S(1)}, f32[237,400]{0,1:T(8,128)}, u32[]{:S(2)}) copy-start(f32[237,400]{0,1:T(8,128)} %param.10) | copy-start | bytes 1137604
  141.2 57.5 %copy-start.1 = (f32[512]{0:T(512)S(1)}, f32[512]{0:T(512)}, u32[]{:S(2)}) copy-start(f32[512]{0:T(512)} %param.9) | copy-start | bytes 6148
Sparse Core Ops, SparseCore 0:
  137.9 41.4 reduce-scatter.3

commit v7 on v6

--- a/solution.py
+++ b/solution.py
@@ -265,6 +265,22 @@
     )(*args)
 
 
+def scatter_over_chips(blocks):
+    reps = blocks.shape[0]
+    chips = reps // 2
+    me = lax.axis_index("rep")
+    chip, core = me >> 1, me & 1
+    pairs = blocks.reshape(chips, 2, *blocks.shape[1:])
+    given = lax.dynamic_index_in_dim(pairs, 1 - core, 1, keepdims=False)
+    kept = lax.dynamic_index_in_dim(pairs, core, 1, keepdims=False)
+    kept = kept + lax.ppermute(given, "rep", [(i, i ^ 1) for i in range(reps)])
+    total = lax.dynamic_index_in_dim(kept, chip, 0, keepdims=False)
+    for step in range(1, chips):
+        given = lax.dynamic_index_in_dim(kept, (chip + step) & (chips - 1), 0, keepdims=False)
+        total = total + lax.ppermute(given, "rep", [(i, (i + 2 * step) % reps) for i in range(reps)])
+    return total
+
+
 def per_device(entity, adagrad_state, relation, src_rows, dst_rows, rel_ids, bucket_counts, noise_rows):
     nh, nl, ny, reps = (lax.axis_size(name) for name in ("h", "l", "y", "rep"))
     near = ("l", "y", "rep")
@@ -324,9 +340,9 @@
     (source,) = call(
         functools.partial(source_kernel, ny, reps), floats((reps * packed, 128)), *edge_args, flops=13 * unit
     )
-    grad = lax.psum_scatter(partial, "h", scatter_dimension=0)
-    shares = lax.all_to_all(source.reshape(reps, packed, 128), "rep", split_axis=0, concat_axis=0, tiled=True)
-    summed = lax.all_gather(grad + jnp.sum(shares, axis=0), "rep").reshape(reps * packed, 128)
+    partial = lax.all_to_all(partial, "h", split_axis=0, concat_axis=0, tiled=True)
+    grad = jnp.sum(partial, axis=0) + scatter_over_chips(source.reshape(reps, packed, 128))
+    summed = lax.all_gather(grad, "rep").reshape(reps * packed, 128)
     new_entity, new_state = call(
         functools.partial(update_kernel, reps),
         floats((features, rows), (1, rows)),

time: 207 us -> 200 us (0.966)
  the two profiles are of different devices: /device:TPU:1 before, /device:TPU:33 now
where the time goes in v7:
time: 200 us
  blocking collectives  113 us (56%)
  starting transfers between devices  29.7 us (15%)
  waiting for transfers between devices  28.1 us (14%)
  Pallas kernels  24.4 us (12%)
  local copies, waits for them, and re-layouts  2.61 us (1%)
    all_to_all x1, blocking collectives, per_device(): lax.all_to_all(found.reshape(wire), near, split_axis=0, concat_axis=0, ti...  37.4 us
    all_gather x1, blocking collectives, per_device(): lax.all_gather(mine.reshape(packed, 128), 'h').reshape(nh * packed, 128)  32.4 us
    all_to_all x1, blocking collectives, per_device(): lax.all_to_all(terms.reshape(wire), near, split_axis=0, concat_axis=0, ti...  29 us
    all_to_all x1, waiting for transfers between devices, per_device(): lax.all_to_all(partial, 'h', split_axis=0, concat_axis=0, tiled=True)  26.7 us
    pallas_call x6, Pallas kernels, call(): pl.pallas_call(kernel, out_shape=shapes, in_specs=[pl.BlockSpec(memory_sp...  24.4 us
    all_gather x1, blocking collectives, per_device(): summed = lax.all_gather(grad, 'rep').reshape(reps * packed, 128)  13.9 us
    all_to_all x1, starting transfers between devices, per_device(): lax.all_to_all(wanted, near, split_axis=0, concat_axis=0, tiled=True)  10 us
    ppermute x3, starting transfers between devices, scatter_over_chips(): lax.ppermute(given, 'rep', [(i, (i + 2 * step) % reps) for i in range(rep...  9.24 us
  transfers between devices with their start and end apart: 6, of which 2 were waited for; matrix products, arithmetic and copies ran while one was open for 1% of the time, Pallas kernels for 2%

profile of v7, /device:TPU:33, one launch (start us, length us, event | category | flops | bytes accessed | tf_op | source)
XLA Modules:
  0.0 199.7 jit_solution(17899406167885577548)
XLA Ops:
  0.6 1.7 shard_map.95
  2.3 10.0 %all-to-all-start = ((s32[64,1,128]{2,1,0:T(1,128)}), s32[64,1,128]{2,1,0:T(1,128)S(1)}, u32[]{:S(2)}, u32[]{:S(2)}) async-start(s32[64,1,128]{2,1,0:T(1,128)} %bitcast.11), calls=%async_computation | async-start | bytes 65536 | tf_op jit(solution)/shard_map/all_to_all | solution.py:311
  12.4 0.9 dynamic-slice_bitcast_fusion.1
  13.3 32.4 %all_gather.9 = f32[8,200,128]{2,1,0:T(8,128)S(1)} all-gather(f32[1,200,128]{2,1,0:T(8,128)S(1)} %all_gather_reshape.3), channel_id=1, replica_groups=mesh['h'=8,'l'=2,'y'=4,'rep'=8] {'h'}, dimensions={0}, use_global_device_ids=true | all-gather | bytes 921600 | tf_op jit(solution)/shard_map/all_gather | solution.py:296
  45.8 0.0 all-to-all-done
  45.8 0.1 copy.16
  45.9 0.2 copy.17
  46.1 0.3 reshape.69.ids_ref
  46.4 7.0 %shard_map.96 = f32[3200,128]{1,0:T(8,128)S(1)} custom-call(f32[1600,128]{1,0:T(8,128)S(1)} %bitcast.58, s32[8,1,1024]{2,1,0:T(1,128)S(1)} %reshape.69.ids_ref), custom_call_target="tpu_custom_call" | custom-call | flops 1677721600 | bytes 2490368 | tf_op jit(solution)/shard_map/pallas_call | solution.py:257
  53.4 0.0 copy-start
  53.5 0.0 copy-start.2
  53.5 37.4 %all_to_all.24 = f32[64,25,2,128]{3,2,1,0:T(2,128)S(1)} all-to-all(f32[64,25,2,128]{3,2,1,0:T(2,128)S(1)} %bitcast.53), channel_id=1, replica_groups=mesh['h'=8,'l'=2,'y'=4,'rep'=8] {'l','y','rep'}, dimensions={0} | all-to-all | bytes 3276800 | tf_op jit(solution)/shard_map/all_to_all | solution.py:328
  90.8 0.0 copy-done
  90.8 0.0 copy-done.2
  90.8 3.1 %shard_map.97 = f32[3200,128]{1,0:T(8,128)S(1)} custom-call(f32[3200,128]{1,0:T(8,128)S(1)} %bitcast.50, f32[400,512]{1,0:T(8,128)S(1)} %bitcast.55, f32[400,237]{1,0:T(8,128)S(1)} %bitcast.62, s32[1,512]{1,0:T(1,128)S(1)} %get-tuple-element.9.src_ref, s32[1,512]{1,0:T(1,128)S(1)} %get-tuple-element.10.rel_ref, f32[1,512]{1,0:T(1,128)S(1)} %get-tuple-element.11.live_ref), custom_call_target="tpu_custom_call" | custom-call | flops 2306867200 | bytes 4481344 | tf_op jit(solution)/shard_map/pallas_call | solution.py:257
  93.9 29.0 %all_to_all.25 = f32[64,25,2,128]{3,2,1,0:T(2,128)S(1)} all-to-all(f32[64,25,2,128]{3,2,1,0:T(2,128)S(1)} %bitcast.54), channel_id=1, replica_groups=mesh['h'=8,'l'=2,'y'=4,'rep'=8] {'l','y','rep'}, dimensions={0} | all-to-all | bytes 3276800 | tf_op jit(solution)/shard_map/all_to_all | solution.py:331
  123.0 8.0 %shard_map.98 = f32[8,200,128]{2,1,0:T(8,128)} custom-call(f32[3200,128]{1,0:T(8,128)S(1)} %bitcast.52, s32[8,1,1024]{2,1,0:T(1,128)S(1)} %reshape.69.ids_ref), custom_call_target="tpu_custom_call" | custom-call | flops 1677721600 | bytes 2490368 | tf_op jit(solution)/shard_map/pallas_call | solution.py:257
  130.9 7.7 %all-to-all-start.3 = ((f32[8,200,128]{2,1,0:T(8,128)}), f32[8,200,128]{2,1,0:T(8,128)}, u32[]{:S(2)}, u32[]{:S(2)}) async-start(f32[8,200,128]{2,1,0:T(8,128)} %shard_map.98), calls=%async_computation.3 | async-start | bytes 1638400 | tf_op jit(solution)/shard_map/all_to_all | solution.py:343
  138.6 0.0 copy-start.3
  138.6 1.0 copy-done.3
  139.6 3.5 %shard_map.99 = f32[1600,128]{1,0:T(8,128)S(1)} custom-call(f32[3200,128]{1,0:T(8,128)S(1)} %bitcast.51, f32[400,512]{1,0:T(8,128)S(1)} %bitcast.56, f32[400,237]{1,0:T(8,128)S(1)} %bitcast.63, s32[1,512]{1,0:T(1,128)S(1)} %get-tuple-element.9.src_ref, s32[1,512]{1,0:T(1,128)S(1)} %get-tuple-element.10.rel_ref, f32[1,512]{1,0:T(1,128)S(1)} %get-tuple-element.11.live_ref), custom_call_target="tpu_custom_call" | custom-call | flops 2726297600 | bytes 3662144 | tf_op jit(solution)/shard_map/pallas_call | solution.py:257
  143.2 2.8 %collective-permute-start = (f32[4,200,128]{2,1,0:T(8,128)S(1)}, f32[4,200,128]{2,1,0:T(8,128)S(1)}, u32[]{:S(2)}, u32[]{:S(2)}) collective-permute-start(f32[4,200,128]{2,1,0:T(8,128)S(1)} %dynamic-slice_bitcast_fusion), channel_id=1, source_target_pairs={{0,1},{1,0},{2,3},{3,2},{4,5},{5,4},{6,7},{7,6},{8,9},{9,8},{10,11... | collective-permute-start | bytes 1228808 | tf_op jit(solution)/shard_map/ppermute | solution.py:276
  146.0 1.3 collective-permute-done
  147.3 0.1 bitcast_add_fusion
  147.4 0.0 copy-start.1
  147.4 2.3 %collective-permute-start.1 = (f32[200,128]{1,0:T(8,128)S(1)}, f32[200,128]{1,0:T(8,128)S(1)}, u32[]{:S(2)}, u32[]{:S(2)}) collective-permute-start(f32[200,128]{1,0:T(8,128)S(1)} %get-tuple-element.14), channel_id=1, source_target_pairs={{0,2},{1,3},{2,4},{3,5},{4,6},{5,7},{6,0},{7,1},{8,10},{9,11},{10,... | collective-permute-start | bytes 307208 | tf_op jit(solution)/shard_map/ppermute | solution.py:280
  149.7 3.8 %collective-permute-start.2 = (f32[200,128]{1,0:T(8,128)S(1)}, f32[200,128]{1,0:T(8,128)S(1)}, u32[]{:S(2)}, u32[]{:S(2)}) collective-permute-start(f32[200,128]{1,0:T(8,128)S(1)} %get-tuple-element.16), channel_id=1, source_target_pairs={{0,4},{1,5},{2,6},{3,7},{4,0},{5,1},{6,2},{7,3},{8,12},{9,13},{10,... | collective-permute-start | bytes 307208 | tf_op jit(solution)/shard_map/ppermute | solution.py:280
  153.5 3.1 %collective-permute-start.3 = (f32[200,128]{1,0:T(8,128)S(1)}, f32[200,128]{1,0:T(8,128)S(1)}, u32[]{:S(2)}, u32[]{:S(2)}) collective-permute-start(f32[200,128]{1,0:T(8,128)S(1)} %get-tuple-element.15), channel_id=1, source_target_pairs={{0,6},{1,7},{2,0},{3,1},{4,2},{5,3},{6,4},{7,5},{8,14},{9,15},{10,... | collective-permute-start | bytes 307208 | tf_op jit(solution)/shard_map/ppermute | solution.py:280
  156.7 26.7 %all-to-all-done.3 = f32[8,200,128]{2,1,0:T(8,128)} async-done(((f32[8,200,128]{2,1,0:T(8,128)}), f32[8,200,128]{2,1,0:T(8,128)}, u32[]{:S(2)}, u32[]{:S(2)}) %all-to-all-start.3) | async-done | bytes 819232 | tf_op jit(solution)/shard_map/all_to_all | solution.py:343
  183.4 1.2 reduce_sum.9
  184.6 0.0 collective-permute-done.1
  184.6 0.0 collective-permute-done.2
  184.6 0.0 collective-permute-done.3
  184.6 13.9 %all-gather.grad_ref = f32[1600,128]{1,0:T(8,128)S(1)} all-gather(f32[200,128]{1,0:T(8,128)S(1)} %fusion.2), channel_id=2, replica_groups=mesh['h'=8,'l'=2,'y'=4,'rep'=8] {'rep'}, dimensions={0}, use_global_device_ids=true | all-gather | bytes 921600 | tf_op jit(solution)/shard_map/all_gather | solution.py:345
  198.6 0.0 copy-done.1
  198.6 1.2 shard_map.100
  (4 shorter events, 0.1 us)
Async XLA Ops:
  2.3 43.5 %all-to-all-start = ((s32[64,1,128]{2,1,0:T(1,128)}), s32[64,1,128]{2,1,0:T(1,128)S(1)}, u32[]{:S(2)}, u32[]{:S(2)}) async-start(s32[64,1,128]{2,1,0:T(1,128)} %bitcast.11), calls=%async_computation | async-start | bytes 65536 | tf_op jit(solution)/shard_map/all_to_all | solution.py:311
  53.4 37.4 %copy-start = (f32[512,400]{0,1:T(8,128)S(1)}, f32[512,400]{0,1:T(8,128)}, u32[]{:S(2)}) copy-start(f32[512,400]{0,1:T(8,128)} %param.8) | copy-start | bytes 2457604
  53.5 37.4 %copy-start.2 = (f32[237,400]{0,1:T(8,128)S(1)}, f32[237,400]{0,1:T(8,128)}, u32[]{:S(2)}) copy-start(f32[237,400]{0,1:T(8,128)} %param.10) | copy-start | bytes 1137604
  130.9 52.4 %all-to-all-start.3 = ((f32[8,200,128]{2,1,0:T(8,128)}), f32[8,200,128]{2,1,0:T(8,128)}, u32[]{:S(2)}, u32[]{:S(2)}) async-start(f32[8,200,128]{2,1,0:T(8,128)} %shard_map.98), calls=%async_computation.3 | async-start | bytes 1638400 | tf_op jit(solution)/shard_map/all_to_all | solution.py:343
  138.6 1.0 copy-start.3
  143.2 4.1 %collective-permute-start = (f32[4,200,128]{2,1,0:T(8,128)S(1)}, f32[4,200,128]{2,1,0:T(8,128)S(1)}, u32[]{:S(2)}, u32[]{:S(2)}) collective-permute-start(f32[4,200,128]{2,1,0:T(8,128)S(1)} %dynamic-slice_bitcast_fusion), channel_id=1, source_target_pairs={{0,1},{1,0},{2,3},{3,2},{4,5},{5,4},{6,7},{7,6},{8,9},{9,8},{10,11... | collective-permute-start | bytes 1228808 | tf_op jit(solution)/shard_map/ppermute | solution.py:276
  147.4 51.2 %copy-start.1 = (f32[512]{0:T(512)S(1)}, f32[512]{0:T(512)}, u32[]{:S(2)}) copy-start(f32[512]{0:T(512)} %param.9) | copy-start | bytes 6148
  147.4 37.2 %collective-permute-start.1 = (f32[200,128]{1,0:T(8,128)S(1)}, f32[200,128]{1,0:T(8,128)S(1)}, u32[]{:S(2)}, u32[]{:S(2)}) collective-permute-start(f32[200,128]{1,0:T(8,128)S(1)} %get-tuple-element.14), channel_id=1, source_target_pairs={{0,2},{1,3},{2,4},{3,5},{4,6},{5,7},{6,0},{7,1},{8,10},{9,11},{10,... | collective-permute-start | bytes 307208 | tf_op jit(solution)/shard_map/ppermute | solution.py:280
  149.7 34.9 %collective-permute-start.2 = (f32[200,128]{1,0:T(8,128)S(1)}, f32[200,128]{1,0:T(8,128)S(1)}, u32[]{:S(2)}, u32[]{:S(2)}) collective-permute-start(f32[200,128]{1,0:T(8,128)S(1)} %get-tuple-element.16), channel_id=1, source_target_pairs={{0,4},{1,5},{2,6},{3,7},{4,0},{5,1},{6,2},{7,3},{8,12},{9,13},{10,... | collective-permute-start | bytes 307208 | tf_op jit(solution)/shard_map/ppermute | solution.py:280
  153.5 31.1 %collective-permute-start.3 = (f32[200,128]{1,0:T(8,128)S(1)}, f32[200,128]{1,0:T(8,128)S(1)}, u32[]{:S(2)}, u32[]{:S(2)}) collective-permute-start(f32[200,128]{1,0:T(8,128)S(1)} %get-tuple-element.15), channel_id=1, source_target_pairs={{0,6},{1,7},{2,0},{3,1},{4,2},{5,3},{6,4},{7,5},{8,14},{9,15},{10,... | collective-permute-start | bytes 307208 | tf_op jit(solution)/shard_map/ppermute | solution.py:280

commit v8 on v7

--- a/solution.py
+++ b/solution.py
@@ -51,20 +51,26 @@
     return mul(a_low, b_high, dims) + mul(a_high, b_low, dims) + mul(a_high, b_high, dims)
 
 
-def swap_blocks(v, slots, lane):
-    n, span = len(v), v[0].shape[1]
-    k = n // 2
-    while k:
-        low = (lane & k) == 0
-        w = list(v)
-        for i in range(n):
-            if not i & k:
-                a, b = v[i], v[i + k]
-                w[i] = jnp.where(low, a, pltpu.roll(b, k * slots, 1))
-                w[i + k] = jnp.where(low, pltpu.roll(a, span - k * slots, 1), b)
-        v = w
-        k //= 2
-    return v
+def skewed(v, block):
+    n = len(v)
+    k = 1
+    while k < n:
+        high = (block & k) != 0
+        v = [jnp.where(high, v[(i + k) % n], v[i]) for i in range(n)]
+        k *= 2
+    return [v[-i % n] for i in range(n)]
+
+
+def rotated(row, blocks, span, slots):
+    parts = [row[:, i * span : (i + 1) * span] for i in range(row.shape[1] // span)]
+    parts = [pltpu.roll(part, shift * slots, 1) if shift else part for part, shift in zip(parts, blocks)]
+    return jnp.concatenate(parts, axis=1)
+
+
+def turned_ids(ids_ref, h, nh, span, slots):
+    row = ids_ref[h]
+    each = row.shape[1] // (2 * span)
+    return rotated(row, [kind * nh + h for kind in range(2) for _ in range(each)], span, slots)
 
 
 def order_kernel(nh, nl, ny, *refs):
@@ -133,9 +139,9 @@
             rows = table_ref[pl.ds(h * tiles * fs + t, fs, stride=tiles), :]
             for i, part in enumerate(split(rows, terms)):
                 stack_ref[i * held : i * held + fs, t * 128 : (t + 1) * 128] = part.astype(F32)
-        found = mul(stack_ref[...].astype(BF16), one_hot(ids_ref[h], tiles * 128))
+        found = mul(stack_ref[...].astype(BF16), one_hot(turned_ids(ids_ref, h, nh, span, slots), tiles * 128))
         got_ref[h] = sum(found[i * held : (i + 1) * held] for i in range(terms - 1, -1, -1))
-    lane = lax.broadcasted_iota(jnp.int32, (8, span), 1) // slots
+    block = lax.broadcasted_iota(jnp.int32, (8, span), 1) // slots
 
     def turn(tile, carry):
         for f in chunks(fs):
@@ -143,9 +149,9 @@
             for kind in range(2):
                 start = pl.multiple_of((kind * devices + tile * n) * slots, span)
                 v += [got_ref[h, f : f + 8, pl.ds(start, span)] for h in range(nh)]
-            v = swap_blocks(v, slots, lane)
+            v = skewed(v, block)
             for i in range(n):
-                out_ref[pl.ds((tile * n + i) * fs + f, 8), :] = v[i]
+                out_ref[pl.ds((tile * n + i) * fs + f, 8), :] = pltpu.roll(v[i], (n - i) % n * slots, 1) if i else v[i]
         return carry
 
     lax.fori_loop(0, devices // n, turn, 0)
@@ -158,11 +164,12 @@
     tiles = out_ref.shape[1] // fs
     n = 2 * nh
     slots = span // n
-    lane = lax.broadcasted_iota(jnp.int32, (8, span), 1) // slots
+    block = lax.broadcasted_iota(jnp.int32, (8, span), 1) // slots
 
     def turn(tile, carry):
         for f in chunks(fs):
-            v = swap_blocks([msg_ref[pl.ds((tile * n + i) * fs + f, 8), :] for i in range(n)], slots, lane)
+            v = [msg_ref[pl.ds((tile * n + i) * fs + f, 8), :] for i in range(n)]
+            v = skewed([pltpu.roll(v[i], i * slots, 1) if i else v[i] for i in range(n)], block)
             for kind in range(2):
                 start = pl.multiple_of((kind * devices + tile * n) * slots, span)
                 for h in range(nh):
@@ -173,7 +180,7 @@
 
     copies = []
     for h in range(nh):
-        grad = pick(got_ref[h], one_hot(ids_ref[h], tiles * 128), NT, 2)
+        grad = pick(got_ref[h], one_hot(turned_ids(ids_ref, h, nh, span, slots), tiles * 128), NT, 2)
         for t in range(tiles):
             sum_ref[h, t * fs : (t + 1) * fs] = grad[:fs, t * 128 : (t + 1) * 128]
         copies.append(pltpu.make_async_copy(sum_ref.at[h], out_ref.at[h], sems.at[h]))

time: 200 us -> 193 us (0.965)
  Pallas kernels: 24.4 us -> 17 us
    pallas_call x6, Pallas kernels: 24.4 us -> 17 us  [call(): pl.pallas_call(kernel, out_shape=shapes, in_specs=[pl.BlockSpec(memory_sp...]
where the time goes in v8:
time: 193 us; the launch traced here: 192 us
  blocking collectives  113 us (59%)
  starting transfers between devices  29.7 us (15%)
  waiting for transfers between devices  28 us (15%)
  Pallas kernels  17 us (9%)
  local copies, waits for them, and re-layouts  2.61 us (1%)
    all_to_all x1, blocking collectives, per_device(): lax.all_to_all(found.reshape(wire), near, split_axis=0, concat_axis=0, ti...  37.4 us
    all_gather x1, blocking collectives, per_device(): lax.all_gather(mine.reshape(packed, 128), 'h').reshape(nh * packed, 128)  32.4 us
    all_to_all x1, blocking collectives, per_device(): lax.all_to_all(terms.reshape(wire), near, split_axis=0, concat_axis=0, ti...  29 us
    all_to_all x1, waiting for transfers between devices, per_device(): lax.all_to_all(partial, 'h', split_axis=0, concat_axis=0, tiled=True)  26.7 us
    pallas_call x6, Pallas kernels, call(): pl.pallas_call(kernel, out_shape=shapes, in_specs=[pl.BlockSpec(memory_sp...  17 us
    all_gather x1, blocking collectives, per_device(): summed = lax.all_gather(grad, 'rep').reshape(reps * packed, 128)  13.9 us
    all_to_all x1, starting transfers between devices, per_device(): lax.all_to_all(wanted, near, split_axis=0, concat_axis=0, tiled=True)  10 us
    ppermute x3, starting transfers between devices, scatter_over_chips(): lax.ppermute(given, 'rep', [(i, (i + 2 * step) % reps) for i in range(rep...  9.24 us
  transfers between devices with their start and end apart: 6, of which 2 were waited for; matrix products, arithmetic and copies ran while one was open for 1% of the time, Pallas kernels for 2%

profile of v8, /device:TPU:33, one launch (start us, length us, event | category | flops | bytes accessed | tf_op | source)
XLA Modules:
  0.0 192.4 jit_solution(17508168929768884909)
XLA Ops:
  0.6 1.7 shard_map.95
  2.3 10.0 %all-to-all-start = ((s32[64,1,128]{2,1,0:T(1,128)}), s32[64,1,128]{2,1,0:T(1,128)S(1)}, u32[]{:S(2)}, u32[]{:S(2)}) async-start(s32[64,1,128]{2,1,0:T(1,128)} %bitcast.11), calls=%async_computation | async-start | bytes 65536 | tf_op jit(solution)/shard_map/all_to_all | solution.py:318
  12.4 0.9 dynamic-slice_bitcast_fusion.1
  13.3 32.4 %all_gather.9 = f32[8,200,128]{2,1,0:T(8,128)S(1)} all-gather(f32[1,200,128]{2,1,0:T(8,128)S(1)} %all_gather_reshape.3), channel_id=1, replica_groups=mesh['h'=8,'l'=2,'y'=4,'rep'=8] {'h'}, dimensions={0}, use_global_device_ids=true | all-gather | bytes 921600 | tf_op jit(solution)/shard_map/all_gather | solution.py:303
  45.8 0.0 all-to-all-done
  45.8 0.1 copy.16
  45.9 0.2 copy.17
  46.1 0.3 reshape.69.ids_ref
  46.4 3.3 %shard_map.96 = f32[3200,128]{1,0:T(8,128)S(1)} custom-call(f32[1600,128]{1,0:T(8,128)S(1)} %bitcast.58, s32[8,1,1024]{2,1,0:T(1,128)S(1)} %reshape.69.ids_ref), custom_call_target="tpu_custom_call" | custom-call | flops 1677721600 | bytes 2490368 | tf_op jit(solution)/shard_map/pallas_call | solution.py:264
  49.7 0.0 copy-start
  49.7 0.0 copy-start.2
  49.7 37.4 %all_to_all.24 = f32[64,25,2,128]{3,2,1,0:T(2,128)S(1)} all-to-all(f32[64,25,2,128]{3,2,1,0:T(2,128)S(1)} %bitcast.53), channel_id=1, replica_groups=mesh['h'=8,'l'=2,'y'=4,'rep'=8] {'l','y','rep'}, dimensions={0} | all-to-all | bytes 3276800 | tf_op jit(solution)/shard_map/all_to_all | solution.py:335
  87.1 0.0 copy-done
  87.1 0.0 copy-done.2
  87.1 3.1 %shard_map.97 = f32[3200,128]{1,0:T(8,128)S(1)} custom-call(f32[3200,128]{1,0:T(8,128)S(1)} %bitcast.50, f32[400,512]{1,0:T(8,128)S(1)} %bitcast.55, f32[400,237]{1,0:T(8,128)S(1)} %bitcast.62, s32[1,512]{1,0:T(1,128)S(1)} %get-tuple-element.9.src_ref, s32[1,512]{1,0:T(1,128)S(1)} %get-tuple-element.10.rel_ref, f32[1,512]{1,0:T(1,128)S(1)} %get-tuple-element.11.live_ref), custom_call_target="tpu_custom_call" | custom-call | flops 2306867200 | bytes 4481344 | tf_op jit(solution)/shard_map/pallas_call | solution.py:264
  90.1 29.0 %all_to_all.25 = f32[64,25,2,128]{3,2,1,0:T(2,128)S(1)} all-to-all(f32[64,25,2,128]{3,2,1,0:T(2,128)S(1)} %bitcast.54), channel_id=1, replica_groups=mesh['h'=8,'l'=2,'y'=4,'rep'=8] {'l','y','rep'}, dimensions={0} | all-to-all | bytes 3276800 | tf_op jit(solution)/shard_map/all_to_all | solution.py:338
  119.2 4.4 %shard_map.98 = f32[8,200,128]{2,1,0:T(8,128)} custom-call(f32[3200,128]{1,0:T(8,128)S(1)} %bitcast.52, s32[8,1,1024]{2,1,0:T(1,128)S(1)} %reshape.69.ids_ref), custom_call_target="tpu_custom_call" | custom-call | flops 1677721600 | bytes 2490368 | tf_op jit(solution)/shard_map/pallas_call | solution.py:264
  123.6 7.7 %all-to-all-start.3 = ((f32[8,200,128]{2,1,0:T(8,128)}), f32[8,200,128]{2,1,0:T(8,128)}, u32[]{:S(2)}, u32[]{:S(2)}) async-start(f32[8,200,128]{2,1,0:T(8,128)} %shard_map.98), calls=%async_computation.3 | async-start | bytes 1638400 | tf_op jit(solution)/shard_map/all_to_all | solution.py:350
  131.2 0.0 copy-start.3
  131.3 1.0 copy-done.3
  132.2 3.5 %shard_map.99 = f32[1600,128]{1,0:T(8,128)S(1)} custom-call(f32[3200,128]{1,0:T(8,128)S(1)} %bitcast.51, f32[400,512]{1,0:T(8,128)S(1)} %bitcast.56, f32[400,237]{1,0:T(8,128)S(1)} %bitcast.63, s32[1,512]{1,0:T(1,128)S(1)} %get-tuple-element.9.src_ref, s32[1,512]{1,0:T(1,128)S(1)} %get-tuple-element.10.rel_ref, f32[1,512]{1,0:T(1,128)S(1)} %get-tuple-element.11.live_ref), custom_call_target="tpu_custom_call" | custom-call | flops 2726297600 | bytes 3662144 | tf_op jit(solution)/shard_map/pallas_call | solution.py:264
  135.8 2.8 %collective-permute-start = (f32[4,200,128]{2,1,0:T(8,128)S(1)}, f32[4,200,128]{2,1,0:T(8,128)S(1)}, u32[]{:S(2)}, u32[]{:S(2)}) collective-permute-start(f32[4,200,128]{2,1,0:T(8,128)S(1)} %dynamic-slice_bitcast_fusion), channel_id=1, source_target_pairs={{0,1},{1,0},{2,3},{3,2},{4,5},{5,4},{6,7},{7,6},{8,9},{9,8},{10,11... | collective-permute-start | bytes 1228808 | tf_op jit(solution)/shard_map/ppermute | solution.py:283
  138.6 1.3 collective-permute-done
  139.9 0.1 bitcast_add_fusion
  140.0 0.0 copy-start.1
  140.0 2.2 %collective-permute-start.1 = (f32[200,128]{1,0:T(8,128)S(1)}, f32[200,128]{1,0:T(8,128)S(1)}, u32[]{:S(2)}, u32[]{:S(2)}) collective-permute-start(f32[200,128]{1,0:T(8,128)S(1)} %get-tuple-element.14), channel_id=1, source_target_pairs={{0,2},{1,3},{2,4},{3,5},{4,6},{5,7},{6,0},{7,1},{8,10},{9,11},{10,... | collective-permute-start | bytes 307208 | tf_op jit(solution)/shard_map/ppermute | solution.py:287
  142.3 3.8 %collective-permute-start.2 = (f32[200,128]{1,0:T(8,128)S(1)}, f32[200,128]{1,0:T(8,128)S(1)}, u32[]{:S(2)}, u32[]{:S(2)}) collective-permute-start(f32[200,128]{1,0:T(8,128)S(1)} %get-tuple-element.16), channel_id=1, source_target_pairs={{0,4},{1,5},{2,6},{3,7},{4,0},{5,1},{6,2},{7,3},{8,12},{9,13},{10,... | collective-permute-start | bytes 307208 | tf_op jit(solution)/shard_map/ppermute | solution.py:287
  146.1 3.1 %collective-permute-start.3 = (f32[200,128]{1,0:T(8,128)S(1)}, f32[200,128]{1,0:T(8,128)S(1)}, u32[]{:S(2)}, u32[]{:S(2)}) collective-permute-start(f32[200,128]{1,0:T(8,128)S(1)} %get-tuple-element.15), channel_id=1, source_target_pairs={{0,6},{1,7},{2,0},{3,1},{4,2},{5,3},{6,4},{7,5},{8,14},{9,15},{10,... | collective-permute-start | bytes 307208 | tf_op jit(solution)/shard_map/ppermute | solution.py:287
  149.3 26.7 %all-to-all-done.3 = f32[8,200,128]{2,1,0:T(8,128)} async-done(((f32[8,200,128]{2,1,0:T(8,128)}), f32[8,200,128]{2,1,0:T(8,128)}, u32[]{:S(2)}, u32[]{:S(2)}) %all-to-all-start.3) | async-done | bytes 819232 | tf_op jit(solution)/shard_map/all_to_all | solution.py:350
  176.0 1.2 reduce_sum.9
  177.2 0.0 collective-permute-done.1
  177.2 0.0 collective-permute-done.2
  177.2 0.0 collective-permute-done.3
  177.3 13.9 %all-gather.grad_ref = f32[1600,128]{1,0:T(8,128)S(1)} all-gather(f32[200,128]{1,0:T(8,128)S(1)} %fusion.2), channel_id=2, replica_groups=mesh['h'=8,'l'=2,'y'=4,'rep'=8] {'rep'}, dimensions={0}, use_global_device_ids=true | all-gather | bytes 921600 | tf_op jit(solution)/shard_map/all_gather | solution.py:352
  191.2 0.0 copy-done.1
  191.2 1.2 shard_map.100
  (4 shorter events, 0.1 us)
Async XLA Ops:
  2.3 43.5 %all-to-all-start = ((s32[64,1,128]{2,1,0:T(1,128)}), s32[64,1,128]{2,1,0:T(1,128)S(1)}, u32[]{:S(2)}, u32[]{:S(2)}) async-start(s32[64,1,128]{2,1,0:T(1,128)} %bitcast.11), calls=%async_computation | async-start | bytes 65536 | tf_op jit(solution)/shard_map/all_to_all | solution.py:318
  49.7 37.4 %copy-start = (f32[512,400]{0,1:T(8,128)S(1)}, f32[512,400]{0,1:T(8,128)}, u32[]{:S(2)}) copy-start(f32[512,400]{0,1:T(8,128)} %param.8) | copy-start | bytes 2457604
  49.7 37.4 %copy-start.2 = (f32[237,400]{0,1:T(8,128)S(1)}, f32[237,400]{0,1:T(8,128)}, u32[]{:S(2)}) copy-start(f32[237,400]{0,1:T(8,128)} %param.10) | copy-start | bytes 1137604
  123.6 52.4 %all-to-all-start.3 = ((f32[8,200,128]{2,1,0:T(8,128)}), f32[8,200,128]{2,1,0:T(8,128)}, u32[]{:S(2)}, u32[]{:S(2)}) async-start(f32[8,200,128]{2,1,0:T(8,128)} %shard_map.98), calls=%async_computation.3 | async-start | bytes 1638400 | tf_op jit(solution)/shard_map/all_to_all | solution.py:350
  131.2 1.0 copy-start.3
  135.8 4.1 %collective-permute-start = (f32[4,200,128]{2,1,0:T(8,128)S(1)}, f32[4,200,128]{2,1,0:T(8,128)S(1)}, u32[]{:S(2)}, u32[]{:S(2)}) collective-permute-start(f32[4,200,128]{2,1,0:T(8,128)S(1)} %dynamic-slice_bitcast_fusion), channel_id=1, source_target_pairs={{0,1},{1,0},{2,3},{3,2},{4,5},{5,4},{6,7},{7,6},{8,9},{9,8},{10,11... | collective-permute-start | bytes 1228808 | tf_op jit(solution)/shard_map/ppermute | solution.py:283
  140.0 51.2 %copy-start.1 = (f32[512]{0:T(512)S(1)}, f32[512]{0:T(512)}, u32[]{:S(2)}) copy-start(f32[512]{0:T(512)} %param.9) | copy-start | bytes 6148
  140.0 37.2 %collective-permute-start.1 = (f32[200,128]{1,0:T(8,128)S(1)}, f32[200,128]{1,0:T(8,128)S(1)}, u32[]{:S(2)}, u32[]{:S(2)}) collective-permute-start(f32[200,128]{1,0:T(8,128)S(1)} %get-tuple-element.14), channel_id=1, source_target_pairs={{0,2},{1,3},{2,4},{3,5},{4,6},{5,7},{6,0},{7,1},{8,10},{9,11},{10,... | collective-permute-start | bytes 307208 | tf_op jit(solution)/shard_map/ppermute | solution.py:287
  142.3 34.9 %collective-permute-start.2 = (f32[200,128]{1,0:T(8,128)S(1)}, f32[200,128]{1,0:T(8,128)S(1)}, u32[]{:S(2)}, u32[]{:S(2)}) collective-permute-start(f32[200,128]{1,0:T(8,128)S(1)} %get-tuple-element.16), channel_id=1, source_target_pairs={{0,4},{1,5},{2,6},{3,7},{4,0},{5,1},{6,2},{7,3},{8,12},{9,13},{10,... | collective-permute-start | bytes 307208 | tf_op jit(solution)/shard_map/ppermute | solution.py:287
  146.1 31.1 %collective-permute-start.3 = (f32[200,128]{1,0:T(8,128)S(1)}, f32[200,128]{1,0:T(8,128)S(1)}, u32[]{:S(2)}, u32[]{:S(2)}) collective-permute-start(f32[200,128]{1,0:T(8,128)S(1)} %get-tuple-element.15), channel_id=1, source_target_pairs={{0,6},{1,7},{2,0},{3,1},{4,2},{5,3},{6,4},{7,5},{8,14},{9,15},{10,... | collective-permute-start | bytes 307208 | tf_op jit(solution)/shard_map/ppermute | solution.py:287

commit v9 on v8

--- a/solution.py
+++ b/solution.py
@@ -85,7 +85,8 @@
     edges = parts * slots
     lane = lax.broadcasted_iota(jnp.int32, (1, edges), 1)
     slot, group = lane % slots, lane // slots
-    h, l, y = group % nh, group // nh % nl, group // (nh * nl)
+    h, g, y = group % nh, group // nh % nl, group // (nh * nl)
+    l = jnp.where(h >= nh // 2, nl - 1 - g, g)
     part = (h * nl + l) * ny + y
     here = one_hot(part, parts)
     stack = jnp.concatenate([src_ref[...], rel_ref[...], dst_ref[...]], axis=0).astype(F32)
@@ -288,9 +289,27 @@
     return total
 
 
+def groups_of(nh, nl, ny, reps):
+    def z(h, g):
+        return h * nl + (nl - 1 - g if h >= nh // 2 else g)
+
+    far = [[z(h, g) for h in range(nh)] for g in range(nl)]
+    near = [
+        [(z(h, g) * ny + y) * reps + r for g in range(nl) for y in range(ny) for r in range(reps)] for h in range(nh)
+    ]
+    return far, near
+
+
 def per_device(entity, adagrad_state, relation, src_rows, dst_rows, rel_ids, bucket_counts, noise_rows):
     nh, nl, ny, reps = (lax.axis_size(name) for name in ("h", "l", "y", "rep"))
-    near = ("l", "y", "rep")
+    far_groups, near_groups = groups_of(nh, nl, ny, reps)
+
+    def exchange(x, names, groups):
+        return lax.all_to_all(x, names, split_axis=0, concat_axis=0, axis_index_groups=groups, tiled=True)
+
+    def near(x):
+        return exchange(x, ("h", "l", "y", "rep"), near_groups)
+
     devices = nl * ny * reps
     rows, features = entity.shape
     slots = src_rows.shape[3]
@@ -300,7 +319,7 @@
 
     et = entity.T
     mine = lax.dynamic_slice_in_dim(et, lax.axis_index("rep") * fs, fs, 0)
-    table = lax.all_gather(mine.reshape(packed, 128), "h").reshape(nh * packed, 128)
+    table = lax.all_gather(mine.reshape(packed, 128), ("h", "l"), axis_index_groups=far_groups).reshape(nh * packed, 128)
 
     def turned(ids):
         return ids.reshape(nh * nl * ny, slots).T
@@ -315,7 +334,7 @@
         scratch=[pltpu.VMEM(a.shape, a.dtype) for a in given] + [pltpu.SemaphoreType.DMA((len(given),))],
         inputs=pltpu.HBM,
     )
-    asked = lax.all_to_all(wanted, near, split_axis=0, concat_axis=0, tiled=True)
+    asked = near(wanted)
     asked = asked.reshape(devices, 2, nh, slots).transpose(2, 1, 0, 3).reshape(nh, 1, -1)
     relt = relation.T
 
@@ -332,10 +351,10 @@
         scratch=[got_shape, pltpu.VMEM((3 * held, rows), F32)],
         flops=8 * unit,
     )
-    got = lax.all_to_all(found.reshape(wire), near, split_axis=0, concat_axis=0, tiled=True).reshape(message)
+    got = near(found.reshape(wire)).reshape(message)
     edge_args = (got, et, relt, src, rel, live)
     (terms,) = call(functools.partial(terms_kernel, ny), floats(message), *edge_args, flops=11 * unit)
-    terms = lax.all_to_all(terms.reshape(wire), near, split_axis=0, concat_axis=0, tiled=True).reshape(message)
+    terms = near(terms.reshape(wire)).reshape(message)
     (partial,) = call(
         functools.partial(scatter_kernel, fs),
         floats((nh, packed, 128)),
@@ -347,7 +366,7 @@
     (source,) = call(
         functools.partial(source_kernel, ny, reps), floats((reps * packed, 128)), *edge_args, flops=13 * unit
     )
-    partial = lax.all_to_all(partial, "h", split_axis=0, concat_axis=0, tiled=True)
+    partial = exchange(partial, ("h", "l"), far_groups)
     grad = jnp.sum(partial, axis=0) + scatter_over_chips(source.reshape(reps, packed, 128))
     summed = lax.all_gather(grad, "rep").reshape(reps * packed, 128)
     new_entity, new_state = call(

time: 193 us -> 194 us (level)
  the two profiles are of different devices: /device:TPU:33 before, /device:TPU:1 now
where the time goes in v9:
time: 194 us
  blocking collectives  115 us (59%)
  starting transfers between devices  30.2 us (16%)
  waiting for transfers between devices  26.4 us (14%)
  Pallas kernels  17 us (9%)
  local copies, waits for them, and re-layouts  2.61 us (1%)
    all_to_all x2, blocking collectives, exchange(): lax.all_to_all(x, names, split_axis=0, concat_axis=0, axis_index_groups=g...  67.6 us
    all_gather x1, blocking collectives, per_device(): lax.all_gather(mine.reshape(packed, 128), ('h', 'l'), axis_index_groups=f...  33 us
    all_to_all x2, waiting for transfers between devices, exchange(): lax.all_to_all(x, names, split_axis=0, concat_axis=0, axis_index_groups=g...  25.1 us
    all_to_all x2, starting transfers between devices, exchange(): lax.all_to_all(x, names, split_axis=0, concat_axis=0, axis_index_groups=g...  17.3 us
    pallas_call x6, Pallas kernels, call(): pl.pallas_call(kernel, out_shape=shapes, in_specs=[pl.BlockSpec(memory_sp...  17 us
    all_gather x1, blocking collectives, per_device(): summed = lax.all_gather(grad, 'rep').reshape(reps * packed, 128)  14.8 us
    ppermute x3, starting transfers between devices, scatter_over_chips(): lax.ppermute(given, 'rep', [(i, (i + 2 * step) % reps) for i in range(rep...  9.97 us
  transfers between devices with their start and end apart: 6, of which 2 were waited for; matrix products, arithmetic and copies ran while one was open for 1% of the time, Pallas kernels for 2%

profile of v9, /device:TPU:1, one launch (start us, length us, event | category | flops | bytes accessed | tf_op | source)
XLA Modules:
  0.0 193.8 jit_solution(2358899493734007084)
XLA Ops:
  0.6 1.7 shard_map.95
  2.3 10.9 %all-to-all-start = ((s32[64,1,128]{2,1,0:T(1,128)}), s32[64,1,128]{2,1,0:T(1,128)S(1)}, u32[]{:S(2)}, u32[]{:S(2)}) async-start(s32[64,1,128]{2,1,0:T(1,128)} %bitcast.11), calls=%async_computation | async-start | bytes 65536 | tf_op jit(solution)/shard_map/all_to_all | solution.py:308
  13.3 0.9 dynamic-slice_bitcast_fusion.1
  14.2 33.0 %all_gather.9 = f32[8,200,128]{2,1,0:T(8,128)S(1)} all-gather(f32[1,200,128]{2,1,0:T(8,128)S(1)} %all_gather_reshape.3), channel_id=1, replica_groups={{0,64,128,192,288,352,416,480},{32,96,160,224,256,320,384,448},{1,65,12..., dimensions={0}, use_global_device_ids=true | all-gather | bytes 921600 | tf_op jit(solution)/shard_map/all_gather | solution.py:322
  47.2 0.0 all-to-all-done
  47.2 0.1 copy.16
  47.3 0.2 copy.17
  47.5 0.3 reshape.69.ids_ref
  47.8 3.3 %shard_map.96 = f32[3200,128]{1,0:T(8,128)S(1)} custom-call(f32[1600,128]{1,0:T(8,128)S(1)} %bitcast.58, s32[8,1,1024]{2,1,0:T(1,128)S(1)} %reshape.69.ids_ref), custom_call_target="tpu_custom_call" | custom-call | flops 1677721600 | bytes 2490368 | tf_op jit(solution)/shard_map/pallas_call | solution.py:265
  51.1 0.0 copy-start
  51.1 0.0 copy-start.2
  51.1 38.6 %all_to_all.24 = f32[64,25,2,128]{3,2,1,0:T(2,128)S(1)} all-to-all(f32[64,25,2,128]{3,2,1,0:T(2,128)S(1)} %bitcast.53), channel_id=1, replica_groups={{0,1,2,3,4,5,6,7,8,9,10,11,12,13,14,15,16,17,18,19,20,21,22,23,24,25,26..., dimensions={0} | all-to-all | bytes 3276800 | tf_op jit(solution)/shard_map/all_to_all | solution.py:308
  89.7 0.0 copy-done
  89.7 0.0 copy-done.2
  89.7 3.1 %shard_map.97 = f32[3200,128]{1,0:T(8,128)S(1)} custom-call(f32[3200,128]{1,0:T(8,128)S(1)} %bitcast.50, f32[400,512]{1,0:T(8,128)S(1)} %bitcast.55, f32[400,237]{1,0:T(8,128)S(1)} %bitcast.62, s32[1,512]{1,0:T(1,128)S(1)} %get-tuple-element.9.src_ref, s32[1,512]{1,0:T(1,128)S(1)} %get-tuple-element.10.rel_ref, f32[1,512]{1,0:T(1,128)S(1)} %get-tuple-element.11.live_ref), custom_call_target="tpu_custom_call" | custom-call | flops 2306867200 | bytes 4481344 | tf_op jit(solution)/shard_map/pallas_call | solution.py:265
  92.8 29.0 %all_to_all.25 = f32[64,25,2,128]{3,2,1,0:T(2,128)S(1)} all-to-all(f32[64,25,2,128]{3,2,1,0:T(2,128)S(1)} %bitcast.54), channel_id=1, replica_groups={{0,1,2,3,4,5,6,7,8,9,10,11,12,13,14,15,16,17,18,19,20,21,22,23,24,25,26..., dimensions={0} | all-to-all | bytes 3276800 | tf_op jit(solution)/shard_map/all_to_all | solution.py:308
  121.8 4.4 %shard_map.98 = f32[8,200,128]{2,1,0:T(8,128)} custom-call(f32[3200,128]{1,0:T(8,128)S(1)} %bitcast.52, s32[8,1,1024]{2,1,0:T(1,128)S(1)} %reshape.69.ids_ref), custom_call_target="tpu_custom_call" | custom-call | flops 1677721600 | bytes 2490368 | tf_op jit(solution)/shard_map/pallas_call | solution.py:265
  126.2 6.4 %all-to-all-start.3 = ((f32[8,200,128]{2,1,0:T(8,128)}), f32[8,200,128]{2,1,0:T(8,128)}, u32[]{:S(2)}, u32[]{:S(2)}) async-start(f32[8,200,128]{2,1,0:T(8,128)} %shard_map.98), calls=%async_computation.3 | async-start | bytes 1638400 | tf_op jit(solution)/shard_map/all_to_all | solution.py:308
  132.6 0.0 copy-start.3
  132.6 1.0 copy-done.3
  133.6 3.5 %shard_map.99 = f32[1600,128]{1,0:T(8,128)S(1)} custom-call(f32[3200,128]{1,0:T(8,128)S(1)} %bitcast.51, f32[400,512]{1,0:T(8,128)S(1)} %bitcast.56, f32[400,237]{1,0:T(8,128)S(1)} %bitcast.63, s32[1,512]{1,0:T(1,128)S(1)} %get-tuple-element.9.src_ref, s32[1,512]{1,0:T(1,128)S(1)} %get-tuple-element.10.rel_ref, f32[1,512]{1,0:T(1,128)S(1)} %get-tuple-element.11.live_ref), custom_call_target="tpu_custom_call" | custom-call | flops 2726297600 | bytes 3662144 | tf_op jit(solution)/shard_map/pallas_call | solution.py:265
  137.1 2.9 %collective-permute-start = (f32[4,200,128]{2,1,0:T(8,128)S(1)}, f32[4,200,128]{2,1,0:T(8,128)S(1)}, u32[]{:S(2)}, u32[]{:S(2)}) collective-permute-start(f32[4,200,128]{2,1,0:T(8,128)S(1)} %dynamic-slice_bitcast_fusion), channel_id=1, source_target_pairs={{0,1},{1,0},{2,3},{3,2},{4,5},{5,4},{6,7},{7,6},{8,9},{9,8},{10,11... | collective-permute-start | bytes 1228808 | tf_op jit(solution)/shard_map/ppermute | solution.py:284
  140.0 1.3 collective-permute-done
  141.4 0.1 bitcast_add_fusion
  141.4 0.0 copy-start.1
  141.5 3.3 %collective-permute-start.1 = (f32[200,128]{1,0:T(8,128)S(1)}, f32[200,128]{1,0:T(8,128)S(1)}, u32[]{:S(2)}, u32[]{:S(2)}) collective-permute-start(f32[200,128]{1,0:T(8,128)S(1)} %get-tuple-element.14), channel_id=1, source_target_pairs={{0,2},{1,3},{2,4},{3,5},{4,6},{5,7},{6,0},{7,1},{8,10},{9,11},{10,... | collective-permute-start | bytes 307208 | tf_op jit(solution)/shard_map/ppermute | solution.py:288
  144.8 3.6 %collective-permute-start.2 = (f32[200,128]{1,0:T(8,128)S(1)}, f32[200,128]{1,0:T(8,128)S(1)}, u32[]{:S(2)}, u32[]{:S(2)}) collective-permute-start(f32[200,128]{1,0:T(8,128)S(1)} %get-tuple-element.16), channel_id=1, source_target_pairs={{0,4},{1,5},{2,6},{3,7},{4,0},{5,1},{6,2},{7,3},{8,12},{9,13},{10,... | collective-permute-start | bytes 307208 | tf_op jit(solution)/shard_map/ppermute | solution.py:288
  148.4 3.0 %collective-permute-start.3 = (f32[200,128]{1,0:T(8,128)S(1)}, f32[200,128]{1,0:T(8,128)S(1)}, u32[]{:S(2)}, u32[]{:S(2)}) collective-permute-start(f32[200,128]{1,0:T(8,128)S(1)} %get-tuple-element.15), channel_id=1, source_target_pairs={{0,6},{1,7},{2,0},{3,1},{4,2},{5,3},{6,4},{7,5},{8,14},{9,15},{10,... | collective-permute-start | bytes 307208 | tf_op jit(solution)/shard_map/ppermute | solution.py:288
  151.5 25.0 %all-to-all-done.3 = f32[8,200,128]{2,1,0:T(8,128)} async-done(((f32[8,200,128]{2,1,0:T(8,128)}), f32[8,200,128]{2,1,0:T(8,128)}, u32[]{:S(2)}, u32[]{:S(2)}) %all-to-all-start.3) | async-done | bytes 819232 | tf_op jit(solution)/shard_map/all_to_all | solution.py:308
  176.5 1.2 reduce_sum.9
  177.7 0.0 collective-permute-done.1
  177.7 0.0 collective-permute-done.2
  177.7 0.0 collective-permute-done.3
  177.8 14.8 %all-gather.grad_ref = f32[1600,128]{1,0:T(8,128)S(1)} all-gather(f32[200,128]{1,0:T(8,128)S(1)} %fusion.2), channel_id=2, replica_groups=mesh['h'=8,'l'=2,'y'=4,'rep'=8] {'rep'}, dimensions={0}, use_global_device_ids=true | all-gather | bytes 921600 | tf_op jit(solution)/shard_map/all_gather | solution.py:371
  192.6 0.0 copy-done.1
  192.6 1.2 shard_map.100
  (4 shorter events, 0.1 us)
Async XLA Ops:
  2.3 44.9 %all-to-all-start = ((s32[64,1,128]{2,1,0:T(1,128)}), s32[64,1,128]{2,1,0:T(1,128)S(1)}, u32[]{:S(2)}, u32[]{:S(2)}) async-start(s32[64,1,128]{2,1,0:T(1,128)} %bitcast.11), calls=%async_computation | async-start | bytes 65536 | tf_op jit(solution)/shard_map/all_to_all | solution.py:308
  51.1 38.6 %copy-start = (f32[512,400]{0,1:T(8,128)S(1)}, f32[512,400]{0,1:T(8,128)}, u32[]{:S(2)}) copy-start(f32[512,400]{0,1:T(8,128)} %param.8) | copy-start | bytes 2457604
  51.1 38.6 %copy-start.2 = (f32[237,400]{0,1:T(8,128)S(1)}, f32[237,400]{0,1:T(8,128)}, u32[]{:S(2)}) copy-start(f32[237,400]{0,1:T(8,128)} %param.10) | copy-start | bytes 1137604
  126.2 50.3 %all-to-all-start.3 = ((f32[8,200,128]{2,1,0:T(8,128)}), f32[8,200,128]{2,1,0:T(8,128)}, u32[]{:S(2)}, u32[]{:S(2)}) async-start(f32[8,200,128]{2,1,0:T(8,128)} %shard_map.98), calls=%async_computation.3 | async-start | bytes 1638400 | tf_op jit(solution)/shard_map/all_to_all | solution.py:308
  132.6 1.0 copy-start.3
  137.1 4.3 %collective-permute-start = (f32[4,200,128]{2,1,0:T(8,128)S(1)}, f32[4,200,128]{2,1,0:T(8,128)S(1)}, u32[]{:S(2)}, u32[]{:S(2)}) collective-permute-start(f32[4,200,128]{2,1,0:T(8,128)S(1)} %dynamic-slice_bitcast_fusion), channel_id=1, source_target_pairs={{0,1},{1,0},{2,3},{3,2},{4,5},{5,4},{6,7},{7,6},{8,9},{9,8},{10,11... | collective-permute-start | bytes 1228808 | tf_op jit(solution)/shard_map/ppermute | solution.py:284
  141.4 51.2 %copy-start.1 = (f32[512]{0:T(512)S(1)}, f32[512]{0:T(512)}, u32[]{:S(2)}) copy-start(f32[512]{0:T(512)} %param.9) | copy-start | bytes 6148
  141.5 36.2 %collective-permute-start.1 = (f32[200,128]{1,0:T(8,128)S(1)}, f32[200,128]{1,0:T(8,128)S(1)}, u32[]{:S(2)}, u32[]{:S(2)}) collective-permute-start(f32[200,128]{1,0:T(8,128)S(1)} %get-tuple-element.14), channel_id=1, source_target_pairs={{0,2},{1,3},{2,4},{3,5},{4,6},{5,7},{6,0},{7,1},{8,10},{9,11},{10,... | collective-permute-start | bytes 307208 | tf_op jit(solution)/shard_map/ppermute | solution.py:288
  144.8 32.9 %collective-permute-start.2 = (f32[200,128]{1,0:T(8,128)S(1)}, f32[200,128]{1,0:T(8,128)S(1)}, u32[]{:S(2)}, u32[]{:S(2)}) collective-permute-start(f32[200,128]{1,0:T(8,128)S(1)} %get-tuple-element.16), channel_id=1, source_target_pairs={{0,4},{1,5},{2,6},{3,7},{4,0},{5,1},{6,2},{7,3},{8,12},{9,13},{10,... | collective-permute-start | bytes 307208 | tf_op jit(solution)/shard_map/ppermute | solution.py:288
  148.4 29.3 %collective-permute-start.3 = (f32[200,128]{1,0:T(8,128)S(1)}, f32[200,128]{1,0:T(8,128)S(1)}, u32[]{:S(2)}, u32[]{:S(2)}) collective-permute-start(f32[200,128]{1,0:T(8,128)S(1)} %get-tuple-element.15), channel_id=1, source_target_pairs={{0,6},{1,7},{2,0},{3,1},{4,2},{5,3},{6,4},{7,5},{8,14},{9,15},{10,... | collective-permute-start | bytes 307208 | tf_op jit(solution)/shard_map/ppermute | solution.py:288

commit v10 on v8

--- a/solution.py
+++ b/solution.py
@@ -315,6 +315,7 @@
         scratch=[pltpu.VMEM(a.shape, a.dtype) for a in given] + [pltpu.SemaphoreType.DMA((len(given),))],
         inputs=pltpu.HBM,
     )
+    table, wanted = lax.optimization_barrier((table, wanted))
     asked = lax.all_to_all(wanted, near, split_axis=0, concat_axis=0, tiled=True)
     asked = asked.reshape(devices, 2, nh, slots).transpose(2, 1, 0, 3).reshape(nh, 1, -1)
     relt = relation.T

time: 193 us -> 195 us (1.010)
  blocking collectives: 113 us -> 126 us
  starting transfers between devices: 29.7 us -> 19.3 us
    all_to_all x0 -> x1, blocking collectives: none -> 19.8 us  [per_device(): lax.all_to_all(wanted, near, split_axis=0, concat_axis=0, tiled=True)]
    all_to_all x1 -> x0, starting transfers between devices: 10 us -> none  [per_device(): lax.all_to_all(wanted, near, split_axis=0, concat_axis=0, tiled=True)]
    all_to_all x1, blocking collectives: 37.4 us -> 29.2 us  [per_device(): lax.all_to_all(found.reshape(wire), near, split_axis=0, concat_axis=0, ti...]
  transfers between devices with their start and end apart: 6 -> 5, of which waited for: 2 -> 2; matrix products, arithmetic and copies ran while one was open for 1% -> 1% of each run, Pallas kernels for 2% -> 2%
where the time goes in v10:
time: 195 us
  blocking collectives  126 us (65%)
  waiting for transfers between devices  28 us (14%)
  starting transfers between devices  19.3 us (10%)
  Pallas kernels  16.4 us (8%)
  local copies, waits for them, and re-layouts  2.61 us (1%)
    all_gather x1, blocking collectives, per_device(): lax.all_gather(mine.reshape(packed, 128), 'h').reshape(nh * packed, 128)  34.3 us
    all_to_all x1, blocking collectives, per_device(): lax.all_to_all(found.reshape(wire), near, split_axis=0, concat_axis=0, ti...  29.2 us
    all_to_all x1, blocking collectives, per_device(): lax.all_to_all(terms.reshape(wire), near, split_axis=0, concat_axis=0, ti...  29 us
    all_to_all x1, waiting for transfers between devices, per_device(): lax.all_to_all(partial, 'h', split_axis=0, concat_axis=0, tiled=True)  26.7 us
    all_to_all x1, blocking collectives, per_device(): lax.all_to_all(wanted, near, split_axis=0, concat_axis=0, tiled=True)  19.8 us
    pallas_call x6, Pallas kernels, call(): pl.pallas_call(kernel, out_shape=shapes, in_specs=[pl.BlockSpec(memory_sp...  16.4 us
    all_gather x1, blocking collectives, per_device(): summed = lax.all_gather(grad, 'rep').reshape(reps * packed, 128)  13.9 us
    ppermute x3, starting transfers between devices, scatter_over_chips(): lax.ppermute(given, 'rep', [(i, (i + 2 * step) % reps) for i in range(rep...  9.24 us
  transfers between devices with their start and end apart: 5, of which 2 were waited for; matrix products, arithmetic and copies ran while one was open for 1% of the time, Pallas kernels for 2%

profile of v10, /device:TPU:33, one launch (start us, length us, event | category | flops | bytes accessed | tf_op | source)
XLA Modules:
  0.0 194.6 jit_solution(197158718344398930)
XLA Ops:
  0.6 0.9 dynamic-slice_bitcast_fusion.1
  1.6 34.3 %all_gather.9 = f32[8,200,128]{2,1,0:T(8,128)S(1)} all-gather(f32[1,200,128]{2,1,0:T(8,128)S(1)} %all_gather_reshape.3), channel_id=1, replica_groups=mesh['h'=8,'l'=2,'y'=4,'rep'=8] {'h'}, dimensions={0}, use_global_device_ids=true | all-gather | bytes 921600 | tf_op jit(solution)/shard_map/all_gather | solution.py:303
  35.8 1.1 shard_map.95
  36.9 19.8 %all_to_all.24 = s32[64,1,128]{2,1,0:T(1,128)S(1)} all-to-all(s32[64,1,128]{2,1,0:T(1,128)S(1)} %bitcast.61), channel_id=1, replica_groups=mesh['h'=8,'l'=2,'y'=4,'rep'=8] {'l','y','rep'}, dimensions={0} | all-to-all | bytes 65536 | tf_op jit(solution)/shard_map/all_to_all | solution.py:319
  56.7 0.1 copy.16
  56.8 0.2 copy.17
  57.0 0.3 reshape.69.ids_ref
  57.3 3.3 %shard_map.96 = f32[3200,128]{1,0:T(8,128)S(1)} custom-call(f32[1600,128]{1,0:T(8,128)S(1)} %bitcast.58, s32[8,1,1024]{2,1,0:T(1,128)S(1)} %reshape.69.ids_ref), custom_call_target="tpu_custom_call" | custom-call | flops 1677721600 | bytes 2490368 | tf_op jit(solution)/shard_map/pallas_call | solution.py:264
  60.6 0.0 copy-start
  60.6 0.0 copy-start.2
  60.6 29.2 %all_to_all.25 = f32[64,25,2,128]{3,2,1,0:T(2,128)S(1)} all-to-all(f32[64,25,2,128]{3,2,1,0:T(2,128)S(1)} %bitcast.53), channel_id=1, replica_groups=mesh['h'=8,'l'=2,'y'=4,'rep'=8] {'l','y','rep'}, dimensions={0} | all-to-all | bytes 3276800 | tf_op jit(solution)/shard_map/all_to_all | solution.py:336
  89.8 0.0 copy-done
  89.8 0.0 copy-done.2
  89.8 3.1 %shard_map.97 = f32[3200,128]{1,0:T(8,128)S(1)} custom-call(f32[3200,128]{1,0:T(8,128)S(1)} %bitcast.50, f32[400,512]{1,0:T(8,128)S(1)} %bitcast.55, f32[400,237]{1,0:T(8,128)S(1)} %bitcast.63, s32[1,512]{1,0:T(1,128)S(1)} %get-tuple-element.13.src_ref, s32[1,512]{1,0:T(1,128)S(1)} %get-tuple-element.14.rel_ref, f32[1,512]{1,0:T(1,128)S(1)} %get-tuple-element.15.live_ref), custom_call_target="tpu_custom_call" | custom-call | flops 2306867200 | bytes 4481344 | tf_op jit(solution)/shard_map/pallas_call | solution.py:264
  92.8 29.0 %all_to_all.26 = f32[64,25,2,128]{3,2,1,0:T(2,128)S(1)} all-to-all(f32[64,25,2,128]{3,2,1,0:T(2,128)S(1)} %bitcast.54), channel_id=1, replica_groups=mesh['h'=8,'l'=2,'y'=4,'rep'=8] {'l','y','rep'}, dimensions={0} | all-to-all | bytes 3276800 | tf_op jit(solution)/shard_map/all_to_all | solution.py:339
  121.9 4.4 %shard_map.98 = f32[8,200,128]{2,1,0:T(8,128)} custom-call(f32[3200,128]{1,0:T(8,128)S(1)} %bitcast.52, s32[8,1,1024]{2,1,0:T(1,128)S(1)} %reshape.69.ids_ref), custom_call_target="tpu_custom_call" | custom-call | flops 1677721600 | bytes 2490368 | tf_op jit(solution)/shard_map/pallas_call | solution.py:264
  126.3 7.3 %all-to-all-start.3 = ((f32[8,200,128]{2,1,0:T(8,128)}), f32[8,200,128]{2,1,0:T(8,128)}, u32[]{:S(2)}, u32[]{:S(2)}) async-start(f32[8,200,128]{2,1,0:T(8,128)} %shard_map.98), calls=%async_computation.3 | async-start | bytes 1638400 | tf_op jit(solution)/shard_map/all_to_all | solution.py:351
  133.5 0.0 copy-start.3
  133.5 1.0 copy-done.3
  134.5 3.5 %shard_map.99 = f32[1600,128]{1,0:T(8,128)S(1)} custom-call(f32[3200,128]{1,0:T(8,128)S(1)} %bitcast.51, f32[400,512]{1,0:T(8,128)S(1)} %bitcast.56, f32[400,237]{1,0:T(8,128)S(1)} %bitcast.64, s32[1,512]{1,0:T(1,128)S(1)} %get-tuple-element.13.src_ref, s32[1,512]{1,0:T(1,128)S(1)} %get-tuple-element.14.rel_ref, f32[1,512]{1,0:T(1,128)S(1)} %get-tuple-element.15.live_ref), custom_call_target="tpu_custom_call" | custom-call | flops 2726297600 | bytes 3662144 | tf_op jit(solution)/shard_map/pallas_call | solution.py:264
  138.1 2.8 %collective-permute-start = (f32[4,200,128]{2,1,0:T(8,128)S(1)}, f32[4,200,128]{2,1,0:T(8,128)S(1)}, u32[]{:S(2)}, u32[]{:S(2)}) collective-permute-start(f32[4,200,128]{2,1,0:T(8,128)S(1)} %dynamic-slice_bitcast_fusion), channel_id=1, source_target_pairs={{0,1},{1,0},{2,3},{3,2},{4,5},{5,4},{6,7},{7,6},{8,9},{9,8},{10,11... | collective-permute-start | bytes 1228808 | tf_op jit(solution)/shard_map/ppermute | solution.py:283
  140.9 1.3 collective-permute-done
  142.2 0.1 bitcast_add_fusion
  142.3 0.0 copy-start.1
  142.3 2.2 %collective-permute-start.1 = (f32[200,128]{1,0:T(8,128)S(1)}, f32[200,128]{1,0:T(8,128)S(1)}, u32[]{:S(2)}, u32[]{:S(2)}) collective-permute-start(f32[200,128]{1,0:T(8,128)S(1)} %get-tuple-element.18), channel_id=1, source_target_pairs={{0,2},{1,3},{2,4},{3,5},{4,6},{5,7},{6,0},{7,1},{8,10},{9,11},{10,... | collective-permute-start | bytes 307208 | tf_op jit(solution)/shard_map/ppermute | solution.py:287
  144.6 3.8 %collective-permute-start.2 = (f32[200,128]{1,0:T(8,128)S(1)}, f32[200,128]{1,0:T(8,128)S(1)}, u32[]{:S(2)}, u32[]{:S(2)}) collective-permute-start(f32[200,128]{1,0:T(8,128)S(1)} %get-tuple-element.20), channel_id=1, source_target_pairs={{0,4},{1,5},{2,6},{3,7},{4,0},{5,1},{6,2},{7,3},{8,12},{9,13},{10,... | collective-permute-start | bytes 307208 | tf_op jit(solution)/shard_map/ppermute | solution.py:287
  148.4 3.1 %collective-permute-start.3 = (f32[200,128]{1,0:T(8,128)S(1)}, f32[200,128]{1,0:T(8,128)S(1)}, u32[]{:S(2)}, u32[]{:S(2)}) collective-permute-start(f32[200,128]{1,0:T(8,128)S(1)} %get-tuple-element.19), channel_id=1, source_target_pairs={{0,6},{1,7},{2,0},{3,1},{4,2},{5,3},{6,4},{7,5},{8,14},{9,15},{10,... | collective-permute-start | bytes 307208 | tf_op jit(solution)/shard_map/ppermute | solution.py:287
  151.6 26.7 %all-to-all-done.3 = f32[8,200,128]{2,1,0:T(8,128)} async-done(((f32[8,200,128]{2,1,0:T(8,128)}), f32[8,200,128]{2,1,0:T(8,128)}, u32[]{:S(2)}, u32[]{:S(2)}) %all-to-all-start.3) | async-done | bytes 819232 | tf_op jit(solution)/shard_map/all_to_all | solution.py:351
  178.3 1.2 reduce_sum.9
  179.5 0.0 collective-permute-done.1
  179.5 0.0 collective-permute-done.2
  179.5 0.0 collective-permute-done.3
  179.5 13.9 %all-gather.grad_ref = f32[1600,128]{1,0:T(8,128)S(1)} all-gather(f32[200,128]{1,0:T(8,128)S(1)} %fusion.2), channel_id=2, replica_groups=mesh['h'=8,'l'=2,'y'=4,'rep'=8] {'rep'}, dimensions={0}, use_global_device_ids=true | all-gather | bytes 921600 | tf_op jit(solution)/shard_map/all_gather | solution.py:353
  193.5 0.0 copy-done.1
  193.5 1.2 shard_map.100
  (4 shorter events, 0.1 us)
Async XLA Ops:
  60.6 29.2 %copy-start = (f32[512,400]{0,1:T(8,128)S(1)}, f32[512,400]{0,1:T(8,128)}, u32[]{:S(2)}) copy-start(f32[512,400]{0,1:T(8,128)} %param.8) | copy-start | bytes 2457604
  60.6 29.2 %copy-start.2 = (f32[237,400]{0,1:T(8,128)S(1)}, f32[237,400]{0,1:T(8,128)}, u32[]{:S(2)}) copy-start(f32[237,400]{0,1:T(8,128)} %param.10) | copy-start | bytes 1137604
  126.3 52.0 %all-to-all-start.3 = ((f32[8,200,128]{2,1,0:T(8,128)}), f32[8,200,128]{2,1,0:T(8,128)}, u32[]{:S(2)}, u32[]{:S(2)}) async-start(f32[8,200,128]{2,1,0:T(8,128)} %shard_map.98), calls=%async_computation.3 | async-start | bytes 1638400 | tf_op jit(solution)/shard_map/all_to_all | solution.py:351
  133.5 1.0 copy-start.3
  138.1 4.1 %collective-permute-start = (f32[4,200,128]{2,1,0:T(8,128)S(1)}, f32[4,200,128]{2,1,0:T(8,128)S(1)}, u32[]{:S(2)}, u32[]{:S(2)}) collective-permute-start(f32[4,200,128]{2,1,0:T(8,128)S(1)} %dynamic-slice_bitcast_fusion), channel_id=1, source_target_pairs={{0,1},{1,0},{2,3},{3,2},{4,5},{5,4},{6,7},{7,6},{8,9},{9,8},{10,11... | collective-permute-start | bytes 1228808 | tf_op jit(solution)/shard_map/ppermute | solution.py:283
  142.3 51.2 %copy-start.1 = (f32[512]{0:T(512)S(1)}, f32[512]{0:T(512)}, u32[]{:S(2)}) copy-start(f32[512]{0:T(512)} %param.9) | copy-start | bytes 6148
  142.3 37.2 %collective-permute-start.1 = (f32[200,128]{1,0:T(8,128)S(1)}, f32[200,128]{1,0:T(8,128)S(1)}, u32[]{:S(2)}, u32[]{:S(2)}) collective-permute-start(f32[200,128]{1,0:T(8,128)S(1)} %get-tuple-element.18), channel_id=1, source_target_pairs={{0,2},{1,3},{2,4},{3,5},{4,6},{5,7},{6,0},{7,1},{8,10},{9,11},{10,... | collective-permute-start | bytes 307208 | tf_op jit(solution)/shard_map/ppermute | solution.py:287
  144.6 34.9 %collective-permute-start.2 = (f32[200,128]{1,0:T(8,128)S(1)}, f32[200,128]{1,0:T(8,128)S(1)}, u32[]{:S(2)}, u32[]{:S(2)}) collective-permute-start(f32[200,128]{1,0:T(8,128)S(1)} %get-tuple-element.20), channel_id=1, source_target_pairs={{0,4},{1,5},{2,6},{3,7},{4,0},{5,1},{6,2},{7,3},{8,12},{9,13},{10,... | collective-permute-start | bytes 307208 | tf_op jit(solution)/shard_map/ppermute | solution.py:287
  148.4 31.1 %collective-permute-start.3 = (f32[200,128]{1,0:T(8,128)S(1)}, f32[200,128]{1,0:T(8,128)S(1)}, u32[]{:S(2)}, u32[]{:S(2)}) collective-permute-start(f32[200,128]{1,0:T(8,128)S(1)} %get-tuple-element.19), channel_id=1, source_target_pairs={{0,6},{1,7},{2,0},{3,1},{4,2},{5,3},{6,4},{7,5},{8,14},{9,15},{10,... | collective-permute-start | bytes 307208 | tf_op jit(solution)/shard_map/ppermute | solution.py:287

commit v11 on v8

--- a/solution.py
+++ b/solution.py
@@ -38,7 +38,7 @@
     return lax.dot_general(a, b, dims, preferred_element_type=F32)
 
 
-def pick(x, hot, dims=NN, terms=3):
+def pick(x, hot, dims=NN, terms=2):
     n = x.shape[0]
     parts = [part.astype(F32) for part in split(x, terms)]
     out = mul(jnp.concatenate(parts, axis=0).astype(BF16), hot, dims)
@@ -329,7 +329,7 @@
         functools.partial(table_kernel, fs),
         floats(message),
         table, asked,
-        scratch=[got_shape, pltpu.VMEM((3 * held, rows), F32)],
+        scratch=[got_shape, pltpu.VMEM((2 * held, rows), F32)],
         flops=8 * unit,
     )
     got = lax.all_to_all(found.reshape(wire), near, split_axis=0, concat_axis=0, tiled=True).reshape(message)

time: 193 us -> 192 us (level)
  no operation moved by 1% of the time
where the time goes in v11:
time: 192 us; the launch traced here: 191 us
  blocking collectives  113 us (59%)
  starting transfers between devices  29.7 us (15%)
  waiting for transfers between devices  28.4 us (15%)
  Pallas kernels  15.7 us (8%)
  local copies, waits for them, and re-layouts  2.61 us (1%)
    all_to_all x1, blocking collectives, per_device(): lax.all_to_all(found.reshape(wire), near, split_axis=0, concat_axis=0, ti...  37.4 us
    all_gather x1, blocking collectives, per_device(): lax.all_gather(mine.reshape(packed, 128), 'h').reshape(nh * packed, 128)  32.4 us
    all_to_all x1, blocking collectives, per_device(): lax.all_to_all(terms.reshape(wire), near, split_axis=0, concat_axis=0, ti...  29 us
    all_to_all x1, waiting for transfers between devices, per_device(): lax.all_to_all(partial, 'h', split_axis=0, concat_axis=0, tiled=True)  27 us
    pallas_call x6, Pallas kernels, call(): pl.pallas_call(kernel, out_shape=shapes, in_specs=[pl.BlockSpec(memory_sp...  15.7 us
    all_gather x1, blocking collectives, per_device(): summed = lax.all_gather(grad, 'rep').reshape(reps * packed, 128)  13.9 us
    all_to_all x1, starting transfers between devices, per_device(): lax.all_to_all(wanted, near, split_axis=0, concat_axis=0, tiled=True)  10 us
    ppermute x3, starting transfers between devices, scatter_over_chips(): lax.ppermute(given, 'rep', [(i, (i + 2 * step) % reps) for i in range(rep...  9.24 us
  transfers between devices with their start and end apart: 6, of which 2 were waited for; matrix products, arithmetic and copies ran while one was open for 1% of the time, Pallas kernels for 2%

profile of v11, /device:TPU:33, one launch (start us, length us, event | category | flops | bytes accessed | tf_op | source)
XLA Modules:
  0.0 191.3 jit_solution(11463249989934576470)
XLA Ops:
  0.6 1.7 shard_map.95
  2.3 10.0 %all-to-all-start = ((s32[64,1,128]{2,1,0:T(1,128)}), s32[64,1,128]{2,1,0:T(1,128)S(1)}, u32[]{:S(2)}, u32[]{:S(2)}) async-start(s32[64,1,128]{2,1,0:T(1,128)} %bitcast.11), calls=%async_computation | async-start | bytes 65536 | tf_op jit(solution)/shard_map/all_to_all | solution.py:318
  12.4 0.9 dynamic-slice_bitcast_fusion.1
  13.3 32.4 %all_gather.9 = f32[8,200,128]{2,1,0:T(8,128)S(1)} all-gather(f32[1,200,128]{2,1,0:T(8,128)S(1)} %all_gather_reshape.3), channel_id=1, replica_groups=mesh['h'=8,'l'=2,'y'=4,'rep'=8] {'h'}, dimensions={0}, use_global_device_ids=true | all-gather | bytes 921600 | tf_op jit(solution)/shard_map/all_gather | solution.py:303
  45.8 0.0 all-to-all-done
  45.8 0.1 copy.16
  45.9 0.2 copy.17
  46.1 0.3 reshape.69.ids_ref
  46.4 2.5 %shard_map.96 = f32[3200,128]{1,0:T(8,128)S(1)} custom-call(f32[1600,128]{1,0:T(8,128)S(1)} %bitcast.58, s32[8,1,1024]{2,1,0:T(1,128)S(1)} %reshape.69.ids_ref), custom_call_target="tpu_custom_call" | custom-call | flops 1677721600 | bytes 2490368 | tf_op jit(solution)/shard_map/pallas_call | solution.py:264
  49.0 0.0 copy-start
  49.0 0.0 copy-start.2
  49.0 37.4 %all_to_all.24 = f32[64,25,2,128]{3,2,1,0:T(2,128)S(1)} all-to-all(f32[64,25,2,128]{3,2,1,0:T(2,128)S(1)} %bitcast.53), channel_id=1, replica_groups=mesh['h'=8,'l'=2,'y'=4,'rep'=8] {'l','y','rep'}, dimensions={0} | all-to-all | bytes 3276800 | tf_op jit(solution)/shard_map/all_to_all | solution.py:335
  86.3 0.0 copy-done
  86.3 0.0 copy-done.2
  86.3 2.8 %shard_map.97 = f32[3200,128]{1,0:T(8,128)S(1)} custom-call(f32[3200,128]{1,0:T(8,128)S(1)} %bitcast.50, f32[400,512]{1,0:T(8,128)S(1)} %bitcast.55, f32[400,237]{1,0:T(8,128)S(1)} %bitcast.62, s32[1,512]{1,0:T(1,128)S(1)} %get-tuple-element.9.src_ref, s32[1,512]{1,0:T(1,128)S(1)} %get-tuple-element.10.rel_ref, f32[1,512]{1,0:T(1,128)S(1)} %get-tuple-element.11.live_ref), custom_call_target="tpu_custom_call" | custom-call | flops 2306867200 | bytes 4481344 | tf_op jit(solution)/shard_map/pallas_call | solution.py:264
  89.1 29.0 %all_to_all.25 = f32[64,25,2,128]{3,2,1,0:T(2,128)S(1)} all-to-all(f32[64,25,2,128]{3,2,1,0:T(2,128)S(1)} %bitcast.54), channel_id=1, replica_groups=mesh['h'=8,'l'=2,'y'=4,'rep'=8] {'l','y','rep'}, dimensions={0} | all-to-all | bytes 3276800 | tf_op jit(solution)/shard_map/all_to_all | solution.py:338
  118.2 4.4 %shard_map.98 = f32[8,200,128]{2,1,0:T(8,128)} custom-call(f32[3200,128]{1,0:T(8,128)S(1)} %bitcast.52, s32[8,1,1024]{2,1,0:T(1,128)S(1)} %reshape.69.ids_ref), custom_call_target="tpu_custom_call" | custom-call | flops 1677721600 | bytes 2490368 | tf_op jit(solution)/shard_map/pallas_call | solution.py:264
  122.5 7.7 %all-to-all-start.3 = ((f32[8,200,128]{2,1,0:T(8,128)}), f32[8,200,128]{2,1,0:T(8,128)}, u32[]{:S(2)}, u32[]{:S(2)}) async-start(f32[8,200,128]{2,1,0:T(8,128)} %shard_map.98), calls=%async_computation.3 | async-start | bytes 1638400 | tf_op jit(solution)/shard_map/all_to_all | solution.py:350
  130.2 0.0 copy-start.3
  130.2 1.0 copy-done.3
  131.2 3.1 %shard_map.99 = f32[1600,128]{1,0:T(8,128)S(1)} custom-call(f32[3200,128]{1,0:T(8,128)S(1)} %bitcast.51, f32[400,512]{1,0:T(8,128)S(1)} %bitcast.56, f32[400,237]{1,0:T(8,128)S(1)} %bitcast.63, s32[1,512]{1,0:T(1,128)S(1)} %get-tuple-element.9.src_ref, s32[1,512]{1,0:T(1,128)S(1)} %get-tuple-element.10.rel_ref, f32[1,512]{1,0:T(1,128)S(1)} %get-tuple-element.11.live_ref), custom_call_target="tpu_custom_call" | custom-call | flops 2726297600 | bytes 3662144 | tf_op jit(solution)/shard_map/pallas_call | solution.py:264
  134.4 2.8 %collective-permute-start = (f32[4,200,128]{2,1,0:T(8,128)S(1)}, f32[4,200,128]{2,1,0:T(8,128)S(1)}, u32[]{:S(2)}, u32[]{:S(2)}) collective-permute-start(f32[4,200,128]{2,1,0:T(8,128)S(1)} %dynamic-slice_bitcast_fusion), channel_id=1, source_target_pairs={{0,1},{1,0},{2,3},{3,2},{4,5},{5,4},{6,7},{7,6},{8,9},{9,8},{10,11... | collective-permute-start | bytes 1228808 | tf_op jit(solution)/shard_map/ppermute | solution.py:283
  137.2 1.3 collective-permute-done
  138.6 0.1 bitcast_add_fusion
  138.6 0.0 copy-start.1
  138.7 2.2 %collective-permute-start.1 = (f32[200,128]{1,0:T(8,128)S(1)}, f32[200,128]{1,0:T(8,128)S(1)}, u32[]{:S(2)}, u32[]{:S(2)}) collective-permute-start(f32[200,128]{1,0:T(8,128)S(1)} %get-tuple-element.14), channel_id=1, source_target_pairs={{0,2},{1,3},{2,4},{3,5},{4,6},{5,7},{6,0},{7,1},{8,10},{9,11},{10,... | collective-permute-start | bytes 307208 | tf_op jit(solution)/shard_map/ppermute | solution.py:287
  140.9 3.8 %collective-permute-start.2 = (f32[200,128]{1,0:T(8,128)S(1)}, f32[200,128]{1,0:T(8,128)S(1)}, u32[]{:S(2)}, u32[]{:S(2)}) collective-permute-start(f32[200,128]{1,0:T(8,128)S(1)} %get-tuple-element.16), channel_id=1, source_target_pairs={{0,4},{1,5},{2,6},{3,7},{4,0},{5,1},{6,2},{7,3},{8,12},{9,13},{10,... | collective-permute-start | bytes 307208 | tf_op jit(solution)/shard_map/ppermute | solution.py:287
  144.8 3.1 %collective-permute-start.3 = (f32[200,128]{1,0:T(8,128)S(1)}, f32[200,128]{1,0:T(8,128)S(1)}, u32[]{:S(2)}, u32[]{:S(2)}) collective-permute-start(f32[200,128]{1,0:T(8,128)S(1)} %get-tuple-element.15), channel_id=1, source_target_pairs={{0,6},{1,7},{2,0},{3,1},{4,2},{5,3},{6,4},{7,5},{8,14},{9,15},{10,... | collective-permute-start | bytes 307208 | tf_op jit(solution)/shard_map/ppermute | solution.py:287
  147.9 27.0 %all-to-all-done.3 = f32[8,200,128]{2,1,0:T(8,128)} async-done(((f32[8,200,128]{2,1,0:T(8,128)}), f32[8,200,128]{2,1,0:T(8,128)}, u32[]{:S(2)}, u32[]{:S(2)}) %all-to-all-start.3) | async-done | bytes 819232 | tf_op jit(solution)/shard_map/all_to_all | solution.py:350
  175.0 1.2 reduce_sum.9
  176.2 0.0 collective-permute-done.1
  176.2 0.0 collective-permute-done.2
  176.2 0.0 collective-permute-done.3
  176.2 13.9 %all-gather.grad_ref = f32[1600,128]{1,0:T(8,128)S(1)} all-gather(f32[200,128]{1,0:T(8,128)S(1)} %fusion.2), channel_id=2, replica_groups=mesh['h'=8,'l'=2,'y'=4,'rep'=8] {'rep'}, dimensions={0}, use_global_device_ids=true | all-gather | bytes 921600 | tf_op jit(solution)/shard_map/all_gather | solution.py:352
  190.2 0.0 copy-done.1
  190.2 1.2 shard_map.100
  (4 shorter events, 0.1 us)
Async XLA Ops:
  2.3 43.5 %all-to-all-start = ((s32[64,1,128]{2,1,0:T(1,128)}), s32[64,1,128]{2,1,0:T(1,128)S(1)}, u32[]{:S(2)}, u32[]{:S(2)}) async-start(s32[64,1,128]{2,1,0:T(1,128)} %bitcast.11), calls=%async_computation | async-start | bytes 65536 | tf_op jit(solution)/shard_map/all_to_all | solution.py:318
  49.0 37.4 %copy-start = (f32[512,400]{0,1:T(8,128)S(1)}, f32[512,400]{0,1:T(8,128)}, u32[]{:S(2)}) copy-start(f32[512,400]{0,1:T(8,128)} %param.8) | copy-start | bytes 2457604
  49.0 37.4 %copy-start.2 = (f32[237,400]{0,1:T(8,128)S(1)}, f32[237,400]{0,1:T(8,128)}, u32[]{:S(2)}) copy-start(f32[237,400]{0,1:T(8,128)} %param.10) | copy-start | bytes 1137604
  122.5 52.4 %all-to-all-start.3 = ((f32[8,200,128]{2,1,0:T(8,128)}), f32[8,200,128]{2,1,0:T(8,128)}, u32[]{:S(2)}, u32[]{:S(2)}) async-start(f32[8,200,128]{2,1,0:T(8,128)} %shard_map.98), calls=%async_computation.3 | async-start | bytes 1638400 | tf_op jit(solution)/shard_map/all_to_all | solution.py:350
  130.2 1.0 copy-start.3
  134.4 4.1 %collective-permute-start = (f32[4,200,128]{2,1,0:T(8,128)S(1)}, f32[4,200,128]{2,1,0:T(8,128)S(1)}, u32[]{:S(2)}, u32[]{:S(2)}) collective-permute-start(f32[4,200,128]{2,1,0:T(8,128)S(1)} %dynamic-slice_bitcast_fusion), channel_id=1, source_target_pairs={{0,1},{1,0},{2,3},{3,2},{4,5},{5,4},{6,7},{7,6},{8,9},{9,8},{10,11... | collective-permute-start | bytes 1228808 | tf_op jit(solution)/shard_map/ppermute | solution.py:283
  138.6 51.5 %copy-start.1 = (f32[512]{0:T(512)S(1)}, f32[512]{0:T(512)}, u32[]{:S(2)}) copy-start(f32[512]{0:T(512)} %param.9) | copy-start | bytes 6148
  138.7 37.5 %collective-permute-start.1 = (f32[200,128]{1,0:T(8,128)S(1)}, f32[200,128]{1,0:T(8,128)S(1)}, u32[]{:S(2)}, u32[]{:S(2)}) collective-permute-start(f32[200,128]{1,0:T(8,128)S(1)} %get-tuple-element.14), channel_id=1, source_target_pairs={{0,2},{1,3},{2,4},{3,5},{4,6},{5,7},{6,0},{7,1},{8,10},{9,11},{10,... | collective-permute-start | bytes 307208 | tf_op jit(solution)/shard_map/ppermute | solution.py:287
  140.9 35.3 %collective-permute-start.2 = (f32[200,128]{1,0:T(8,128)S(1)}, f32[200,128]{1,0:T(8,128)S(1)}, u32[]{:S(2)}, u32[]{:S(2)}) collective-permute-start(f32[200,128]{1,0:T(8,128)S(1)} %get-tuple-element.16), channel_id=1, source_target_pairs={{0,4},{1,5},{2,6},{3,7},{4,0},{5,1},{6,2},{7,3},{8,12},{9,13},{10,... | collective-permute-start | bytes 307208 | tf_op jit(solution)/shard_map/ppermute | solution.py:287
  144.8 31.4 %collective-permute-start.3 = (f32[200,128]{1,0:T(8,128)S(1)}, f32[200,128]{1,0:T(8,128)S(1)}, u32[]{:S(2)}, u32[]{:S(2)}) collective-permute-start(f32[200,128]{1,0:T(8,128)S(1)} %get-tuple-element.15), channel_id=1, source_target_pairs={{0,6},{1,7},{2,0},{3,1},{4,2},{5,3},{6,4},{7,5},{8,14},{9,15},{10,... | collective-permute-start | bytes 307208 | tf_op jit(solution)/shard_map/ppermute | solution.py:287

commit v12 on v11

--- a/solution.py
+++ b/solution.py
@@ -348,7 +348,7 @@
         functools.partial(source_kernel, ny, reps), floats((reps * packed, 128)), *edge_args, flops=13 * unit
     )
     partial = lax.all_to_all(partial, "h", split_axis=0, concat_axis=0, tiled=True)
-    grad = jnp.sum(partial, axis=0) + scatter_over_chips(source.reshape(reps, packed, 128))
+    grad = scatter_over_chips(source.reshape(reps, packed, 128)) + sum(partial[h] for h in range(nh))
     summed = lax.all_gather(grad, "rep").reshape(reps * packed, 128)
     new_entity, new_state = call(
         functools.partial(update_kernel, reps),

time: 192 us -> 192 us (level)
    all_to_all x1, waiting for transfers between devices: 27 us -> 24.4 us  [per_device(): lax.all_to_all(partial, 'h', split_axis=0, concat_axis=0, tiled=True)]
    ppermute x3, waiting for transfers between devices: 0.01 us -> 2.65 us  [scatter_over_chips(): lax.ppermute(given, 'rep', [(i, (i + 2 * step) % reps) for i in range(rep...]
  transfers between devices with their start and end apart: 6 -> 6, of which waited for: 2 -> 4; matrix products, arithmetic and copies ran while one was open for 1% -> 1% of each run, Pallas kernels for 2% -> 2%
where the time goes in v12:
time: 192 us; the launch traced here: 191 us
  blocking collectives  113 us (59%)
  starting transfers between devices  29.7 us (15%)
  waiting for transfers between devices  28.4 us (15%)
  Pallas kernels  15.7 us (8%)
  local copies, waits for them, and re-layouts  2.61 us (1%)
    all_to_all x1, blocking collectives, per_device(): lax.all_to_all(found.reshape(wire), near, split_axis=0, concat_axis=0, ti...  37.4 us
    all_gather x1, blocking collectives, per_device(): lax.all_gather(mine.reshape(packed, 128), 'h').reshape(nh * packed, 128)  32.4 us
    all_to_all x1, blocking collectives, per_device(): lax.all_to_all(terms.reshape(wire), near, split_axis=0, concat_axis=0, ti...  29 us
    all_to_all x1, waiting for transfers between devices, per_device(): lax.all_to_all(partial, 'h', split_axis=0, concat_axis=0, tiled=True)  24.4 us
    pallas_call x6, Pallas kernels, call(): pl.pallas_call(kernel, out_shape=shapes, in_specs=[pl.BlockSpec(memory_sp...  15.7 us
    all_gather x1, blocking collectives, per_device(): summed = lax.all_gather(grad, 'rep').reshape(reps * packed, 128)  13.9 us
    all_to_all x1, starting transfers between devices, per_device(): lax.all_to_all(wanted, near, split_axis=0, concat_axis=0, tiled=True)  10 us
    ppermute x3, starting transfers between devices, scatter_over_chips(): lax.ppermute(given, 'rep', [(i, (i + 2 * step) % reps) for i in range(rep...  9.24 us
  transfers between devices with their start and end apart: 6, of which 4 were waited for; matrix products, arithmetic and copies ran while one was open for 1% of the time, Pallas kernels for 2%

profile of v12, /device:TPU:33, one launch (start us, length us, event | category | flops | bytes accessed | tf_op | source)
XLA Modules:
  0.0 191.3 jit_solution(17838332085018878871)
XLA Ops:
  0.6 1.7 shard_map.95
  2.3 10.0 %all-to-all-start = ((s32[64,1,128]{2,1,0:T(1,128)}), s32[64,1,128]{2,1,0:T(1,128)S(1)}, u32[]{:S(2)}, u32[]{:S(2)}) async-start(s32[64,1,128]{2,1,0:T(1,128)} %bitcast.11), calls=%async_computation | async-start | bytes 65536 | tf_op jit(solution)/shard_map/all_to_all | solution.py:318
  12.4 0.9 dynamic-slice_bitcast_fusion.1
  13.3 32.4 %all_gather.9 = f32[8,200,128]{2,1,0:T(8,128)S(1)} all-gather(f32[1,200,128]{2,1,0:T(8,128)S(1)} %all_gather_reshape.3), channel_id=1, replica_groups=mesh['h'=8,'l'=2,'y'=4,'rep'=8] {'h'}, dimensions={0}, use_global_device_ids=true | all-gather | bytes 921600 | tf_op jit(solution)/shard_map/all_gather | solution.py:303
  45.8 0.0 all-to-all-done
  45.8 0.1 copy.16
  45.9 0.2 copy.17
  46.1 0.3 reshape.76.ids_ref
  46.4 2.5 %shard_map.96 = f32[3200,128]{1,0:T(8,128)S(1)} custom-call(f32[1600,128]{1,0:T(8,128)S(1)} %bitcast.62, s32[8,1,1024]{2,1,0:T(1,128)S(1)} %reshape.76.ids_ref), custom_call_target="tpu_custom_call" | custom-call | flops 1677721600 | bytes 2490368 | tf_op jit(solution)/shard_map/pallas_call | solution.py:264
  49.0 0.0 copy-start
  49.0 0.0 copy-start.2
  49.0 37.4 %all_to_all.24 = f32[64,25,2,128]{3,2,1,0:T(2,128)S(1)} all-to-all(f32[64,25,2,128]{3,2,1,0:T(2,128)S(1)} %bitcast.57), channel_id=1, replica_groups=mesh['h'=8,'l'=2,'y'=4,'rep'=8] {'l','y','rep'}, dimensions={0} | all-to-all | bytes 3276800 | tf_op jit(solution)/shard_map/all_to_all | solution.py:335
  86.3 0.0 copy-done
  86.3 0.0 copy-done.2
  86.3 2.8 %shard_map.98 = f32[3200,128]{1,0:T(8,128)S(1)} custom-call(f32[3200,128]{1,0:T(8,128)S(1)} %bitcast.54, f32[400,512]{1,0:T(8,128)S(1)} %bitcast.59, f32[400,237]{1,0:T(8,128)S(1)} %bitcast.66, s32[1,512]{1,0:T(1,128)S(1)} %get-tuple-element.9.src_ref, s32[1,512]{1,0:T(1,128)S(1)} %get-tuple-element.10.rel_ref, f32[1,512]{1,0:T(1,128)S(1)} %get-tuple-element.11.live_ref), custom_call_target="tpu_custom_call" | custom-call | flops 2306867200 | bytes 4481344 | tf_op jit(solution)/shard_map/pallas_call | solution.py:264
  89.1 29.0 %all_to_all.25 = f32[64,25,2,128]{3,2,1,0:T(2,128)S(1)} all-to-all(f32[64,25,2,128]{3,2,1,0:T(2,128)S(1)} %bitcast.58), channel_id=1, replica_groups=mesh['h'=8,'l'=2,'y'=4,'rep'=8] {'l','y','rep'}, dimensions={0} | all-to-all | bytes 3276800 | tf_op jit(solution)/shard_map/all_to_all | solution.py:338
  118.2 4.4 %shard_map.99 = f32[8,200,128]{2,1,0:T(8,128)} custom-call(f32[3200,128]{1,0:T(8,128)S(1)} %bitcast.56, s32[8,1,1024]{2,1,0:T(1,128)S(1)} %reshape.76.ids_ref), custom_call_target="tpu_custom_call" | custom-call | flops 1677721600 | bytes 2490368 | tf_op jit(solution)/shard_map/pallas_call | solution.py:264
  122.5 7.7 %all-to-all-start.3 = ((f32[8,200,128]{2,1,0:T(8,128)}), f32[8,200,128]{2,1,0:T(8,128)}, u32[]{:S(2)}, u32[]{:S(2)}) async-start(f32[8,200,128]{2,1,0:T(8,128)} %shard_map.99), calls=%async_computation.3 | async-start | bytes 1638400 | tf_op jit(solution)/shard_map/all_to_all | solution.py:350
  130.2 0.0 copy-start.3
  130.2 1.0 copy-done.3
  131.2 3.1 %shard_map.97 = f32[1600,128]{1,0:T(8,128)S(1)} custom-call(f32[3200,128]{1,0:T(8,128)S(1)} %bitcast.55, f32[400,512]{1,0:T(8,128)S(1)} %bitcast.60, f32[400,237]{1,0:T(8,128)S(1)} %bitcast.67, s32[1,512]{1,0:T(1,128)S(1)} %get-tuple-element.9.src_ref, s32[1,512]{1,0:T(1,128)S(1)} %get-tuple-element.10.rel_ref, f32[1,512]{1,0:T(1,128)S(1)} %get-tuple-element.11.live_ref), custom_call_target="tpu_custom_call" | custom-call | flops 2726297600 | bytes 3662144 | tf_op jit(solution)/shard_map/pallas_call | solution.py:264
  134.4 2.8 %collective-permute-start = (f32[4,200,128]{2,1,0:T(8,128)S(1)}, f32[4,200,128]{2,1,0:T(8,128)S(1)}, u32[]{:S(2)}, u32[]{:S(2)}) collective-permute-start(f32[4,200,128]{2,1,0:T(8,128)S(1)} %dynamic-slice_bitcast_fusion), channel_id=1, source_target_pairs={{0,1},{1,0},{2,3},{3,2},{4,5},{5,4},{6,7},{7,6},{8,9},{9,8},{10,11... | collective-permute-start | bytes 1228808 | tf_op jit(solution)/shard_map/ppermute | solution.py:283
  137.2 1.3 collective-permute-done
  138.6 0.1 bitcast_add_fusion
  138.6 0.0 copy-start.1
  138.7 2.2 %collective-permute-start.1 = (f32[200,128]{1,0:T(8,128)S(1)}, f32[200,128]{1,0:T(8,128)S(1)}, u32[]{:S(2)}, u32[]{:S(2)}) collective-permute-start(f32[200,128]{1,0:T(8,128)S(1)} %get-tuple-element.14), channel_id=1, source_target_pairs={{0,2},{1,3},{2,4},{3,5},{4,6},{5,7},{6,0},{7,1},{8,10},{9,11},{10,... | collective-permute-start | bytes 307208 | tf_op jit(solution)/shard_map/ppermute | solution.py:287
  140.9 3.8 %collective-permute-start.2 = (f32[200,128]{1,0:T(8,128)S(1)}, f32[200,128]{1,0:T(8,128)S(1)}, u32[]{:S(2)}, u32[]{:S(2)}) collective-permute-start(f32[200,128]{1,0:T(8,128)S(1)} %get-tuple-element.16), channel_id=1, source_target_pairs={{0,4},{1,5},{2,6},{3,7},{4,0},{5,1},{6,2},{7,3},{8,12},{9,13},{10,... | collective-permute-start | bytes 307208 | tf_op jit(solution)/shard_map/ppermute | solution.py:287
  144.8 3.1 %collective-permute-start.3 = (f32[200,128]{1,0:T(8,128)S(1)}, f32[200,128]{1,0:T(8,128)S(1)}, u32[]{:S(2)}, u32[]{:S(2)}) collective-permute-start(f32[200,128]{1,0:T(8,128)S(1)} %get-tuple-element.15), channel_id=1, source_target_pairs={{0,6},{1,7},{2,0},{3,1},{4,2},{5,3},{6,4},{7,5},{8,14},{9,15},{10,... | collective-permute-start | bytes 307208 | tf_op jit(solution)/shard_map/ppermute | solution.py:287
  147.9 0.0 collective-permute-done.1
  147.9 0.3 collective-permute-done.2
  148.2 2.4 %collective-permute-done.3 = f32[200,128]{1,0:T(8,128)S(1)} collective-permute-done((f32[200,128]{1,0:T(8,128)S(1)}, f32[200,128]{1,0:T(8,128)S(1)}, u32[]{:S(2)}, u32[]{:S(2)}) %collective-permute-start.3) | collective-permute-done | bytes 102432 | tf_op jit(solution)/shard_map/ppermute | solution.py:287
  150.6 24.4 %all-to-all-done.3 = f32[8,200,128]{2,1,0:T(8,128)} async-done(((f32[8,200,128]{2,1,0:T(8,128)}), f32[8,200,128]{2,1,0:T(8,128)}, u32[]{:S(2)}, u32[]{:S(2)}) %all-to-all-start.3) | async-done | bytes 819232 | tf_op jit(solution)/shard_map/all_to_all | solution.py:350
  175.0 1.3 fusion.1
  176.3 13.9 %all-gather.grad_ref = f32[1600,128]{1,0:T(8,128)S(1)} all-gather(f32[200,128]{1,0:T(8,128)S(1)} %fusion.1), channel_id=2, replica_groups=mesh['h'=8,'l'=2,'y'=4,'rep'=8] {'rep'}, dimensions={0}, use_global_device_ids=true | all-gather | bytes 921600 | tf_op jit(solution)/shard_map/all_gather | solution.py:352
  190.2 0.0 copy-done.1
  190.2 1.2 shard_map.100
  (3 shorter events, 0.1 us)
Async XLA Ops:
  2.3 43.5 %all-to-all-start = ((s32[64,1,128]{2,1,0:T(1,128)}), s32[64,1,128]{2,1,0:T(1,128)S(1)}, u32[]{:S(2)}, u32[]{:S(2)}) async-start(s32[64,1,128]{2,1,0:T(1,128)} %bitcast.11), calls=%async_computation | async-start | bytes 65536 | tf_op jit(solution)/shard_map/all_to_all | solution.py:318
  49.0 37.4 %copy-start = (f32[512,400]{0,1:T(8,128)S(1)}, f32[512,400]{0,1:T(8,128)}, u32[]{:S(2)}) copy-start(f32[512,400]{0,1:T(8,128)} %param.8) | copy-start | bytes 2457604
  49.0 37.4 %copy-start.2 = (f32[237,400]{0,1:T(8,128)S(1)}, f32[237,400]{0,1:T(8,128)}, u32[]{:S(2)}) copy-start(f32[237,400]{0,1:T(8,128)} %param.10) | copy-start | bytes 1137604
  122.5 52.4 %all-to-all-start.3 = ((f32[8,200,128]{2,1,0:T(8,128)}), f32[8,200,128]{2,1,0:T(8,128)}, u32[]{:S(2)}, u32[]{:S(2)}) async-start(f32[8,200,128]{2,1,0:T(8,128)} %shard_map.99), calls=%async_computation.3 | async-start | bytes 1638400 | tf_op jit(solution)/shard_map/all_to_all | solution.py:350
  130.2 1.0 copy-start.3
  134.4 4.1 %collective-permute-start = (f32[4,200,128]{2,1,0:T(8,128)S(1)}, f32[4,200,128]{2,1,0:T(8,128)S(1)}, u32[]{:S(2)}, u32[]{:S(2)}) collective-permute-start(f32[4,200,128]{2,1,0:T(8,128)S(1)} %dynamic-slice_bitcast_fusion), channel_id=1, source_target_pairs={{0,1},{1,0},{2,3},{3,2},{4,5},{5,4},{6,7},{7,6},{8,9},{9,8},{10,11... | collective-permute-start | bytes 1228808 | tf_op jit(solution)/shard_map/ppermute | solution.py:283
  138.6 51.6 %copy-start.1 = (f32[512]{0:T(512)S(1)}, f32[512]{0:T(512)}, u32[]{:S(2)}) copy-start(f32[512]{0:T(512)} %param.9) | copy-start | bytes 6148
  138.7 9.3 %collective-permute-start.1 = (f32[200,128]{1,0:T(8,128)S(1)}, f32[200,128]{1,0:T(8,128)S(1)}, u32[]{:S(2)}, u32[]{:S(2)}) collective-permute-start(f32[200,128]{1,0:T(8,128)S(1)} %get-tuple-element.14), channel_id=1, source_target_pairs={{0,2},{1,3},{2,4},{3,5},{4,6},{5,7},{6,0},{7,1},{8,10},{9,11},{10,... | collective-permute-start | bytes 307208 | tf_op jit(solution)/shard_map/ppermute | solution.py:287
  140.9 7.3 %collective-permute-start.2 = (f32[200,128]{1,0:T(8,128)S(1)}, f32[200,128]{1,0:T(8,128)S(1)}, u32[]{:S(2)}, u32[]{:S(2)}) collective-permute-start(f32[200,128]{1,0:T(8,128)S(1)} %get-tuple-element.16), channel_id=1, source_target_pairs={{0,4},{1,5},{2,6},{3,7},{4,0},{5,1},{6,2},{7,3},{8,12},{9,13},{10,... | collective-permute-start | bytes 307208 | tf_op jit(solution)/shard_map/ppermute | solution.py:287
  144.8 5.8 %collective-permute-start.3 = (f32[200,128]{1,0:T(8,128)S(1)}, f32[200,128]{1,0:T(8,128)S(1)}, u32[]{:S(2)}, u32[]{:S(2)}) collective-permute-start(f32[200,128]{1,0:T(8,128)S(1)} %get-tuple-element.15), channel_id=1, source_target_pairs={{0,6},{1,7},{2,0},{3,1},{4,2},{5,3},{6,4},{7,5},{8,14},{9,15},{10,... | collective-permute-start | bytes 307208 | tf_op jit(solution)/shard_map/ppermute | solution.py:287
